TPU v7x, 256 devices: a whole 4x4x8 slice. The times are simulated.
256 devices in a mesh: batch: 8 (over z), tm: 8 (over x, y_lo), space: 4 (over y_hi, core).
Axes of the slice: x: 4, y: 4 (y_hi: 2, y_lo: 2; y = y_hi * 2 + y_lo), z: 8, core: 2. Of those that a mesh axis runs over, the one named last changes fastest.
Arguments:
- video: bfloat16 [16, 32, 16, 16, 1024], P('batch', 'tm', 'space'), may hold values from -8 to 8
- shifts: int32 [16, 3], P('batch'), may hold values from -4 to 4, as said below
- head_scale: float32 [16], replicated, may hold values from 4 to 16
- w_qkv: bfloat16 [1024, 3072], replicated, may hold values from -0.1875 to 0.1875
- w_out: bfloat16 [1024, 1024], replicated, may hold values from -0.1875 to 0.1875
- w_emb: bfloat16 [1024, 768], replicated, may hold values from -0.1875 to 0.1875
- text: bfloat16 [16, 768], P('batch'), may hold values from -0.21875 to 0.21875
- bucket: int32 [16, 16], P('batch'), may hold values from 0 to 3
- bucket_scale: float32 [4], replicated, may hold values from 0.25 to 4
Outputs:
- video_grad: bfloat16 [16, 32, 16, 16, 1024], P('batch', 'tm', 'space')
- text_grad: float32 [16, 768], P('batch')
- contrast_loss: float32 [], replicated
Inputs may be any that keep to these rules, and one draw needn't show every extreme that they name: `shifts`: columns 0 and 1 of the shift of clip c are nonzero and at most 2 in magnitude, positive for even c and negative for odd c; column 2 is at most 4 in magnitude.
All inputs are finite; a program needn't handle non-finite values.
Results may differ from a plain program's by a relative error of at most 0.015.
Values may be sent and summed in bfloat16 or wider, within the bound.
No kernel may reach another device: no remote copies, remote signals or barrier semaphores. Data moves between devices by JAX's collectives and lax.ppermute only.
A program may use at most 128 MiB of HBM per device.

v0:
```python
from functools import partial

import jax
import jax.numpy as jnp
from jax import lax
from jax.sharding import PartitionSpec as P

HEADS = 16
HEAD_DIM = 64
WT = 4
WH = 4
WW = 8
HALO = 2


SOFTMAX_TEMP = 0.07
NORM_EPS = 1e-05
QUERY_EPS = 1e-06
EMBED_EPS = 1e-06
PRECISE_MATMUL = lax.Precision.HIGHEST


def padded(cells, sides, width):
    for axis, dim in sides:
        count = lax.axis_size(axis)
        head = lax.slice_in_dim(cells, 0, width, axis=dim)
        tail = lax.slice_in_dim(cells, cells.shape[dim] - width, cells.shape[dim], axis=dim)
        cells = jnp.concatenate(
            [
                lax.ppermute(tail, axis, [(i, (i + 1) % count) for i in range(count)]),
                cells,
                lax.ppermute(head, axis, [((i + 1) % count, i) for i in range(count)]),
            ],
            axis=dim,
        )
    return cells


def outside_range(position, offset, extent):
    moved = position + offset
    return jnp.logical_or(moved < 0, moved >= extent).astype(jnp.int32)


def region_labels(frame_pos, row_pos, column_pos, offset, frame_extent, row_extent, column_extent):
    first_label = outside_range(frame_pos, offset[0], frame_extent)
    second_label = outside_range(row_pos, offset[1], row_extent)
    third_label = outside_range(column_pos, offset[2], column_extent)
    return (
        first_label[:, None, None] * 4
        + second_label[None, :, None] * 2
        + third_label[None, None, :]
    )


def window_split(blocks):
    clips_here, frames, row_count, columns, feature_dim = blocks.shape
    tiled = blocks.reshape(
        clips_here, frames // WT, WT, row_count // WH, WH, columns // WW, WW, feature_dim
    )
    tiled = tiled.transpose(0, 1, 3, 5, 2, 4, 6, 7)
    return tiled.reshape(-1, WT * WH * WW, feature_dim)


def window_merge(tiles, clips_here, frames, row_count, columns):
    feature_dim = tiles.shape[-1]
    tiled = tiles.reshape(
        clips_here, frames // WT, row_count // WH, columns // WW, WT, WH, WW, feature_dim
    )
    tiled = tiled.transpose(0, 1, 4, 2, 5, 3, 6, 7)
    return tiled.reshape(clips_here, frames, row_count, columns, feature_dim)


def cut_block(extended, offset, direction, frames, row_count):
    start_frame = HALO + direction * offset[0]
    start_row = HALO + direction * offset[1]
    anchor = jnp.zeros((), jnp.int32)
    sizes_out = (frames, row_count, extended.shape[2], extended.shape[3])
    return lax.dynamic_slice(extended, (start_frame, start_row, anchor, anchor), sizes_out)


def attend_forward(blocks, labels, w_qkv, head_scale):
    tiles = window_split(blocks)
    marks = window_split(labels[..., None])[..., 0]
    win_count, win_size, model_width = tiles.shape
    wide = tiles.astype(jnp.float32)
    centered = wide - jnp.mean(wide, axis=-1, keepdims=True)
    inv_std = lax.rsqrt(jnp.mean(centered * centered, axis=-1, keepdims=True) + NORM_EPS)
    normed = centered * inv_std
    flat = normed.astype(jnp.bfloat16).reshape(win_count * win_size, model_width)
    projected = jnp.dot(flat, w_qkv, preferred_element_type=jnp.float32)
    projected = projected.reshape(win_count, win_size, 3, HEADS, HEAD_DIM)
    query = projected[:, :, 0]
    key_part = projected[:, :, 1]
    value_part = projected[:, :, 2]
    q_norm = jnp.sqrt(jnp.sum(query * query, axis=-1, keepdims=True) + QUERY_EPS)
    k_norm = jnp.sqrt(jnp.sum(key_part * key_part, axis=-1, keepdims=True) + QUERY_EPS)
    q_unit = query / q_norm
    k_unit = key_part / k_norm
    q_low = q_unit.astype(jnp.bfloat16)
    k_low = k_unit.astype(jnp.bfloat16)
    v_low = value_part.astype(jnp.bfloat16)
    scores = jnp.einsum("wqhe,wkhe->whqk", q_low, k_low, preferred_element_type=jnp.float32)
    scores = scores * head_scale[None, :, None, None]
    same = (marks[:, :, None] == marks[:, None, :])[:, None]
    exp_score = jnp.where(same, jnp.exp(scores), 0.0)
    prob = exp_score / jnp.sum(exp_score, axis=-1, keepdims=True)
    prob_low = prob.astype(jnp.bfloat16)
    mixed = jnp.einsum("whqk,wkhe->wqhe", prob_low, v_low, preferred_element_type=jnp.float32)
    out_low = mixed.reshape(win_count, win_size, model_width).astype(jnp.bfloat16)
    stored = (normed, inv_std, q_unit, k_unit, q_norm, k_norm, q_low, k_low, v_low, prob, prob_low)
    return (stored, out_low)


def attend_backward(stored, clip_rows, out_rows, w_qkv, head_scale):
    normed, inv_std, q_unit, k_unit, q_norm, k_norm, q_low, k_low, v_low, prob, prob_low = stored
    win_count, win_size, model_width = normed.shape
    d_heads = out_rows.reshape(win_count, HEADS, HEAD_DIM)
    along = jnp.einsum("whe,wkhe->whk", d_heads, v_low, preferred_element_type=jnp.float32)
    inner = jnp.sum(prob * along[:, :, None, :], axis=-1, keepdims=True)
    d_score = (prob * (along[:, :, None, :] - inner)).astype(jnp.bfloat16)
    scale = head_scale[None, None, :, None]
    dq_unit = (
        jnp.einsum("whqk,wkhe->wqhe", d_score, k_low, preferred_element_type=jnp.float32) * scale
    )
    dk_unit = (
        jnp.einsum("whqk,wqhe->wkhe", d_score, q_low, preferred_element_type=jnp.float32) * scale
    )
    mass = jnp.sum(prob_low, axis=2, dtype=jnp.float32)
    d_values = jnp.transpose(mass, (0, 2, 1))[..., None] * d_heads.astype(jnp.float32)[:, None]
    d_query = (dq_unit - q_unit * jnp.sum(q_unit * dq_unit, axis=-1, keepdims=True)) / q_norm
    d_keys = (dk_unit - k_unit * jnp.sum(k_unit * dk_unit, axis=-1, keepdims=True)) / k_norm
    d_projected = jnp.stack([d_query, d_keys, d_values], axis=2)
    d_projected = d_projected.reshape(win_count * win_size, 3 * model_width).astype(jnp.bfloat16)
    d_normed = lax.dot_general(
        d_projected, w_qkv, (((1,), (1,)), ((), ())), preferred_element_type=jnp.float32
    )
    d_normed = d_normed.reshape(win_count, win_size, model_width)
    first_mean = jnp.mean(d_normed, axis=-1, keepdims=True)
    second_mean = jnp.mean(d_normed * normed, axis=-1, keepdims=True)
    d_tokens = inv_std * (d_normed - first_mean - normed * second_mean)
    return (clip_rows[:, None, :] + d_tokens).astype(jnp.bfloat16)


def local(video, shifts, head_scale, w_qkv, w_out, w_emb, text, bucket, bucket_scale):
    clip_dev, frames_dev, rows_dev, column_count, model_width = video.shape
    frames_all = frames_dev * lax.axis_size("tm")
    rows_all = rows_dev * lax.axis_size("space")
    clip_tokens = frames_all * rows_all * column_count
    clips_all = clip_dev * lax.axis_size("batch")
    token_sum = jnp.sum(video, axis=(1, 2, 3), dtype=jnp.float32)
    extended = padded(video, (("tm", 1), ("space", 2)), HALO)
    rolled = jax.vmap(partial(cut_block, direction=1, frames=frames_dev, row_count=rows_dev))(
        extended, shifts
    )
    rolled = jax.vmap(lambda blocks, offset: jnp.roll(blocks, -offset[2], axis=2))(rolled, shifts)
    frame_pos = lax.axis_index("tm") * frames_dev + jnp.arange(frames_dev, dtype=jnp.int32)
    row_pos = lax.axis_index("space") * rows_dev + jnp.arange(rows_dev, dtype=jnp.int32)
    column_pos = jnp.arange(column_count, dtype=jnp.int32)
    labels = jax.vmap(
        lambda offset: region_labels(
            frame_pos, row_pos, column_pos, offset, frames_all, rows_all, column_count
        )
    )(shifts)
    stored, out_low = attend_forward(rolled, labels, w_qkv, head_scale)
    per_clip = out_low.shape[0] // clip_dev
    out_sum = jnp.sum(out_low.reshape(clip_dev, -1, model_width), axis=1, dtype=jnp.float32)
    token_total, out_total = lax.psum((token_sum, out_sum), ("tm", "space"))
    out_mean = (out_total / clip_tokens).astype(jnp.bfloat16)
    pooled = token_total / clip_tokens + jnp.dot(
        out_mean, w_out, preferred_element_type=jnp.float32
    )
    embedded = jnp.dot(pooled.astype(jnp.bfloat16), w_emb, preferred_element_type=jnp.float32)
    emb_norm = jnp.sqrt(jnp.sum(embedded * embedded, axis=-1, keepdims=True) + EMBED_EPS)
    clip_unit_vector = embedded / emb_norm
    captions = lax.all_gather(text, "batch", axis=0, tiled=True)
    caption_wide = captions.astype(jnp.float32)
    caption_norm = jnp.sqrt(
        jnp.sum(caption_wide * caption_wide, axis=-1, keepdims=True) + EMBED_EPS
    )
    caption_unit_vector = caption_wide / caption_norm
    levels = jnp.arange(bucket_scale.shape[0], dtype=jnp.int32)
    weights = jnp.sum(jnp.where(bucket[..., None] == levels, bucket_scale, 0.0), axis=-1)
    first_row = lax.axis_index("batch") * clip_dev
    own_rows = first_row + jnp.arange(clip_dev, dtype=jnp.int32)
    own_pair = own_rows[:, None] == jnp.arange(clips_all, dtype=jnp.int32)[None, :]
    similarity_logits = (
        jnp.dot(clip_unit_vector, caption_unit_vector.T, precision=PRECISE_MATMUL) / SOFTMAX_TEMP
    )
    exp_logit = jnp.exp(similarity_logits)
    negative = jnp.where(own_pair, 0.0, weights * exp_logit)
    other_weight = jnp.where(own_pair, 0.0, weights)
    self_logit = jnp.sum(jnp.where(own_pair, similarity_logits, 0.0), axis=1)
    self_exp = jnp.exp(self_logit)
    row_weight = jnp.sum(other_weight, axis=1)
    row_partition = self_exp + (clips_all - 1) * jnp.sum(negative, axis=1) / row_weight
    row_loss = jnp.sum(jnp.log(row_partition) - self_logit)
    column_mass, column_weight, column_self, rows_summed = lax.psum(
        (
            jnp.sum(negative, axis=0),
            jnp.sum(other_weight, axis=0),
            jnp.sum(jnp.where(own_pair, similarity_logits, 0.0), axis=0),
            row_loss,
        ),
        "batch",
    )
    column_partition = jnp.exp(column_self) + (clips_all - 1) * column_mass / column_weight
    contrast_loss = (rows_summed + jnp.sum(jnp.log(column_partition) - column_self)) / (
        2 * clips_all
    )
    own_column = jnp.sum(jnp.where(own_pair, column_partition[None, :], 0.0), axis=1)
    scaled = (clips_all - 1) * weights * exp_logit
    off_grad = (
        scaled * (1.0 / (row_weight * row_partition))[:, None]
        + scaled * (1.0 / (column_weight * column_partition))[None, :]
    )
    on_grad = self_exp / row_partition - 1.0 + self_exp / own_column - 1.0
    logit_gradient = jnp.where(own_pair, on_grad[:, None], off_grad)
    clip_gradient = (
        jnp.dot(logit_gradient, caption_unit_vector, precision=PRECISE_MATMUL) / SOFTMAX_TEMP
    )
    caption_loss_terms = (
        jnp.dot(logit_gradient.T, clip_unit_vector, precision=PRECISE_MATMUL) / SOFTMAX_TEMP
    )
    d_caption = lax.psum_scatter(
        caption_loss_terms.astype(jnp.bfloat16), "batch", scatter_dimension=0, tiled=True
    ).astype(jnp.float32)
    text_wide = text.astype(jnp.float32)
    text_norm = jnp.sqrt(jnp.sum(text_wide * text_wide, axis=-1, keepdims=True) + EMBED_EPS)
    text_unit_vector = text_wide / text_norm
    text_grad = (
        d_caption - text_unit_vector * jnp.sum(text_unit_vector * d_caption, axis=-1, keepdims=True)
    ) / text_norm
    d_embed = (
        clip_gradient
        - clip_unit_vector * jnp.sum(clip_unit_vector * clip_gradient, axis=-1, keepdims=True)
    ) / emb_norm
    clip_grad = jnp.dot(d_embed, w_emb.astype(jnp.float32).T, precision=PRECISE_MATMUL)
    d_out = jnp.dot(clip_grad, w_out.astype(jnp.float32).T, precision=PRECISE_MATMUL).astype(
        jnp.bfloat16
    )
    clip_rows = jnp.repeat(clip_grad, per_clip, axis=0)
    out_rows = jnp.repeat(d_out, per_clip, axis=0)
    d_tiles = attend_backward(stored, clip_rows, out_rows, w_qkv, head_scale)
    d_rolled = window_merge(d_tiles, clip_dev, frames_dev, rows_dev, column_count)
    d_rolled = jax.vmap(lambda blocks, offset: jnp.roll(blocks, offset[2], axis=2))(
        d_rolled, shifts
    )
    d_extended = padded(d_rolled, (("tm", 1), ("space", 2)), HALO)
    video_grad = jax.vmap(partial(cut_block, direction=-1, frames=frames_dev, row_count=rows_dev))(
        d_extended, shifts
    )
    return (video_grad, text_grad, contrast_loss)


def solution(mesh):
    in_specs = (
        P("batch", "tm", "space", None, None),
        P("batch", None),
        P(),
        P(),
        P(),
        P(),
        P("batch", None),
        P("batch", None),
        P(),
    )
    out_specs = (P("batch", "tm", "space", None, None), P("batch", None), P())
    return jax.shard_map(local, mesh=mesh, in_specs=in_specs, out_specs=out_specs, check_vma=False)
```

profile of v0, /device:TPU:30, one launch (start us, length us, event | category | flops | bytes accessed | tf_op | source)
XLA Modules:
  0.0 362.5 jit_solution(1430223668799975769)
XLA Ops:
  6.1 8.8 %copy.57 = bf16[1024,3072]{0,1:T(8,128)(2,1)} copy(bf16[1024,3072]{1,0:T(8,128)(2,1)} %param.14) | data formatting | bytes 12582912 | tf_op args[3]
  15.3 28.0 %all-gather = bf16[8,2,768]{2,1,0:T(2,128)(2,1)S(1)} all-gather(bf16[1,2,768]{2,1,0:T(2,128)(2,1)S(1)} %bitcast.154), channel_id=1, replica_groups=mesh['batch'=8,'tm'=8,'space'=4] {'batch'}, dimensions={0}, use_global_device_ids=true | all-gather | bytes 27648 | tf_op jit(solution)/shard_map/all_gather | solution.py:175
  46.0 3.5 collective-permute-start.3
  50.0 21.1 %collective-permute-done.2 = bf16[2,8,2,16,1024]{4,3,0,2,1:T(8,128)(2,1)S(1)} collective-permute-done((bf16[2,8,2,16,1024]{4,3,0,2,1:T(8,128)(2,1)S(1)}, bf16[2,8,2,16,1024]{4,3,0,2,1:T(8,128)(2,1)S(1)}, u32[]{:S(2)}, u32[]{:S(2)}) %collective-permute-start.2) | collective-permute-done | bytes 1048608 | tf_op jit(solution)/shard_map/ppermute | solution.py:30
  71.1 2.3 pad_maximum_fusion
  73.4 2.8 gather_fusion
  76.5 3.0 copy.55
  79.5 3.0 gather_fusion.2
  86.8 6.6 %fusion.85 = f32[4,128,3,16,64]{1,4,3,2,0:T(8,128)S(1)} fusion(bf16[4,128,1024,1,1]{2,1,4,3,0:T(8,128)(2,1)S(1)} %bitcast.149, bf16[3,16,64,1024,1]{3,2,1,0,4:T(8,128)(2,1)} %bitcast.145), kind=kOutput, calls=%fused_computation.178 | convolution fusion | flops 3221225472 | bytes 13631488 | tf_op jit(solution)/shard_map/dot_general | solution.py:90
  97.5 2.1 copy-done.2
  100.5 123.2 %all-reduce.1 = (f32[2,1024]{1,0:T(2,128)S(1)}, f32[2,1024]{1,0:T(2,128)S(1)}) all-reduce(f32[2,1024]{1,0:T(2,128)S(1)} %convert_reduce_fusion.2, f32[2,1024]{1,0:T(2,128)S(1)} %reduce_sum.267), channel_id=1, replica_groups=mesh['batch'=8,'tm'=8,'space'=4] {'tm','space'}, use_global_device_ids=true, to_apply=%region_1.2 | all-reduce | flops 4096 | bytes 32768 | tf_op jit(solution)/shard_map/psum | solution.py:167
  223.7 2.2 multiply_reduce_fusion.7
  227.0 16.9 %all-reduce.2 = (f32[16]{0:T(128)S(1)}, f32[16]{0:T(128)S(1)}, f32[16]{0:T(128)S(1)}, f32[]{:T(128)}) all-reduce(f32[16]{0:T(128)S(1)} %get-tuple-element.21, f32[16]{0:T(128)S(1)} %get-tuple-element.20, f32[16]{0:T(128)S(1)} %get-tuple-element.11, f32[]{:T(128)} %subtract_reduce_fusion.1), channel_id=1, replica_groups=mesh['batch'=8,'tm'=8,'space'=4] {'batch'}, use_global_device_ids=true, to_apply=%region_21.23 | all-reduce | flops 49 | bytes 392 | tf_op jit(solution)/shard_map/psum | solution.py:197
  245.1 2.7 fusion.34
  247.9 1.7 convolution_convert_fusion.1
  249.7 2.0 fusion.30
  251.7 4.5 %multiply_reduce_fusion = (f32[4,16,128]{2,1,0:T(8,128)S(1)}, f32[4,16,128]{2,1,0:T(8,128)S(1)}) fusion(f32[4,16,128]{2,1,0:T(8,128)S(1)} %bitcast.150, f32[4,16,128]{2,1,0:T(8,128)S(1)} %get-tuple-element.46, f32[4,16,128,128]{2,3,1,0:T(8,128)} %copy-done.4, f32[16]{0:T(128)S(1)} %copy-done.9, pred[4,128,128]{1,2,0:T(8,128)(4,1)S(1)} %broadcast_compare_fusion), kind=kLoop, calls=%fused_computation.12 | loop fusion | flops 8372224 | bytes 4390976 | tf_op jit(solution)/shard_map/reduce_sum | solution.py:119
  256.2 3.9 %fusion.23 = f32[4,16,64,128]{3,2,1,0:T(8,128)} fusion(f32[4,16,128,128]{2,3,1,0:T(8,128)S(1)} %copy-done.3, f32[4,16,128]{2,1,0:T(8,128)S(1)} %get-tuple-element.6, f32[4,16,128]{2,1,0:T(8,128)S(1)} %bitcast.151, f32[4,128,3,16,64]{1,4,3,2,0:T(8,128)} %copy-done.5, f32[4,128,16]{1,2,0:T(8,128)S(1)} %get-tuple-element.56), kind=kOutput, calls=%fused_computation.59 | convolution fusion | flops 138412032 | bytes 8486912 | tf_op jit(solution)/shard_map/whqk,wkhe->wqhe/dot_general | solution.py:123
  260.1 4.2 %fusion.27 = f32[4,16,64,128]{3,2,1,0:T(8,128)} fusion(f32[4,16,128,128]{2,3,1,0:T(8,128)S(1)} %copy-done.3, f32[4,16,128]{2,1,0:T(8,128)S(1)} %get-tuple-element.6, f32[4,16,128]{2,1,0:T(8,128)S(1)} %bitcast.152, f32[4,128,3,16,64]{1,4,3,2,0:T(8,128)} %copy-done.5, f32[4,128,16]{1,2,0:T(8,128)S(1)} %get-tuple-element.57), kind=kOutput, calls=%fused_computation.63 | convolution fusion | flops 138412032 | bytes 8486912 | tf_op jit(solution)/shard_map/whqk,wqhe->wkhe/dot_general | solution.py:126
  265.3 4.5 %fusion.12 = bf16[4,128,1,16,64]{1,4,3,0,2:T(8,128)(2,1)S(1)} fusion(f32[4,16,64,128]{3,2,1,0:T(8,128)} %fusion.23, f32[16]{0:T(128)S(1)} %copy-done.9, f32[4,128,16]{1,2,0:T(8,128)S(1)} %get-tuple-element.57, f32[4,128,3,16,64]{1,4,3,2,0:T(8,128)} %copy-done.5), kind=kOutput, calls=%fused_computation.45 | output fusion | flops 4726847 | bytes 9503744 | tf_op jit(solution)/shard_map/mul | solution.py:130
  269.8 3.2 fusion.13
  274.7 5.0 %fusion.79 = (f32[4,128]{1,0:T(4,128)S(1)}, f32[4,128]{1,0:T(4,128)S(1)}, f32[4,128,1024]{2,1,0:T(8,128)}) fusion(f32[4,128]{1,0:T(4,128)S(1)} %rsqrt.13, f32[4,128,1024]{2,1,0:T(8,128)S(1)} %bitcast.141, f32[4,128]{1,0:T(4,128)S(1)} %div.178, bf16[4,128,3072]{1,2,0:T(8,128)(2,1)S(1)} %bitcast.148, bf16[1024,3072]{1,0:T(8,128)(2,1)S(1)} %bitcast.144), kind=kOutput, calls=%fused_computation.172 | convolution fusion | flops 3223845888 | bytes 13639680 | tf_op jit(solution)/shard_map/dot_general | solution.py:134
  279.8 2.3 add_convert_fusion
  284.4 1.5 gather_fusion.3
  286.4 2.8 collective-permute-start.4
  289.2 20.8 %collective-permute-done.4 = bf16[2,2,4,16,1024]{4,2,1,3,0:T(4,128)(2,1)S(1)} collective-permute-done((bf16[2,2,4,16,1024]{4,2,1,3,0:T(4,128)(2,1)S(1)}, bf16[2,2,4,16,1024]{4,2,1,3,0:T(4,128)(2,1)S(1)}, u32[]{:S(2)}, u32[]{:S(2)}) %collective-permute-start.4) | collective-permute-done | bytes 524320 | tf_op jit(solution)/shard_map/ppermute | solution.py:30
  311.0 3.1 fusion.81
  314.1 3.2 collective-permute-start.7
  320.3 27.1 %all-reduce = bf16[16,768]{1,0:T(8,128)(2,1)S(1)} all-reduce(bf16[16,768]{1,0:T(8,128)(2,1)S(1)} %fusion.14), channel_id=2, replica_groups=mesh['batch'=8,'tm'=8,'space'=4] {'batch'}, use_global_device_ids=true, to_apply=%region_30.32.clone | all-reduce | flops 12288 | bytes 49152
  348.3 4.6 %pad_maximum_fusion.1 = bf16[2,8,8,16,1024]{4,2,1,3,0:T(8,128)(2,1)S(1)} fusion(bf16[2,8,2,16,1024]{4,2,1,3,0:T(2,128)(2,1)} %collective-permute-done.7, bf16[2,8,4,16,1024]{4,2,1,3,0:T(4,128)(2,1)S(1)} %constant_dynamic-update-slice_fusion.3, bf16[2,8,2,16,1024]{4,2,1,3,0:T(2,128)(2,1)} %collective-permute-done.6), kind=kLoop, calls=%fused_computation.9 | loop fusion | flops 12582912 | bytes 8388608 | tf_op jit(solution)/shard_map/concatenate | solution.py:28
  353.0 4.4 %copy.65 = bf16[2,8,8,16,1024]{4,3,0,2,1:T(8,128)(2,1)} copy(bf16[2,8,8,16,1024]{4,2,1,3,0:T(8,128)(2,1)S(1)} %pad_maximum_fusion.1) | data formatting | bytes 8388608 | tf_op jit(solution)/shard_map/concatenate | solution.py:28
  357.4 3.8 %gather_fusion.1 = bf16[2,4,4,16,1024]{4,3,2,1,0:T(8,128)(2,1)} fusion(bf16[2,8,8,16,1024]{4,3,0,2,1:T(8,128)(2,1)} %copy.65, s32[2]{0:T(128)S(1)} %get-tuple-element.14), kind=kCustom, calls=%fused_computation.3 | custom fusion | bytes 2097192 | tf_op jit(solution)/shard_map/vmap()/gather | solution.py:78
  (117 shorter events, 29.3 us)
Async XLA Ops:
  0.6 223.1 %copy-start = (bf16[1024,1024]{1,0:T(8,128)(2,1)S(1)}, bf16[1024,1024]{1,0:T(8,128)(2,1)}, u32[]{:S(2)}) copy-start(bf16[1024,1024]{1,0:T(8,128)(2,1)} %param.15) | copy-start | bytes 6291460
  0.6 5.2 %copy-start.8 = (s32[2,3]{1,0:T(2,128)S(1)}, s32[2,3]{1,0:T(2,128)}, u32[]{:S(2)}) copy-start(s32[2,3]{1,0:T(2,128)} %param.12) | copy-start | bytes 76
  2.9 40.5 %collective-permute-start = (bf16[2,2,4,16,1024]{4,3,0,2,1:T(8,128)(2,1)}, bf16[2,2,4,16,1024]{4,3,0,2,1:T(8,128)(2,1)}, u32[]{:S(2)}, u32[]{:S(2)}) collective-permute-start(bf16[2,2,4,16,1024]{4,3,0,2,1:T(8,128)(2,1)} %copy.78), channel_id=1, source_target_pairs={{0,4},{4,8},{8,12},{12,16},{16,20},{20,24},{24,28},{28,0},{1,5},{5... | collective-permute-start | bytes 1572872 | tf_op jit(solution)/shard_map/ppermute | solution.py:30
  4.5 40.2 %collective-permute-start.1 = (bf16[2,2,4,16,1024]{4,3,0,2,1:T(8,128)(2,1)}, bf16[2,2,4,16,1024]{4,3,0,2,1:T(8,128)(2,1)}, u32[]{:S(2)}, u32[]{:S(2)}) collective-permute-start(bf16[2,2,4,16,1024]{4,3,0,2,1:T(8,128)(2,1)} %copy.79), channel_id=1, source_target_pairs={{4,0},{8,4},{12,8},{16,12},{20,16},{24,20},{28,24},{0,28},{5,1},{9... | collective-permute-start | bytes 1572872 | tf_op jit(solution)/shard_map/ppermute | solution.py:32
  6.1 9.2 %copy-start.7 = (bf16[2,768]{1,0:T(2,128)(2,1)S(1)}, bf16[2,768]{1,0:T(2,128)(2,1)}, u32[]{:S(2)}) copy-start(bf16[2,768]{1,0:T(2,128)(2,1)} %param.17) | copy-start | bytes 9220
  6.1 37.3 %copy-start.10 = (s32[2,16]{1,0:T(2,128)S(1)}, s32[2,16]{1,0:T(2,128)}, u32[]{:S(2)}) copy-start(s32[2,16]{1,0:T(2,128)} %param.18) | copy-start | bytes 388
  6.1 37.2 %copy-start.11 = (f32[4]{0:T(128)S(1)}, f32[4]{0:T(128)}, u32[]{:S(2)}) copy-start(f32[4]{0:T(128)} %param.19) | copy-start | bytes 52
  6.1 38.4 %copy-start.6 = (bf16[2,4,4,16,1024]{4,3,2,1,0:T(8,128)(2,1)S(1)}, bf16[2,4,4,16,1024]{4,3,2,1,0:T(8,128)(2,1)}, u32[]{:S(2)}) copy-start(bf16[2,4,4,16,1024]{4,3,2,1,0:T(8,128)(2,1)} %param.11) | copy-start | bytes 3145732
  45.9 25.2 %collective-permute-start.2 = (bf16[2,8,2,16,1024]{4,3,0,2,1:T(8,128)(2,1)S(1)}, bf16[2,8,2,16,1024]{4,3,0,2,1:T(8,128)(2,1)S(1)}, u32[]{:S(2)}, u32[]{:S(2)}) collective-permute-start(bf16[2,8,2,16,1024]{4,3,0,2,1:T(8,128)(2,1)S(1)} %get-tuple-element.37), channel_id=1, source_target_pairs={{0,1},{1,2},{2,3},{3,0},{4,5},{5,6},{6,7},{7,4},{8,9},{9,10},{10,1... | collective-permute-start | bytes 3145736 | tf_op jit(solution)/shard_map/ppermute | solution.py:30
  46.0 25.1 %collective-permute-start.3 = (bf16[2,8,2,16,1024]{4,3,0,2,1:T(8,128)(2,1)S(1)}, bf16[2,8,2,16,1024]{4,3,0,2,1:T(8,128)(2,1)S(1)}, u32[]{:S(2)}, u32[]{:S(2)}) collective-permute-start(bf16[2,8,2,16,1024]{4,3,0,2,1:T(8,128)(2,1)S(1)} %get-tuple-element.38), channel_id=1, source_target_pairs={{1,0},{2,1},{3,2},{0,3},{5,4},{6,5},{7,6},{4,7},{9,8},{10,9},{11,1... | collective-permute-start | bytes 3145736 | tf_op jit(solution)/shard_map/ppermute | solution.py:32
  93.4 3.2 copy-start.5
  93.4 0.8 copy-start.9
  95.5 2.0 copy-start.4
  97.5 2.1 copy-start.2
  251.7 4.5 %copy-start.3 = (f32[4,16,128,128]{2,3,1,0:T(8,128)S(1)}, f32[4,16,128,128]{2,3,1,0:T(8,128)}, u32[]{:S(2)}) copy-start(f32[4,16,128,128]{2,3,1,0:T(8,128)} %copy-done.2) | copy-start | bytes 12582916
  265.3 4.5 %copy-start.13 = (f32[4,16,64,128]{3,2,1,0:T(8,128)S(1)}, f32[4,16,64,128]{3,2,1,0:T(8,128)}, u32[]{:S(2)}) copy-start(f32[4,16,64,128]{3,2,1,0:T(8,128)} %fusion.27) | copy-start | bytes 6291460
  265.3 9.4 %slice-start = ((s8[6291456]{0:T(1024)(128)(4,1)}), s8[4194304]{0:T(1024)(128)(4,1)S(1)}, s32[]{:S(2)}) async-start(s8[6291456]{0:T(1024)(128)(4,1)} %bitcast.143), calls=%async_computation | async-start | bytes 8388608
  269.8 5.0 %slice-start.1 = ((s8[6291456]{0:T(1024)(128)(4,1)}), s8[2097152]{0:T(1024)(128)(4,1)S(1)}, s32[]{:S(2)}) async-start(s8[6291456]{0:T(1024)(128)(4,1)} %bitcast.143), calls=%async_computation.1 | async-start | bytes 4194304
  286.4 23.5 %collective-permute-start.4 = (bf16[2,2,4,16,1024]{4,2,1,3,0:T(4,128)(2,1)S(1)}, bf16[2,2,4,16,1024]{4,2,1,3,0:T(4,128)(2,1)S(1)}, u32[]{:S(2)}, u32[]{:S(2)}) collective-permute-start(bf16[2,2,4,16,1024]{4,2,1,3,0:T(4,128)(2,1)S(1)} %get-tuple-element.40), channel_id=1, source_target_pairs={{0,4},{4,8},{8,12},{12,16},{16,20},{20,24},{24,28},{28,0},{1,5},{5... | collective-permute-start | bytes 1572872 | tf_op jit(solution)/shard_map/ppermute | solution.py:30
  289.2 21.5 %collective-permute-start.5 = (bf16[2,2,4,16,1024]{4,2,1,3,0:T(4,128)(2,1)S(1)}, bf16[2,2,4,16,1024]{4,2,1,3,0:T(4,128)(2,1)S(1)}, u32[]{:S(2)}, u32[]{:S(2)}) collective-permute-start(bf16[2,2,4,16,1024]{4,2,1,3,0:T(4,128)(2,1)S(1)} %get-tuple-element.39), channel_id=1, source_target_pairs={{4,0},{8,4},{12,8},{16,12},{20,16},{24,20},{28,24},{0,28},{5,1},{9... | collective-permute-start | bytes 1572872 | tf_op jit(solution)/shard_map/ppermute | solution.py:32
  311.0 6.3 %copy-start.12 = (u32[256]{0:T(256)S(1)}, u32[256]{0:T(256)}, u32[]{:S(2)}) copy-start(u32[256]{0:T(256)} %constant.274) | copy-start | bytes 3076
  314.1 34.2 %collective-permute-start.6 = (bf16[2,8,2,16,1024]{4,2,1,3,0:T(2,128)(2,1)}, bf16[2,8,2,16,1024]{4,2,1,3,0:T(2,128)(2,1)}, u32[]{:S(2)}, u32[]{:S(2)}) collective-permute-start(bf16[2,8,2,16,1024]{4,2,1,3,0:T(2,128)(2,1)} %get-tuple-element.35), channel_id=1, source_target_pairs={{0,1},{1,2},{2,3},{3,0},{4,5},{5,6},{6,7},{7,4},{8,9},{9,10},{10,1... | collective-permute-start | bytes 3145736 | tf_op jit(solution)/shard_map/ppermute | solution.py:30
  314.1 34.2 %collective-permute-start.7 = (bf16[2,8,2,16,1024]{4,2,1,3,0:T(2,128)(2,1)S(1)}, bf16[2,8,2,16,1024]{4,2,1,3,0:T(2,128)(2,1)}, u32[]{:S(2)}, u32[]{:S(2)}) collective-permute-start(bf16[2,8,2,16,1024]{4,2,1,3,0:T(2,128)(2,1)S(1)} %get-tuple-element.36), channel_id=1, source_target_pairs={{1,0},{2,1},{3,2},{0,3},{5,4},{6,5},{7,6},{4,7},{9,8},{10,9},{11,1... | collective-permute-start | bytes 3145736 | tf_op jit(solution)/shard_map/ppermute | solution.py:32
  353.0 8.2 %copy-start.1 = (bf16[1024,1024]{1,0:T(8,128)(2,1)S(1)}, bf16[1024,1024]{1,0:T(8,128)(2,1)}, u32[]{:S(2)}) copy-start(bf16[1024,1024]{1,0:T(8,128)(2,1)} %param.15) | copy-start | bytes 6291460
where the time goes:
time: 367 us; the launch traced here: 363 us
  blocking collectives  195 us (53%)
  local copies, waits for them, and re-layouts  44 us (12%)
  waiting for transfers between devices  41.8 us (11%)
  other arithmetic  33.8 us (9%)
  matrix products  31.5 us (9%)
  starting transfers between devices  11.6 us (3%)
  between operations  4.53 us (1%)
    psum x1, blocking collectives, local(): token_total, out_total = lax.psum((token_sum, out_sum), ('tm', 'space'))  123 us
    ppermute x4, waiting for transfers between devices, padded(): lax.ppermute(tail, axis, [(i, (i + 1) % count) for i in range(count)])  41.8 us
    all_gather x1, blocking collectives, local(): captions = lax.all_gather(text, 'batch', axis=0, tiled=True)  28 us
    unnamed x1, blocking collectives  27.1 us
    psum x1, blocking collectives, local(): lax.psum((jnp.sum(negative, axis=0), jnp.sum(other_weight, axis=0), jnp.s...  16.9 us
    unnamed x40, local copies, waits for them, and re-layouts  16.1 us
    ppermute x4, starting transfers between devices, padded(): lax.ppermute(head, axis, [((i + 1) % count, i) for i in range(count)])  8.12 us
  transfers between devices with their start and end apart: 8, of which 2 were waited for; matrix products, arithmetic and copies ran while one was open for 4% of the time, Pallas kernels for 0%

commit v1 on v0

v1 whole, which is shorter than its diff:
```python
from functools import partial

import jax
import jax.numpy as jnp
from jax import lax
from jax.experimental import pallas as pl
from jax.experimental.pallas import tpu as pltpu
from jax.sharding import PartitionSpec as P

HEADS = 16
HEAD_DIM = 64
D = 1024
EMB = 768
WT = 4
WH = 4
WW = 8
COLS = 16
HALO = 2
TOK = WT * WH * WW
QUADS = 4
QW = 256

SOFTMAX_TEMP = 0.07
NORM_EPS = 1e-05
QUERY_EPS = 1e-06
EMBED_EPS = 1e-06
LOG2E = 1.4426950408889634
F32 = jnp.float32
BF16 = jnp.bfloat16
VMEM_LIMIT = 56 * 1024 * 1024

NT = (((1,), (1,)), ((), ()))
TN = (((0,), (0,)), ((), ()))

GRID = 6
OWN = ((0, 4, 0, 4), (2, 4, 2, 4))
PIECES = (
    ((4, 2, 1, 3), (1, 3, 4, 2), (4, 2, 4, 2)),
    ((0, 2, 2, 3), (2, 3, 0, 2), (0, 2, 0, 2)),
)
GIVEN = (
    ((0, 2, 1, 3), (1, 3, 0, 2), (0, 2, 0, 2)),
    ((2, 2, 0, 3), (0, 3, 2, 2), (2, 2, 2, 2)),
)
PIECE_SHAPES = tuple((g[1], g[3], COLS, D) for g in GIVEN[0])


def vmem():
    return pl.BlockSpec(memory_space=pltpu.VMEM)


def smem():
    return pl.BlockSpec(memory_space=pltpu.SMEM)


def hbm():
    return pl.BlockSpec(memory_space=pl.ANY)


def whole(shape):
    return pl.BlockSpec(shape, lambda i: (0,) * len(shape))


def params(**more):
    return pltpu.CompilerParams(vmem_limit_bytes=VMEM_LIMIT, **more)


def pack_kernel(video, *refs):
    outs, sems = refs[:6], refs[6]
    copies = []
    for c in range(2):
        for k in range(3):
            f, nf, r, nr = GIVEN[c][k]
            copies.append(
                pltpu.make_async_copy(
                    video.at[c, pl.ds(f, nf), pl.ds(r, nr)], outs[3 * c + k], sems.at[3 * c + k]
                )
            )
    for copy in copies:
        copy.start()
    for copy in copies:
        copy.wait()


def pack(video):
    return pl.pallas_call(
        pack_kernel,
        out_shape=[jax.ShapeDtypeStruct(s, BF16) for s in PIECE_SHAPES * 2],
        in_specs=[hbm()],
        out_specs=[hbm()] * 6,
        scratch_shapes=[pltpu.SemaphoreType.DMA((6,))],
        compiler_params=params(),
        name="pack",
    )(video)


def exchange(pieces, clip, sign):
    tm, space = lax.axis_size("tm"), lax.axis_size("space")
    step = sign if clip == 0 else -sign
    out = []
    for piece, (dt, ds) in zip(pieces, ((step, 0), (0, step), (step, step))):
        pairs = [
            (t * space + s, ((t + dt) % tm) * space + (s + ds) % space)
            for t in range(tm)
            for s in range(space)
        ]
        out.append(lax.ppermute(piece, ("tm", "space"), pairs))
    return out


def head_blocks(shape, width):
    row = lax.broadcasted_iota(jnp.int32, shape, 0) // width
    lane = lax.broadcasted_iota(jnp.int32, shape, 1) // HEAD_DIM
    return (row == lane).astype(F32).astype(BF16)


def low_lanes(shape):
    return lax.broadcasted_iota(jnp.int32, shape, 1) < HEAD_DIM


def split_heads(pair):
    low = low_lanes(pair.shape)
    wide = pair.astype(F32)
    return jnp.concatenate(
        [jnp.where(low, wide, 0.0), jnp.where(low, 0.0, wide)], axis=0
    ).astype(BF16)


def window_mask(frame0, row0, col0, s0, s1, s2, frames, rows):
    shape = (TOK, 2 * TOK)

    def label(index):
        f = frame0 + index // (WH * WW) + s0
        r = row0 + (index // WW) % WH + s1
        c = col0 + index % WW + s2
        one = lambda v, n: jnp.where((v < 0) | (v >= n), 1, 0)
        return one(f, frames) * 4 + one(r, rows) * 2 + one(c, COLS)

    key = lax.broadcasted_iota(jnp.int32, shape, 0)
    query = lax.broadcasted_iota(jnp.int32, shape, 1) % TOK
    return jnp.where(label(key) == label(query), 1.0, 0.0)


def forward_kernel(clips, frames, rows_all, pos, shifts, hscale, video, *refs):
    nc = len(clips)
    halo = refs[: 3 * nc]
    wq, wk, wv = refs[3 * nc : 3 * nc + 3]
    outs = refs[3 * nc + 3 :]
    ql, kl, vl, rq, rk, mass, prob, n32, istd, sums = outs[:10]
    ext, xb, masks, ones4, ones2, qs, ks = outs[10:]
    step = pl.program_id(0)

    @pl.when(step == 0)
    def _():
        ones4[...] = head_blocks((QW, QW), HEAD_DIM)
        ones2[...] = head_blocks((2 * TOK, 2 * HEAD_DIM), TOK)
        for n, c in enumerate(clips):
            f, nf, r, nr = OWN[c]
            ext[n, f : f + nf, r : r + nr] = video[n]
            for k in range(3):
                f, nf, r, nr = PIECES[c][k]
                ext[n, f : f + nf, r : r + nr] = halo[3 * n + k][...]
            s0, s1, s2 = shifts[c, 0], shifts[c, 1], shifts[c, 2]
            off0, off1 = s0 + HALO * c, s1 + HALO * c
            turn = (COLS - s2) % COLS

            def cells(a, total):
                for b in range(WH):
                    x = ext[n, a + off0, b + off1].astype(F32)
                    total = total + x
                    x = pltpu.roll(x, turn, 0)
                    centered = x - jnp.mean(x, axis=-1, keepdims=True)
                    inv = lax.rsqrt(
                        jnp.mean(centered * centered, axis=-1, keepdims=True) + NORM_EPS
                    )
                    y = centered * inv
                    wide = jnp.broadcast_to(inv, (COLS, 128))
                    for w in range(2):
                        start = pl.multiple_of(
                            (2 * n + w) * TOK + a * (WH * WW) + b * WW, WW
                        )
                        n32[pl.ds(start, WW)] = y[w * WW : (w + 1) * WW]
                        istd[pl.ds(start, WW)] = wide[w * WW : (w + 1) * WW]
                return total

            total = lax.fori_loop(0, WT, cells, jnp.zeros((COLS, D), F32))
            sums[2 * n : 2 * n + 1] = jnp.sum(total, axis=0, keepdims=True)
            for w in range(2):
                masks[2 * n + w] = window_mask(
                    pos[0] * WT, pos[1] * WH, w * WW, s0, s1, s2, frames, rows_all
                )
        xb[...] = n32[...].astype(BF16)

    x = xb[...]
    qs[...] = jnp.dot(x, wq[...], preferred_element_type=F32)
    ks[...] = jnp.dot(x, wk[...], preferred_element_type=F32)
    vl[...] = jnp.dot(x, wv[...], preferred_element_type=F32).astype(BF16)
    for full, unit, inverse in ((qs, ql, rq), (ks, kl, rk)):
        for w in range(2 * nc):
            at = slice(w * TOK, (w + 1) * TOK)
            value = full[at]
            square = jnp.dot(
                (value * value).astype(BF16), ones4[...], preferred_element_type=F32
            )
            inv = lax.rsqrt(square + QUERY_EPS)
            inverse[at] = inv
            unit[at] = (value * inv).astype(BF16)
    lane = lax.broadcasted_iota(jnp.int32, (1, 2 * TOK), 1)
    for p in range(2):
        head = step * 4 + 2 * p
        lanes = slice(p * 128, (p + 1) * 128)
        factor = jnp.where(lane < TOK, hscale[head], hscale[head + 1]) * LOG2E
        for n in range(nc):
            gathered = jnp.zeros((1, 128), F32)
            for w in range(2 * n, 2 * n + 2):
                at = slice(w * TOK, (w + 1) * TOK)
                score = lax.dot_general(
                    kl[at, lanes], split_heads(ql[at, lanes]), NT, preferred_element_type=F32
                )
                e = jnp.exp2(score * factor) * masks[w]
                pt = e * (1.0 / jnp.sum(e, axis=0, keepdims=True))
                prob[0, 2 * w + p] = pt
                held = jnp.dot(pt.astype(BF16), ones2[...], preferred_element_type=F32)
                mass[at, lanes] = held
                gathered = gathered + jnp.sum(
                    held * vl[at, lanes].astype(F32), axis=0, keepdims=True
                )
            start = pl.multiple_of(step * QW + p * 128, 128)
            sums[2 * n + 1 : 2 * n + 2, pl.ds(start, 128)] = gathered


def forward(clips, pos, shifts, hscale, video, halo, w_qkv):
    nc = len(clips)
    n = nc * 2 * TOK
    frames = lax.axis_size("tm") * WT
    rows_all = lax.axis_size("space") * WH
    first = clips[0] // nc
    column = lambda part: pl.BlockSpec((D, QW), lambda i: (0, part * QUADS + i))
    by_quad = lambda: pl.BlockSpec((n, QW), lambda i: (0, i))
    return pl.pallas_call(
        partial(forward_kernel, clips, frames, rows_all),
        grid=(QUADS,),
        out_shape=[jax.ShapeDtypeStruct((n, D), BF16)] * 3
        + [jax.ShapeDtypeStruct((n, D), F32)] * 3
        + [
            jax.ShapeDtypeStruct((QUADS, 4 * nc, TOK, 2 * TOK), F32),
            jax.ShapeDtypeStruct((n, D), F32),
            jax.ShapeDtypeStruct((n, 128), F32),
            jax.ShapeDtypeStruct((2 * nc, D), F32),
        ],
        in_specs=[smem(), smem(), smem()]
        + [pl.BlockSpec((nc, WT, WH, COLS, D), lambda i: (first, 0, 0, 0, 0))]
        + [whole(h.shape) for h in halo]
        + [column(0), column(1), column(2)],
        out_specs=[by_quad() for _ in range(6)]
        + [
            pl.BlockSpec((1, 4 * nc, TOK, 2 * TOK), lambda i: (i, 0, 0, 0)),
            whole((n, D)),
            whole((n, 128)),
            whole((2 * nc, D)),
        ],
        scratch_shapes=[
            pltpu.VMEM((nc, GRID, GRID, COLS, D), BF16),
            pltpu.VMEM((n, D), BF16),
            pltpu.VMEM((2 * nc, TOK, 2 * TOK), F32),
            pltpu.VMEM((QW, QW), BF16),
            pltpu.VMEM((2 * TOK, 2 * HEAD_DIM), BF16),
            pltpu.VMEM((n, QW), F32),
            pltpu.VMEM((n, QW), F32),
        ],
        compiler_params=params(dimension_semantics=("arbitrary",)),
        cost_estimate=pl.CostEstimate(
            flops=2 * n * D * 3 * D, bytes_accessed=12 * 2**20, transcendentals=n * 2048
        ),
        name="forward",
    )(pos, shifts, hscale, video, *halo, w_qkv, w_qkv, w_qkv)


def embed_kernel(tokens, got, w_out, w_emb, text, bucket, levels, out):
    total = jnp.sum(got[...], axis=0)
    mean = (jnp.concatenate([total[1:2], total[3:4]], axis=0) / tokens).astype(BF16)
    token_mean = jnp.concatenate([total[0:1], total[2:3]], axis=0) / tokens
    pooled = token_mean + jnp.dot(mean, w_out[...], preferred_element_type=F32)
    embedded = jnp.dot(pooled.astype(BF16), w_emb[...], preferred_element_type=F32)
    held = bucket[...]
    weight = jnp.zeros(held.shape, F32)
    for level in range(levels.shape[0]):
        weight = weight + jnp.where(held == level, levels[level], 0.0)
    weight = jnp.concatenate(
        [weight, jnp.zeros((held.shape[0], 128 - held.shape[1]), F32)], axis=1
    )
    words = text[...].astype(F32)
    block = jnp.concatenate(
        [
            jnp.concatenate([embedded, weight], axis=1),
            jnp.concatenate([words, jnp.zeros_like(weight)], axis=1),
        ],
        axis=0,
    )
    for peer in range(out.shape[0]):
        out[peer] = block


def embed(got, w_out, w_emb, text, bucket, levels, tokens, peers):
    return pl.pallas_call(
        partial(embed_kernel, tokens),
        out_shape=jax.ShapeDtypeStruct((peers, 4, EMB + 128), F32),
        in_specs=[vmem()] * 5 + [smem()],
        out_specs=vmem(),
        compiler_params=params(),
        name="embed",
    )(got, w_out, w_emb, text, bucket, levels)


def three_parts(wide):
    high = wide.astype(BF16)
    rest = wide - high.astype(F32)
    middle = rest.astype(BF16)
    low = (rest - middle.astype(F32)).astype(BF16)
    return jnp.concatenate([high, middle, low], axis=0)


def full_dot(wide, weight):
    n = wide.shape[0]
    got = lax.dot_general(three_parts(wide), weight, NT, preferred_element_type=F32)
    return got[:n] + got[n : 2 * n] + got[2 * n :]


def contrast_kernel(pos, got, w_emb, w_out, text_grad, loss, clip_grad, d_out):
    peers = got.shape[0]
    n = 2 * peers
    embedded = jnp.concatenate([got[p, 0:2, :EMB] for p in range(peers)], axis=0)
    weights = jnp.concatenate([got[p, 0:2, EMB:] for p in range(peers)], axis=0)[:, :n]
    words = jnp.concatenate([got[p, 2:4, :EMB] for p in range(peers)], axis=0)
    clip_norm = jnp.sqrt(jnp.sum(embedded * embedded, axis=-1, keepdims=True) + EMBED_EPS)
    text_norm = jnp.sqrt(jnp.sum(words * words, axis=-1, keepdims=True) + EMBED_EPS)
    clip_unit = embedded / clip_norm
    text_unit = words / text_norm
    exact = lax.Precision.HIGHEST
    logits = (
        lax.dot_general(clip_unit, text_unit, NT, precision=exact, preferred_element_type=F32)
        / SOFTMAX_TEMP
    )
    own = lax.broadcasted_iota(jnp.int32, (n, n), 0) == lax.broadcasted_iota(
        jnp.int32, (n, n), 1
    )
    exp_logit = jnp.exp(logits)
    other = jnp.where(own, 0.0, weights)
    negative = other * exp_logit
    diagonal = jnp.where(own, logits, 0.0)
    row_self = jnp.sum(diagonal, axis=1, keepdims=True)
    col_self = jnp.sum(diagonal, axis=0, keepdims=True)
    row_weight = jnp.sum(other, axis=1, keepdims=True)
    col_weight = jnp.sum(other, axis=0, keepdims=True)
    row_part = (
        jnp.exp(row_self) + (n - 1) * jnp.sum(negative, axis=1, keepdims=True) / row_weight
    )
    col_part = (
        jnp.exp(col_self) + (n - 1) * jnp.sum(negative, axis=0, keepdims=True) / col_weight
    )
    summed = jnp.sum(jnp.log(row_part) - row_self, axis=0, keepdims=True) + jnp.sum(
        jnp.log(col_part) - col_self, axis=1, keepdims=True
    )
    loss[...] = summed / (2 * n)
    scaled = (n - 1) * weights * exp_logit
    off = scaled * (1.0 / (row_weight * row_part)) + scaled * (1.0 / (col_weight * col_part))
    on = exp_logit / row_part - 1.0 + exp_logit / col_part - 1.0
    grad = jnp.where(own, on, off)
    d_clip = (
        jnp.dot(grad, text_unit, precision=exact, preferred_element_type=F32) / SOFTMAX_TEMP
    )
    d_text = (
        lax.dot_general(grad, clip_unit, TN, precision=exact, preferred_element_type=F32)
        / SOFTMAX_TEMP
    )
    text_all = (
        d_text - text_unit * jnp.sum(text_unit * d_text, axis=-1, keepdims=True)
    ) / text_norm
    embed_all = (
        d_clip - clip_unit * jnp.sum(clip_unit * d_clip, axis=-1, keepdims=True)
    ) / clip_norm
    row = lax.broadcasted_iota(jnp.int32, (n, 1), 0)

    def mine(array):
        return jnp.concatenate(
            [
                jnp.sum(
                    jnp.where(row == 2 * pos[2] + c, array, 0.0), axis=0, keepdims=True
                )
                for c in range(2)
            ],
            axis=0,
        )

    text_grad[...] = mine(text_all)
    pooled_grad = full_dot(mine(embed_all), w_emb[...])
    clip_grad[...] = pooled_grad
    d_out[...] = full_dot(pooled_grad, w_out[...])


def contrast(pos, got, w_emb, w_out):
    return pl.pallas_call(
        contrast_kernel,
        out_shape=[
            jax.ShapeDtypeStruct((2, EMB), F32),
            jax.ShapeDtypeStruct((1, 1), F32),
            jax.ShapeDtypeStruct((2, D), F32),
            jax.ShapeDtypeStruct((2, D), F32),
        ],
        in_specs=[smem(), vmem(), vmem(), vmem()],
        out_specs=[vmem()] * 4,
        compiler_params=params(),
        name="contrast",
    )(pos, got, w_emb, w_out)


def backward_kernel(clips, shifts, hscale, clip_grad, d_out, *refs):
    nc = len(clips)
    ql, kl, vl, rq, rk, mass, prob, n32, istd, wq, wk, wv = refs[:12]
    outs = refs[12 : 12 + 4 * nc]
    ext, total, ones4, dqs, dks, dqb, dkb, dvb = refs[12 + 4 * nc :]
    step = pl.program_id(0)

    @pl.when(step == 0)
    def _():
        ones4[...] = head_blocks((QW, QW), HEAD_DIM)

    low = low_lanes((TOK, 128))
    upper = lax.broadcasted_iota(jnp.int32, (128, TOK), 0) < HEAD_DIM
    lane = lax.broadcasted_iota(jnp.int32, (1, 128), 1)
    for p in range(2):
        head = step * 4 + 2 * p
        lanes = slice(p * 128, (p + 1) * 128)
        factor = jnp.where(lane < HEAD_DIM, hscale[head], hscale[head + 1])
        for n, c in enumerate(clips):
            row = d_out[c : c + 1, lanes].astype(BF16).astype(F32)
            spread = jnp.transpose(jnp.broadcast_to(row, (TOK, 128)))
            spread = jnp.concatenate(
                [jnp.where(upper, spread, 0.0), jnp.where(upper, 0.0, spread)], axis=1
            ).astype(BF16)
            for w in range(2 * n, 2 * n + 2):
                at = slice(w * TOK, (w + 1) * TOK)
                along = jnp.dot(vl[at, lanes], spread, preferred_element_type=F32)
                pt = prob[0, 2 * w + p]
                inner = jnp.sum(pt * along, axis=0, keepdims=True)
                ds = (pt * (along - inner)).astype(BF16)
                dk = jnp.dot(ds, split_heads(ql[at, lanes]), preferred_element_type=F32)
                dq = lax.dot_general(ds, kl[at, lanes], TN, preferred_element_type=F32)
                dks[at, lanes] = dk * factor
                dqs[at, lanes] = jnp.where(low, dq[:TOK], dq[TOK:]) * factor
                dvb[at, lanes] = (mass[at, lanes] * row).astype(BF16)
    for unit, grad, inverse, done in ((ql, dqs, rq, dqb), (kl, dks, rk, dkb)):
        for w in range(2 * nc):
            at = slice(w * TOK, (w + 1) * TOK)
            u = unit[at].astype(F32)
            g = grad[at]
            inner = jnp.dot((u * g).astype(BF16), ones4[...], preferred_element_type=F32)
            done[at] = ((g - u * inner) * inverse[at]).astype(BF16)
    part = (
        lax.dot_general(dqb[...], wq[...], NT, preferred_element_type=F32)
        + lax.dot_general(dkb[...], wk[...], NT, preferred_element_type=F32)
        + lax.dot_general(dvb[...], wv[...], NT, preferred_element_type=F32)
    )

    @pl.when(step == 0)
    def _():
        total[...] = part

    @pl.when(step > 0)
    def _():
        total[...] = total[...] + part

    @pl.when(step == QUADS - 1)
    def _():
        for n, c in enumerate(clips):
            s0, s1, s2 = shifts[c, 0], shifts[c, 1], shifts[c, 2]
            off0, off1 = s0 + HALO * c, s1 + HALO * c
            turn = (COLS + s2) % COLS
            base = clip_grad[c : c + 1]

            def cells(a, carry):
                for b in range(WH):
                    halves = []
                    for w in range(2):
                        start = pl.multiple_of(
                            (2 * n + w) * TOK + a * (WH * WW) + b * WW, WW
                        )
                        dn = total[pl.ds(start, WW)]
                        y = n32[pl.ds(start, WW)]
                        inv = istd[pl.ds(start, WW)][:, :1]
                        first = jnp.mean(dn, axis=-1, keepdims=True)
                        second = jnp.mean(dn * y, axis=-1, keepdims=True)
                        halves.append(base + inv * (dn - first - y * second))
                    cell = pltpu.roll(jnp.concatenate(halves, axis=0), turn, 0)
                    ext[n, a + off0, b + off1] = cell.astype(BF16)
                return carry

            lax.fori_loop(0, WT, cells, 0)
            f, nf, r, nr = OWN[c]
            outs[4 * n][...] = ext[n, f : f + nf, r : r + nr]
            for k in range(3):
                f, nf, r, nr = PIECES[c][k]
                outs[4 * n + 1 + k][...] = ext[n, f : f + nf, r : r + nr]


def backward(clips, shifts, hscale, clip_grad, d_out, stored, w_qkv):
    nc = len(clips)
    n = nc * 2 * TOK
    column = lambda part: pl.BlockSpec((D, QW), lambda i: (0, part * QUADS + i))
    by_quad = lambda: pl.BlockSpec((n, QW), lambda i: (0, i))
    shapes = ((WT, WH, COLS, D),) + PIECE_SHAPES
    return pl.pallas_call(
        partial(backward_kernel, clips),
        grid=(QUADS,),
        out_shape=[jax.ShapeDtypeStruct(s, BF16) for s in shapes * nc],
        in_specs=[smem(), smem(), whole((2, D)), pl.BlockSpec((2, QW), lambda i: (0, i))]
        + [by_quad() for _ in range(6)]
        + [
            pl.BlockSpec((1, 4 * nc, TOK, 2 * TOK), lambda i: (i, 0, 0, 0)),
            whole((n, D)),
            whole((n, 128)),
            column(0),
            column(1),
            column(2),
        ],
        out_specs=[whole(s) for s in shapes * nc],
        scratch_shapes=[
            pltpu.VMEM((nc, GRID, GRID, COLS, D), BF16),
            pltpu.VMEM((n, D), F32),
            pltpu.VMEM((QW, QW), BF16),
            pltpu.VMEM((n, QW), F32),
            pltpu.VMEM((n, QW), F32),
            pltpu.VMEM((n, QW), BF16),
            pltpu.VMEM((n, QW), BF16),
            pltpu.VMEM((n, QW), BF16),
        ],
        compiler_params=params(dimension_semantics=("arbitrary",)),
        cost_estimate=pl.CostEstimate(
            flops=2 * n * D * 3 * D, bytes_accessed=16 * 2**20, transcendentals=0
        ),
        name="backward",
    )(shifts, hscale, clip_grad, d_out, *stored, w_qkv, w_qkv, w_qkv)


def merge_kernel(shifts, *refs):
    own, got, out = refs[:2], refs[2:8], refs[8]
    for c in range(2):
        s0, s1 = shifts[c, 0], shifts[c, 1]
        a, b, corner = got[3 * c : 3 * c + 3]
        for f in range(WT):
            for r in range(WH):
                if c == 0:
                    far_f, far_r = f < HALO, r < HALO
                    gone_f, gone_r = f < s0, r < s1
                    at_a, at_b, at_c = (f, r - 1), (f - 1, r), (f, r)
                else:
                    far_f, far_r = f >= WT - HALO, r >= WH - HALO
                    gone_f, gone_r = f >= WT + s0, r >= WH + s1
                    at_a, at_b, at_c = (f - 2, r), (f, r - 2), (f - 2, r - 2)
                value = own[c][f, r]
                in_a = far_f and 0 <= at_a[1] < 3
                in_b = far_r and 0 <= at_b[0] < 3
                if in_a:
                    take = jnp.logical_and(gone_f, jnp.logical_not(gone_r))
                    value = jnp.where(take, a[at_a], value)
                if in_b:
                    take = jnp.logical_and(jnp.logical_not(gone_f), gone_r)
                    value = jnp.where(take, b[at_b], value)
                if far_f and far_r:
                    value = jnp.where(jnp.logical_and(gone_f, gone_r), corner[at_c], value)
                out[c, f, r] = value


def merge(shifts, own, got):
    return pl.pallas_call(
        merge_kernel,
        out_shape=jax.ShapeDtypeStruct((2, WT, WH, COLS, D), BF16),
        in_specs=[smem()] + [vmem()] * 8,
        out_specs=vmem(),
        compiler_params=params(),
        name="merge",
    )(shifts, *own, *got)


def local(video, shifts, head_scale, w_qkv, w_out, w_emb, text, bucket, bucket_scale):
    tokens = lax.axis_size("tm") * lax.axis_size("space") * WT * WH * COLS
    plane = lax.axis_size("tm") * lax.axis_size("space")
    peers = lax.axis_size("batch")
    pos = jnp.stack(
        [lax.axis_index("tm"), lax.axis_index("space"), lax.axis_index("batch")]
    ).astype(jnp.int32)
    pieces = pack(video)
    halo = exchange(pieces[:3], 0, -1) + exchange(pieces[3:], 1, -1)
    *stored, sums = forward((0, 1), pos, shifts, head_scale, video, halo, w_qkv)
    spread = jnp.broadcast_to(sums[None], (plane,) + sums.shape)
    got = lax.all_to_all(spread, ("tm", "space"), 0, 0)
    packed = embed(got, w_out, w_emb, text, bucket, bucket_scale, tokens, peers)
    got = lax.all_to_all(packed, "batch", 0, 0)
    text_grad, loss, clip_grad, d_out = contrast(pos, got, w_emb, w_out)
    outs = backward((0, 1), shifts, head_scale, clip_grad, d_out, stored, w_qkv)
    back = exchange(outs[1:4], 0, 1) + exchange(outs[5:8], 1, 1)
    video_grad = merge(shifts, (outs[0], outs[4]), back)
    return (video_grad, text_grad, loss[0, 0])


def solution(mesh):
    in_specs = (
        P("batch", "tm", "space", None, None),
        P("batch", None),
        P(),
        P(),
        P(),
        P(),
        P("batch", None),
        P("batch", None),
        P(),
    )
    out_specs = (P("batch", "tm", "space", None, None), P("batch", None), P())
    return jax.shard_map(local, mesh=mesh, in_specs=in_specs, out_specs=out_specs, check_vma=False)
```

time: 367 us -> 158 us (0.43)
  the two profiles are of different devices: /device:TPU:30 before, /device:TPU:1 now
where the time goes in v1:
time: 158 us
  Pallas kernels  79 us (50%)
  blocking collectives  35.7 us (23%)
  starting transfers between devices  20.2 us (13%)
  waiting for transfers between devices  19.3 us (12%)
  local copies, waits for them, and re-layouts  2.18 us (1%)
    pallas_call x1, Pallas kernels, pack(): pl.pallas_call(pack_kernel, out_shape=[jax.ShapeDtypeStruct(s, BF16) for...  32.9 us
    ppermute x12, starting transfers between devices, exchange(): out.append(lax.ppermute(piece, ('tm', 'space'), pairs))  20.2 us
    pallas_call x1, Pallas kernels, backward(): pl.pallas_call(partial(backward_kernel, clips), grid=(QUADS,), out_shape=...  20.1 us
    all_to_all x1, blocking collectives, local(): got = lax.all_to_all(spread, ('tm', 'space'), 0, 0)  19.8 us
    ppermute x12, waiting for transfers between devices, exchange(): out.append(lax.ppermute(piece, ('tm', 'space'), pairs))  19.3 us
    all_to_all x1, blocking collectives, local(): got = lax.all_to_all(packed, 'batch', 0, 0)  16 us
    pallas_call x1, Pallas kernels, forward(): pl.pallas_call(partial(forward_kernel, clips, frames, rows_all), grid=(QU...  15.2 us
    pallas_call x1, Pallas kernels, contrast(): pl.pallas_call(contrast_kernel, out_shape=[jax.ShapeDtypeStruct((2, EMB),...  4.54 us
  transfers between devices with their start and end apart: 12, of which 8 were waited for; matrix products, arithmetic and copies ran while one was open for 0% of the time, Pallas kernels for 0%

profile of v1, /device:TPU:1, one launch (start us, length us, event | category | flops | bytes accessed | tf_op | source)
XLA Modules:
  0.0 157.6 jit_solution(13678741761022758858)
XLA Ops:
  0.6 32.9 %pack.1 = (bf16[2,3,16,1024]{3,2,1,0:T(8,128)(2,1)}, bf16[3,2,16,1024]{3,2,1,0:T(8,128)(2,1)}, bf16[2,2,16,1024]{3,2,1,0:T(8,128)(2,1)}, bf16[2,3,16,1024]{3,2,1...) custom-call(bf16[2,4,4,16,1024]{4,3,2,1,0:T(8,128)(2,1)} %video.3), custom_call_target="tpu_custom_call" | custom-call | tf_op jit(solution)/shard_map/pack/pallas_call | solution.py:86
  33.6 5.0 %collective-permute-start.2 = (bf16[2,2,16,1024]{3,2,1,0:T(8,128)(2,1)}, bf16[2,2,16,1024]{3,2,1,0:T(8,128)(2,1)S(1)}, u32[]{:S(2)}, u32[]{:S(2)}) collective-permute-start(bf16[2,2,16,1024]{3,2,1,0:T(8,128)(2,1)} %get-tuple-element.33), channel_id=1, source_target_pairs={{0,31},{1,28},{2,29},{3,30},{4,3},{5,0},{6,1},{7,2},{8,7},{9,4},{1... | collective-permute-start | bytes 393224 | tf_op jit(solution)/shard_map/ppermute | solution.py:107
  38.5 0.2 collective-permute-start
  38.7 1.2 collective-permute-start.1
  39.9 1.6 %collective-permute-start.3 = (bf16[2,3,16,1024]{3,2,1,0:T(8,128)(2,1)}, bf16[2,3,16,1024]{3,2,1,0:T(8,128)(2,1)S(1)}, u32[]{:S(2)}, u32[]{:S(2)}) collective-permute-start(bf16[2,3,16,1024]{3,2,1,0:T(8,128)(2,1)} %get-tuple-element.34), channel_id=1, source_target_pairs={{0,4},{1,5},{2,6},{3,7},{4,8},{5,9},{6,10},{7,11},{8,12},{9,13},{1... | collective-permute-start | bytes 589832 | tf_op jit(solution)/shard_map/ppermute | solution.py:107
  41.5 2.6 %collective-permute-start.4 = (bf16[3,2,16,1024]{3,2,1,0:T(8,128)(2,1)}, bf16[3,2,16,1024]{3,2,1,0:T(8,128)(2,1)S(1)}, u32[]{:S(2)}, u32[]{:S(2)}) collective-permute-start(bf16[3,2,16,1024]{3,2,1,0:T(8,128)(2,1)} %get-tuple-element.35), channel_id=1, source_target_pairs={{0,1},{1,2},{2,3},{3,0},{4,5},{5,6},{6,7},{7,4},{8,9},{9,10},{10,1... | collective-permute-start | bytes 589832 | tf_op jit(solution)/shard_map/ppermute | solution.py:107
  44.1 0.5 collective-permute-start.5
  44.7 0.6 pad_add_fusion.pos
  45.2 7.2 %collective-permute-done.5.refs_5_ = bf16[2,2,16,1024]{3,2,1,0:T(8,128)(2,1)S(1)} collective-permute-done((bf16[2,2,16,1024]{3,2,1,0:T(8,128)(2,1)}, bf16[2,2,16,1024]{3,2,1,0:T(8,128)(2,1)S(1)}, u32[]{:S(2)}, u32[]{:S(2)}) %collective-permute-start.5) | collective-permute-done | bytes 131104 | tf_op jit(solution)/shard_map/ppermute | solution.py:107
  52.4 0.0 collective-permute-done.refs_0_
  52.4 1.1 collective-permute-done.4.refs_4_
  53.5 0.7 copy-done.3
  54.2 15.2 %forward.1 = (bf16[512,1024]{1,0:T(8,128)(2,1)}, bf16[512,1024]{1,0:T(8,128)(2,1)}, bf16[512,1024]{1,0:T(8,128)(2,1)}, f32[512,1024]{1,0:T(8,128)}, f32[512,1024...) custom-call(s32[3]{0:T(128)} %pad_add_fusion.pos, ...), custom_call_target="tpu_custom_call" | custom-call | flops 3221225472 | bytes 12582912 | tf_op jit(solution)/shard_map/forward/pallas_call | solution.py:240
  69.4 0.8 broadcast_in_dim.2
  70.2 19.8 %all_to_all.10.got = f32[32,4,1024]{2,1,0:T(4,128)} all-to-all(f32[32,4,1024]{2,1,0:T(4,128)S(1)} %broadcast_in_dim.2), channel_id=1, replica_groups=mesh['batch'=8,'tm'=8,'space'=4] {'tm','space'}, dimensions={0} | all-to-all | bytes 1048576 | tf_op jit(solution)/shard_map/all_to_all | solution.py:596
  90.0 3.6 %embed.1 = f32[8,4,896]{2,1,0:T(4,128)} custom-call(f32[32,4,1024]{2,1,0:T(4,128)} %all_to_all.10.got, bf16[1024,1024]{1,0:T(8,128)(2,1)} %w_out.3, bf16[1024,768]{1,0:T(8,128)(2,1)} %w_emb.3, bf16[2,768]{1,0:T(2,128)(2,1)} %text.1, s32[2,16]{1,0:T(2,128)} %bucket.1, f32[4]{0:T(128)} %levels.1), custom_call_target="tpu_custom_call" | custom-call | tf_op jit(solution)/shard_map/embed/pallas_call | solution.py:305
  93.6 16.0 %all_to_all.11.got = f32[8,4,896]{2,1,0:T(4,128)} all-to-all(f32[8,4,896]{2,1,0:T(4,128)} %embed.1), channel_id=1, replica_groups=mesh['batch'=8,'tm'=8,'space'=4] {'batch'}, dimensions={0} | all-to-all | bytes 229376 | tf_op jit(solution)/shard_map/all_to_all | solution.py:598
  109.5 4.5 %contrast.1 = (f32[2,768]{1,0:T(2,128)}, f32[1,1]{1,0:T(1,128)}, f32[2,1024]{1,0:T(2,128)}, f32[2,1024]{1,0:T(2,128)}) custom-call(s32[3]{0:T(128)} %pad_add_fusion.pos, f32[8,4,896]{2,1,0:T(4,128)} %all_to_all.11.got, bf16[1024,768]{1,0:T(8,128)(2,1)} %w_emb.3, bf16[1024,1024]{1,0:T(8,128)(2,1)} %w_out.3), custom_call_target="tpu_custom_call" | custom-call | tf_op jit(solution)/shard_map/contrast/pallas_call | solution.py:402
  114.1 20.1 %backward.1 = (bf16[4,4,16,1024]{3,2,1,0:T(8,128)(2,1)}, bf16[2,3,16,1024]{3,2,1,0:T(8,128)(2,1)}, bf16[3,2,16,1024]{3,2,1,0:T(8,128)(2,1)}, bf16[2,2,16,1024]{3...) custom-call(s32[2,3]{1,0:T(2,128)} %shifts.5, ...), custom_call_target="tpu_custom_call" | custom-call | flops 3221225472 | bytes 16777216 | tf_op jit(solution)/shard_map/backward/pallas_call | solution.py:512
  134.2 3.1 %collective-permute-start.8 = (bf16[2,2,16,1024]{3,2,1,0:T(8,128)(2,1)}, bf16[2,2,16,1024]{3,2,1,0:T(8,128)(2,1)S(1)}, u32[]{:S(2)}, u32[]{:S(2)}) collective-permute-start(bf16[2,2,16,1024]{3,2,1,0:T(8,128)(2,1)} %get-tuple-element.53), channel_id=1, source_target_pairs={{0,5},{1,6},{2,7},{3,4},{4,9},{5,10},{6,11},{7,8},{8,13},{9,14},{1... | collective-permute-start | bytes 393224 | tf_op jit(solution)/shard_map/ppermute | solution.py:107
  137.4 1.6 collective-permute-start.7
  138.9 2.0 %collective-permute-start.9 = (bf16[2,3,16,1024]{3,2,1,0:T(8,128)(2,1)}, bf16[2,3,16,1024]{3,2,1,0:T(8,128)(2,1)S(1)}, u32[]{:S(2)}, u32[]{:S(2)}) collective-permute-start(bf16[2,3,16,1024]{3,2,1,0:T(8,128)(2,1)} %get-tuple-element.54), channel_id=1, source_target_pairs={{0,28},{1,29},{2,30},{3,31},{4,0},{5,1},{6,2},{7,3},{8,4},{9,5},{1... | collective-permute-start | bytes 589832 | tf_op jit(solution)/shard_map/ppermute | solution.py:107
  140.9 0.8 collective-permute-start.10
  141.7 0.1 collective-permute-done.8.refs_4_
  141.8 1.6 collective-permute-start.11
  143.4 4.5 %collective-permute-done.11.refs_7_ = bf16[2,2,16,1024]{3,2,1,0:T(8,128)(2,1)S(1)} collective-permute-done((bf16[2,2,16,1024]{3,2,1,0:T(8,128)(2,1)}, bf16[2,2,16,1024]{3,2,1,0:T(8,128)(2,1)S(1)}, u32[]{:S(2)}, u32[]{:S(2)}) %collective-permute-start.11) | collective-permute-done | bytes 131104 | tf_op jit(solution)/shard_map/ppermute | solution.py:107
  147.9 0.1 collective-permute-done.6.refs_2_
  148.0 4.2 %collective-permute-done.7.refs_3_ = bf16[3,2,16,1024]{3,2,1,0:T(8,128)(2,1)S(1)} collective-permute-done((bf16[3,2,16,1024]{3,2,1,0:T(8,128)(2,1)}, bf16[3,2,16,1024]{3,2,1,0:T(8,128)(2,1)S(1)}, u32[]{:S(2)}, u32[]{:S(2)}) %collective-permute-start.7) | collective-permute-done | bytes 196640 | tf_op jit(solution)/shard_map/ppermute | solution.py:107
  152.2 1.4 collective-permute-done.9.refs_5_
  153.6 0.8 collective-permute-done.10.refs_6_
  154.4 0.6 copy-done.7
  155.0 2.6 %merge.1 = bf16[2,4,4,16,1024]{4,3,2,1,0:T(8,128)(2,1)} custom-call(s32[2,3]{1,0:T(2,128)} %shifts.5, bf16[4,4,16,1024]{3,2,1,0:T(8,128)(2,1)} %get-tuple-element.49.refs_0_, bf16[4,4,16,1024]{3,2,1,0:T(8,128)(2,1)} %get-tuple-element.50.refs_1_, bf16[2,3,16,1024]{3,2,1,0:T(8,128)(2,1)} %copy-done.4, bf16[3,2,16,1024]{3,2,1,0:T(8,128)(2,1)} %copy-done.5, ...), custom_call_target="tpu_custom_call" | custom-call | tf_op jit(solution)/shard_map/merge/pallas_call | solution.py:575
  (26 shorter events, 0.1 us)
Async XLA Ops:
  33.6 10.6 %collective-permute-start.2 = (bf16[2,2,16,1024]{3,2,1,0:T(8,128)(2,1)}, bf16[2,2,16,1024]{3,2,1,0:T(8,128)(2,1)S(1)}, u32[]{:S(2)}, u32[]{:S(2)}) collective-permute-start(bf16[2,2,16,1024]{3,2,1,0:T(8,128)(2,1)} %get-tuple-element.33), channel_id=1, source_target_pairs={{0,31},{1,28},{2,29},{3,30},{4,3},{5,0},{6,1},{7,2},{8,7},{9,4},{1... | collective-permute-start | bytes 393224 | tf_op jit(solution)/shard_map/ppermute | solution.py:107
  38.5 13.9 %collective-permute-start = (bf16[2,3,16,1024]{3,2,1,0:T(8,128)(2,1)}, bf16[2,3,16,1024]{3,2,1,0:T(8,128)(2,1)S(1)}, u32[]{:S(2)}, u32[]{:S(2)}) collective-permute-start(bf16[2,3,16,1024]{3,2,1,0:T(8,128)(2,1)} %get-tuple-element.31), channel_id=1, source_target_pairs={{0,28},{1,29},{2,30},{3,31},{4,0},{5,1},{6,2},{7,3},{8,4},{9,5},{1... | collective-permute-start | bytes 589832 | tf_op jit(solution)/shard_map/ppermute | solution.py:107
  38.7 13.7 %collective-permute-start.1 = (bf16[3,2,16,1024]{3,2,1,0:T(8,128)(2,1)}, bf16[3,2,16,1024]{3,2,1,0:T(8,128)(2,1)S(1)}, u32[]{:S(2)}, u32[]{:S(2)}) collective-permute-start(bf16[3,2,16,1024]{3,2,1,0:T(8,128)(2,1)} %get-tuple-element.32), channel_id=1, source_target_pairs={{0,3},{1,0},{2,1},{3,2},{4,7},{5,4},{6,5},{7,6},{8,11},{9,8},{10,9... | collective-permute-start | bytes 589832 | tf_op jit(solution)/shard_map/ppermute | solution.py:107
  39.9 12.5 %collective-permute-start.3 = (bf16[2,3,16,1024]{3,2,1,0:T(8,128)(2,1)}, bf16[2,3,16,1024]{3,2,1,0:T(8,128)(2,1)S(1)}, u32[]{:S(2)}, u32[]{:S(2)}) collective-permute-start(bf16[2,3,16,1024]{3,2,1,0:T(8,128)(2,1)} %get-tuple-element.34), channel_id=1, source_target_pairs={{0,4},{1,5},{2,6},{3,7},{4,8},{5,9},{6,10},{7,11},{8,12},{9,13},{1... | collective-permute-start | bytes 589832 | tf_op jit(solution)/shard_map/ppermute | solution.py:107
  41.5 11.9 %collective-permute-start.4 = (bf16[3,2,16,1024]{3,2,1,0:T(8,128)(2,1)}, bf16[3,2,16,1024]{3,2,1,0:T(8,128)(2,1)S(1)}, u32[]{:S(2)}, u32[]{:S(2)}) collective-permute-start(bf16[3,2,16,1024]{3,2,1,0:T(8,128)(2,1)} %get-tuple-element.35), channel_id=1, source_target_pairs={{0,1},{1,2},{2,3},{3,0},{4,5},{5,6},{6,7},{7,4},{8,9},{9,10},{10,1... | collective-permute-start | bytes 589832 | tf_op jit(solution)/shard_map/ppermute | solution.py:107
  44.1 9.4 %copy-start.8 = (bf16[2,2,16,1024]{3,2,1,0:T(8,128)(2,1)}, bf16[2,2,16,1024]{3,2,1,0:T(8,128)(2,1)S(1)}, u32[]{:S(2)}) copy-start(bf16[2,2,16,1024]{3,2,1,0:T(8,128)(2,1)S(1)} %collective-permute-done.2.refs_2_) | copy-start | bytes 393220
  44.1 8.2 %collective-permute-start.5 = (bf16[2,2,16,1024]{3,2,1,0:T(8,128)(2,1)}, bf16[2,2,16,1024]{3,2,1,0:T(8,128)(2,1)S(1)}, u32[]{:S(2)}, u32[]{:S(2)}) collective-permute-start(bf16[2,2,16,1024]{3,2,1,0:T(8,128)(2,1)} %get-tuple-element.36), channel_id=1, source_target_pairs={{0,5},{1,6},{2,7},{3,4},{4,9},{5,10},{6,11},{7,8},{8,13},{9,14},{1... | collective-permute-start | bytes 393224 | tf_op jit(solution)/shard_map/ppermute | solution.py:107
  52.4 1.1 copy-start.9
  52.4 1.1 copy-start
  52.4 1.1 copy-start.1
  52.4 1.1 copy-start.2
  53.5 0.7 copy-start.3
  134.2 7.6 %collective-permute-start.8 = (bf16[2,2,16,1024]{3,2,1,0:T(8,128)(2,1)}, bf16[2,2,16,1024]{3,2,1,0:T(8,128)(2,1)S(1)}, u32[]{:S(2)}, u32[]{:S(2)}) collective-permute-start(bf16[2,2,16,1024]{3,2,1,0:T(8,128)(2,1)} %get-tuple-element.53), channel_id=1, source_target_pairs={{0,5},{1,6},{2,7},{3,4},{4,9},{5,10},{6,11},{7,8},{8,13},{9,14},{1... | collective-permute-start | bytes 393224 | tf_op jit(solution)/shard_map/ppermute | solution.py:107
  137.4 10.6 %collective-permute-start.6 = (bf16[2,3,16,1024]{3,2,1,0:T(8,128)(2,1)}, bf16[2,3,16,1024]{3,2,1,0:T(8,128)(2,1)S(1)}, u32[]{:S(2)}, u32[]{:S(2)}) collective-permute-start(bf16[2,3,16,1024]{3,2,1,0:T(8,128)(2,1)} %get-tuple-element.51), channel_id=1, source_target_pairs={{0,4},{1,5},{2,6},{3,7},{4,8},{5,9},{6,10},{7,11},{8,12},{9,13},{1... | collective-permute-start | bytes 589832 | tf_op jit(solution)/shard_map/ppermute | solution.py:107
  137.4 14.8 %collective-permute-start.7 = (bf16[3,2,16,1024]{3,2,1,0:T(8,128)(2,1)}, bf16[3,2,16,1024]{3,2,1,0:T(8,128)(2,1)S(1)}, u32[]{:S(2)}, u32[]{:S(2)}) collective-permute-start(bf16[3,2,16,1024]{3,2,1,0:T(8,128)(2,1)} %get-tuple-element.52), channel_id=1, source_target_pairs={{0,1},{1,2},{2,3},{3,0},{4,5},{5,6},{6,7},{7,4},{8,9},{9,10},{10,1... | collective-permute-start | bytes 589832 | tf_op jit(solution)/shard_map/ppermute | solution.py:107
  138.9 14.7 %collective-permute-start.9 = (bf16[2,3,16,1024]{3,2,1,0:T(8,128)(2,1)}, bf16[2,3,16,1024]{3,2,1,0:T(8,128)(2,1)S(1)}, u32[]{:S(2)}, u32[]{:S(2)}) collective-permute-start(bf16[2,3,16,1024]{3,2,1,0:T(8,128)(2,1)} %get-tuple-element.54), channel_id=1, source_target_pairs={{0,28},{1,29},{2,30},{3,31},{4,0},{5,1},{6,2},{7,3},{8,4},{9,5},{1... | collective-permute-start | bytes 589832 | tf_op jit(solution)/shard_map/ppermute | solution.py:107
  140.9 13.4 %collective-permute-start.10 = (bf16[3,2,16,1024]{3,2,1,0:T(8,128)(2,1)}, bf16[3,2,16,1024]{3,2,1,0:T(8,128)(2,1)S(1)}, u32[]{:S(2)}, u32[]{:S(2)}) collective-permute-start(bf16[3,2,16,1024]{3,2,1,0:T(8,128)(2,1)} %get-tuple-element.55), channel_id=1, source_target_pairs={{0,3},{1,0},{2,1},{3,2},{4,7},{5,4},{6,5},{7,6},{8,11},{9,8},{10,9... | collective-permute-start | bytes 589832 | tf_op jit(solution)/shard_map/ppermute | solution.py:107
  141.8 12.6 %copy-start.10 = (bf16[2,2,16,1024]{3,2,1,0:T(8,128)(2,1)}, bf16[2,2,16,1024]{3,2,1,0:T(8,128)(2,1)S(1)}, u32[]{:S(2)}) copy-start(bf16[2,2,16,1024]{3,2,1,0:T(8,128)(2,1)S(1)} %collective-permute-done.8.refs_4_) | copy-start | bytes 393220
  141.8 6.1 %collective-permute-start.11 = (bf16[2,2,16,1024]{3,2,1,0:T(8,128)(2,1)}, bf16[2,2,16,1024]{3,2,1,0:T(8,128)(2,1)S(1)}, u32[]{:S(2)}, u32[]{:S(2)}) collective-permute-start(bf16[2,2,16,1024]{3,2,1,0:T(8,128)(2,1)} %get-tuple-element.56), channel_id=1, source_target_pairs={{0,31},{1,28},{2,29},{3,30},{4,3},{5,0},{6,1},{7,2},{8,7},{9,4},{1... | collective-permute-start | bytes 393224 | tf_op jit(solution)/shard_map/ppermute | solution.py:107
  147.9 6.5 %copy-start.11 = (bf16[2,2,16,1024]{3,2,1,0:T(8,128)(2,1)}, bf16[2,2,16,1024]{3,2,1,0:T(8,128)(2,1)S(1)}, u32[]{:S(2)}) copy-start(bf16[2,2,16,1024]{3,2,1,0:T(8,128)(2,1)S(1)} %collective-permute-done.11.refs_7_) | copy-start | bytes 393220
  148.0 6.4 %copy-start.4 = (bf16[2,3,16,1024]{3,2,1,0:T(8,128)(2,1)}, bf16[2,3,16,1024]{3,2,1,0:T(8,128)(2,1)S(1)}, u32[]{:S(2)}) copy-start(bf16[2,3,16,1024]{3,2,1,0:T(8,128)(2,1)S(1)} %collective-permute-done.6.refs_2_) | copy-start | bytes 589828
  152.2 2.1 %copy-start.5 = (bf16[3,2,16,1024]{3,2,1,0:T(8,128)(2,1)}, bf16[3,2,16,1024]{3,2,1,0:T(8,128)(2,1)S(1)}, u32[]{:S(2)}) copy-start(bf16[3,2,16,1024]{3,2,1,0:T(8,128)(2,1)S(1)} %collective-permute-done.7.refs_3_) | copy-start | bytes 589828
  153.6 0.8 copy-start.6
  154.4 0.7 copy-start.7

commit v2 on v1

v2 whole, which is shorter than its diff:
```python
from functools import partial

import jax
import jax.numpy as jnp
from jax import lax
from jax.experimental import pallas as pl
from jax.experimental.pallas import tpu as pltpu
from jax.sharding import PartitionSpec as P

HEADS = 16
HEAD_DIM = 64
D = 1024
EMB = 768
WT = 4
WH = 4
WW = 8
COLS = 16
HALO = 2
TOK = WT * WH * WW
QUADS = 4
QW = 256

SOFTMAX_TEMP = 0.07
NORM_EPS = 1e-05
QUERY_EPS = 1e-06
EMBED_EPS = 1e-06
LOG2E = 1.4426950408889634
F32 = jnp.float32
BF16 = jnp.bfloat16
VMEM_LIMIT = 24 * 1024 * 1024

NT = (((1,), (1,)), ((), ()))
TN = (((0,), (0,)), ((), ()))

GRID = 6
OWN = ((0, 4, 0, 4), (2, 4, 2, 4))
PIECES = (
    ((4, 2, 1, 3), (1, 3, 4, 2), (4, 2, 4, 2)),
    ((0, 2, 2, 3), (2, 3, 0, 2), (0, 2, 0, 2)),
)
GIVEN = (
    ((0, 2, 1, 3), (1, 3, 0, 2), (0, 2, 0, 2)),
    ((2, 2, 0, 3), (0, 3, 2, 2), (2, 2, 2, 2)),
)
PIECE_SHAPES = tuple((g[1], g[3], COLS, D) for g in GIVEN[0])


def vmem():
    return pl.BlockSpec(memory_space=pltpu.VMEM)


def smem():
    return pl.BlockSpec(memory_space=pltpu.SMEM)


def params(**more):
    return pltpu.CompilerParams(vmem_limit_bytes=VMEM_LIMIT, **more)


def pack_kernel(video, *outs):
    for c in range(2):
        for k in range(3):
            f, nf, r, nr = GIVEN[c][k]
            outs[3 * c + k][...] = video[c, f : f + nf, r : r + nr]


def pack(video):
    return pl.pallas_call(
        pack_kernel,
        out_shape=[jax.ShapeDtypeStruct(s, BF16) for s in PIECE_SHAPES * 2],
        in_specs=[vmem()],
        out_specs=[vmem()] * 6,
        compiler_params=params(),
        name="pack",
    )(video)


def exchange(pieces, clip, sign):
    tm, space = lax.axis_size("tm"), lax.axis_size("space")
    step = sign if clip == 0 else -sign
    out = []
    for piece, (dt, ds) in zip(pieces, ((step, 0), (0, step), (step, step))):
        pairs = [
            (t * space + s, ((t + dt) % tm) * space + (s + ds) % space)
            for t in range(tm)
            for s in range(space)
        ]
        out.append(lax.ppermute(piece, ("tm", "space"), pairs))
    return out


def head_blocks(shape, width):
    row = lax.broadcasted_iota(jnp.int32, shape, 0) // width
    lane = lax.broadcasted_iota(jnp.int32, shape, 1) // HEAD_DIM
    return (row == lane).astype(F32).astype(BF16)


def low_lanes(shape):
    return lax.broadcasted_iota(jnp.int32, shape, 1) < HEAD_DIM


def split_heads(pair):
    low = low_lanes((1, 2 * HEAD_DIM)).astype(F32)
    return jnp.concatenate(
        [pair * low.astype(BF16), pair * (1.0 - low).astype(BF16)], axis=0
    )


def window_mask(frame0, row0, col0, s0, s1, s2, frames, rows):
    shape = (TOK, 2 * TOK)

    def label(index):
        f = frame0 + index // (WH * WW) + s0
        r = row0 + (index // WW) % WH + s1
        c = col0 + index % WW + s2
        one = lambda v, n: jnp.where((v < 0) | (v >= n), 1, 0)
        return one(f, frames) * 4 + one(r, rows) * 2 + one(c, COLS)

    key = lax.broadcasted_iota(jnp.int32, shape, 0)
    query = lax.broadcasted_iota(jnp.int32, shape, 1) % TOK
    return jnp.where(label(key) == label(query), 1.0, 0.0)


def forward_kernel(clips, frames, rows_all, pos, shifts, hscale, video, *refs):
    nc = len(clips)
    halo = refs[: 3 * nc]
    w_qkv = refs[3 * nc]
    ql, kl, vl, rq, rk, mass, prob, n32, istd, sums = refs[3 * nc + 1 : 3 * nc + 11]
    ext, xb, masks, ones4, ones2, qs, ks = refs[3 * nc + 11 :]
    ones4[...] = head_blocks((QW, QW), HEAD_DIM)
    ones2[...] = head_blocks((2 * TOK, 2 * HEAD_DIM), TOK)
    for n, c in enumerate(clips):
        f, nf, r, nr = OWN[c]
        ext[n, f : f + nf, r : r + nr] = video[c]
        for k in range(3):
            f, nf, r, nr = PIECES[c][k]
            ext[n, f : f + nf, r : r + nr] = halo[3 * n + k][...]
        s0, s1, s2 = shifts[c, 0], shifts[c, 1], shifts[c, 2]
        off0, off1 = s0 + HALO * c, s1 + HALO * c
        turn = (COLS - s2) % COLS

        def cells(half, total):
            for j in range(2 * WH):
                a, b = 2 * half + j // WH, j % WH
                x = ext[n, a + off0, b + off1].astype(F32)
                total = total + x
                x = pltpu.roll(x, turn, 0)
                centered = x - jnp.mean(x, axis=-1, keepdims=True)
                inv = lax.rsqrt(
                    jnp.mean(centered * centered, axis=-1, keepdims=True) + NORM_EPS
                )
                y = centered * inv
                wide = jnp.broadcast_to(inv, (COLS, 128))
                for w in range(2):
                    start = pl.multiple_of((2 * n + w) * TOK + a * (WH * WW) + b * WW, WW)
                    n32[pl.ds(start, WW)] = y[w * WW : (w + 1) * WW]
                    istd[pl.ds(start, WW)] = wide[w * WW : (w + 1) * WW]
            return total

        total = lax.fori_loop(0, WT // 2, cells, jnp.zeros((COLS, D), F32))
        sums[2 * n : 2 * n + 1] = jnp.sum(total, axis=0, keepdims=True)
        for w in range(2):
            masks[2 * n + w] = window_mask(
                pos[0] * WT, pos[1] * WH, w * WW, s0, s1, s2, frames, rows_all
            )
    xb[...] = n32[...].astype(BF16)
    lane = lax.broadcasted_iota(jnp.int32, (1, 2 * TOK), 1)

    def project(quad):
        jobs = []
        at_quad = slice(quad * QW, (quad + 1) * QW)
        for part in range(3):

            def job(part=part):
                w = w_qkv[:, part * D + quad * QW : part * D + (quad + 1) * QW]
                value = jnp.dot(xb[...], w, preferred_element_type=F32)
                if part == 2:
                    vl[:, at_quad] = value.astype(BF16)
                else:
                    (qs, ks)[part][...] = value

            jobs.append(job)
        for part in range(2):
            for w in range(2 * nc):

                def job(part=part, w=w):
                    at = slice(w * TOK, (w + 1) * TOK)
                    full, unit, inverse = ((qs, ql, rq), (ks, kl, rk))[part]
                    value = full[at]
                    square = jnp.dot(
                        (value * value).astype(BF16), ones4[...], preferred_element_type=F32
                    )
                    inv = lax.rsqrt(square + QUERY_EPS)
                    inverse[at, at_quad] = inv
                    unit[at, at_quad] = (value * inv).astype(BF16)

                jobs.append(job)
        return jobs

    def attend(quad):
        firsts, seconds = [], []
        for p in range(2):
            head = quad * 4 + 2 * p
            lanes = slice(quad * QW + p * 128, quad * QW + (p + 1) * 128)
            for w in range(2 * nc):
                at = slice(w * TOK, (w + 1) * TOK)
                held = {}

                def first(head=head, lanes=lanes, w=w, at=at, p=p, held=held):
                    factor = jnp.where(lane < TOK, hscale[head], hscale[head + 1]) * LOG2E
                    score = lax.dot_general(
                        kl[at, lanes], split_heads(ql[at, lanes]), NT, preferred_element_type=F32
                    )
                    e = jnp.exp2(score * factor) * masks[w]
                    held["e"] = e
                    held["inv"] = 1.0 / jnp.sum(e, axis=0, keepdims=True)

                def second(lanes=lanes, w=w, at=at, p=p, held=held):
                    pt = held["e"] * held["inv"]
                    prob[quad, 2 * w + p] = pt
                    mass_here = jnp.dot(pt.astype(BF16), ones2[...], preferred_element_type=F32)
                    mass[at, lanes] = mass_here
                    gathered = jnp.sum(
                        mass_here * vl[at, lanes].astype(F32), axis=0, keepdims=True
                    )
                    row = slice(w // 2 * 2 + 1, w // 2 * 2 + 2)
                    if w % 2:
                        sums[row, lanes] = sums[row, lanes] + gathered
                    else:
                        sums[row, lanes] = gathered

                firsts.append(first)
                seconds.append(second)
        return staged(firsts, seconds)

    interleave(project(0))
    for quad in range(QUADS):
        interleave(attend(quad), project(quad + 1) if quad + 1 < QUADS else [])


def staged(*stages, lag=3):
    count = len(stages[0])
    jobs = []
    for turn in range(count + lag * (len(stages) - 1)):
        for depth, stage in enumerate(stages):
            unit = turn - lag * depth
            if 0 <= unit < count:
                jobs.append(stage[unit])
    return jobs


def interleave(*lists):
    order = []
    for which, jobs in enumerate(lists):
        for k, job in enumerate(jobs):
            order.append(((k + 0.5) / len(jobs), which, k, job))
    for item in sorted(order, key=lambda t: t[:3]):
        item[3]()


def forward(clips, pos, shifts, hscale, video, halo, w_qkv):
    nc = len(clips)
    n = nc * 2 * TOK
    frames = lax.axis_size("tm") * WT
    rows_all = lax.axis_size("space") * WH
    return pl.pallas_call(
        partial(forward_kernel, clips, frames, rows_all),
        out_shape=[jax.ShapeDtypeStruct((n, D), BF16)] * 3
        + [jax.ShapeDtypeStruct((n, D), F32)] * 3
        + [
            jax.ShapeDtypeStruct((QUADS, 4 * nc, TOK, 2 * TOK), F32),
            jax.ShapeDtypeStruct((n, D), F32),
            jax.ShapeDtypeStruct((n, 128), F32),
            jax.ShapeDtypeStruct((2 * nc, D), F32),
        ],
        in_specs=[smem(), smem(), smem()] + [vmem()] * (2 + 3 * nc),
        out_specs=[vmem()] * 10,
        scratch_shapes=[
            pltpu.VMEM((nc, GRID, GRID, COLS, D), BF16),
            pltpu.VMEM((n, D), BF16),
            pltpu.VMEM((2 * nc, TOK, 2 * TOK), F32),
            pltpu.VMEM((QW, QW), BF16),
            pltpu.VMEM((2 * TOK, 2 * HEAD_DIM), BF16),
            pltpu.VMEM((n, QW), F32),
            pltpu.VMEM((n, QW), F32),
        ],
        compiler_params=params(),
        cost_estimate=pl.CostEstimate(
            flops=2 * n * D * 3 * D, bytes_accessed=12 * 2**20, transcendentals=n * 2048
        ),
        name="forward",
    )(pos, shifts, hscale, video, *halo, w_qkv)


def embed_kernel(tokens, got, w_out, w_emb, text, bucket, levels, out):
    total = jnp.sum(got[...], axis=0)
    mean = (jnp.concatenate([total[1:2], total[3:4]], axis=0) / tokens).astype(BF16)
    token_mean = jnp.concatenate([total[0:1], total[2:3]], axis=0) / tokens
    pooled = token_mean + jnp.dot(mean, w_out[...], preferred_element_type=F32)
    embedded = jnp.dot(pooled.astype(BF16), w_emb[...], preferred_element_type=F32)
    held = bucket[...]
    weight = jnp.zeros(held.shape, F32)
    for level in range(levels.shape[0]):
        weight = weight + jnp.where(held == level, levels[level], 0.0)
    weight = jnp.concatenate(
        [weight, jnp.zeros((held.shape[0], 128 - held.shape[1]), F32)], axis=1
    )
    words = text[...].astype(F32)
    block = jnp.concatenate(
        [
            jnp.concatenate([embedded, weight], axis=1),
            jnp.concatenate([words, jnp.zeros_like(weight)], axis=1),
        ],
        axis=0,
    )
    for peer in range(out.shape[0]):
        out[peer] = block


def embed(got, w_out, w_emb, text, bucket, levels, tokens, peers):
    return pl.pallas_call(
        partial(embed_kernel, tokens),
        out_shape=jax.ShapeDtypeStruct((peers, 4, EMB + 128), F32),
        in_specs=[vmem()] * 5 + [smem()],
        out_specs=vmem(),
        compiler_params=params(),
        name="embed",
    )(got, w_out, w_emb, text, bucket, levels)


def three_parts(wide):
    high = wide.astype(BF16)
    rest = wide - high.astype(F32)
    middle = rest.astype(BF16)
    low = (rest - middle.astype(F32)).astype(BF16)
    return jnp.concatenate([high, middle, low], axis=0)


def full_dot(wide, weight):
    n = wide.shape[0]
    got = lax.dot_general(three_parts(wide), weight, NT, preferred_element_type=F32)
    return got[:n] + got[n : 2 * n] + got[2 * n :]


def contrast_kernel(pos, got, w_emb, w_out, text_grad, loss, clip_grad, d_out):
    peers = got.shape[0]
    n = 2 * peers
    embedded = jnp.concatenate([got[p, 0:2, :EMB] for p in range(peers)], axis=0)
    weights = jnp.concatenate([got[p, 0:2, EMB:] for p in range(peers)], axis=0)[:, :n]
    words = jnp.concatenate([got[p, 2:4, :EMB] for p in range(peers)], axis=0)
    clip_norm = jnp.sqrt(jnp.sum(embedded * embedded, axis=-1, keepdims=True) + EMBED_EPS)
    text_norm = jnp.sqrt(jnp.sum(words * words, axis=-1, keepdims=True) + EMBED_EPS)
    clip_unit = embedded / clip_norm
    text_unit = words / text_norm
    exact = lax.Precision.HIGHEST
    logits = (
        lax.dot_general(clip_unit, text_unit, NT, precision=exact, preferred_element_type=F32)
        / SOFTMAX_TEMP
    )
    own = lax.broadcasted_iota(jnp.int32, (n, n), 0) == lax.broadcasted_iota(
        jnp.int32, (n, n), 1
    )
    exp_logit = jnp.exp(logits)
    other = jnp.where(own, 0.0, weights)
    negative = other * exp_logit
    diagonal = jnp.where(own, logits, 0.0)
    row_self = jnp.sum(diagonal, axis=1, keepdims=True)
    col_self = jnp.sum(diagonal, axis=0, keepdims=True)
    row_weight = jnp.sum(other, axis=1, keepdims=True)
    col_weight = jnp.sum(other, axis=0, keepdims=True)
    row_part = (
        jnp.exp(row_self) + (n - 1) * jnp.sum(negative, axis=1, keepdims=True) / row_weight
    )
    col_part = (
        jnp.exp(col_self) + (n - 1) * jnp.sum(negative, axis=0, keepdims=True) / col_weight
    )
    summed = jnp.sum(jnp.log(row_part) - row_self, axis=0, keepdims=True) + jnp.sum(
        jnp.log(col_part) - col_self, axis=1, keepdims=True
    )
    loss[...] = summed / (2 * n)
    scaled = (n - 1) * weights * exp_logit
    off = scaled * (1.0 / (row_weight * row_part)) + scaled * (1.0 / (col_weight * col_part))
    on = exp_logit / row_part - 1.0 + exp_logit / col_part - 1.0
    grad = jnp.where(own, on, off)
    d_clip = (
        jnp.dot(grad, text_unit, precision=exact, preferred_element_type=F32) / SOFTMAX_TEMP
    )
    d_text = (
        lax.dot_general(grad, clip_unit, TN, precision=exact, preferred_element_type=F32)
        / SOFTMAX_TEMP
    )
    text_all = (
        d_text - text_unit * jnp.sum(text_unit * d_text, axis=-1, keepdims=True)
    ) / text_norm
    embed_all = (
        d_clip - clip_unit * jnp.sum(clip_unit * d_clip, axis=-1, keepdims=True)
    ) / clip_norm
    row = lax.broadcasted_iota(jnp.int32, (n, 1), 0)

    def mine(array):
        return jnp.concatenate(
            [
                jnp.sum(
                    jnp.where(row == 2 * pos[2] + c, array, 0.0), axis=0, keepdims=True
                )
                for c in range(2)
            ],
            axis=0,
        )

    text_grad[...] = mine(text_all)
    pooled_grad = full_dot(mine(embed_all), w_emb[...])
    clip_grad[...] = pooled_grad
    d_out[...] = full_dot(pooled_grad, w_out[...])


def contrast(pos, got, w_emb, w_out):
    return pl.pallas_call(
        contrast_kernel,
        out_shape=[
            jax.ShapeDtypeStruct((2, EMB), F32),
            jax.ShapeDtypeStruct((1, 1), F32),
            jax.ShapeDtypeStruct((2, D), F32),
            jax.ShapeDtypeStruct((2, D), F32),
        ],
        in_specs=[smem(), vmem(), vmem(), vmem()],
        out_specs=[vmem()] * 4,
        compiler_params=params(),
        name="contrast",
    )(pos, got, w_emb, w_out)


def backward_kernel(clips, shifts, hscale, clip_grad, d_out, *refs):
    nc = len(clips)
    ql, kl, vl, rq, rk, mass, prob, n32, istd, w_qkv = refs[:10]
    outs = refs[10 : 10 + 4 * nc]
    ext, total, ones4, dqs, dks, dqb, dkb, dvb = refs[10 + 4 * nc :]
    rows = nc * 2 * TOK
    ones4[...] = head_blocks((QW, QW), HEAD_DIM)
    low = low_lanes((TOK, 128))
    upper = lax.broadcasted_iota(jnp.int32, (128, TOK), 0) < HEAD_DIM
    lane = lax.broadcasted_iota(jnp.int32, (1, 128), 1)

    def attend(quad):
        firsts, seconds, thirds, norms = [], [], [], []
        for n, c in enumerate(clips):
            for p in range(2):
                head = quad * 4 + 2 * p
                lanes = slice(quad * QW + p * 128, quad * QW + (p + 1) * 128)
                factor = jnp.where(lane < HEAD_DIM, hscale[head], hscale[head + 1])
                shared = {}
                for w in range(2 * n, 2 * n + 2):
                    at = slice(w * TOK, (w + 1) * TOK)
                    held = {}

                    def first(lanes=lanes, w=w, p=p, c=c, at=at, shared=shared, held=held):
                        if not shared:
                            row = d_out[c : c + 1, lanes].astype(BF16).astype(F32)
                            spread = jnp.transpose(jnp.broadcast_to(row, (TOK, 128)))
                            shared["row"] = row
                            shared["spread"] = jnp.concatenate(
                                [jnp.where(upper, spread, 0.0), jnp.where(upper, 0.0, spread)],
                                axis=1,
                            ).astype(BF16)
                        along = jnp.dot(
                            vl[at, lanes], shared["spread"], preferred_element_type=F32
                        )
                        pt = prob[quad, 2 * w + p]
                        inner = jnp.sum(pt * along, axis=0, keepdims=True)
                        held["ds"] = (pt * (along - inner)).astype(BF16)
                        dvb[at, lanes] = (mass[at, lanes] * shared["row"]).astype(BF16)

                    def second(lanes=lanes, at=at, factor=factor, held=held):
                        ds = held["ds"]
                        dk = jnp.dot(ds, split_heads(ql[at, lanes]), preferred_element_type=F32)
                        dks[at, lanes] = dk * factor
                        held["turned"] = jnp.concatenate(
                            [jnp.transpose(ds[:, :TOK]), jnp.transpose(ds[:, TOK:])], axis=1
                        )

                    def third(lanes=lanes, at=at, factor=factor, held=held):
                        dq = jnp.dot(
                            held["turned"],
                            split_heads(kl[at, lanes]),
                            preferred_element_type=F32,
                        )
                        dqs[at, lanes] = dq * factor

                    firsts.append(first)
                    seconds.append(second)
                    thirds.append(third)
            for w in range(2 * n, 2 * n + 2):
                for part in range(2):

                    def job(w=w, part=part):
                        unit, grad, inverse, done = (
                            (ql, dqs, rq, dqb),
                            (kl, dks, rk, dkb),
                        )[part]
                        at = slice(w * TOK, (w + 1) * TOK)
                        q = slice(quad * QW, (quad + 1) * QW)
                        u = unit[at, q].astype(F32)
                        g = grad[at, q]
                        inner = jnp.dot(
                            (u * g).astype(BF16), ones4[...], preferred_element_type=F32
                        )
                        done[at, q] = ((g - u * inner) * inverse[at, q]).astype(BF16)

                    norms.append(job)
        return staged(firsts, seconds, thirds, lag=2) + norms

    def collect(quad):
        jobs = []
        for part in range(0, D, QW):

            def job(part=part):
                cols = slice(part, part + QW)
                got = None
                for k, grad in enumerate((dqb, dkb, dvb)):
                    term = lax.dot_general(
                        grad[:, quad * QW : (quad + 1) * QW],
                        w_qkv[cols, k * D + quad * QW : k * D + (quad + 1) * QW],
                        NT,
                        preferred_element_type=F32,
                    )
                    got = term if got is None else got + term
                total[:, cols] = got if quad == 0 else total[:, cols] + got

            jobs.append(job)
        return jobs

    for quad in range(QUADS):
        interleave(attend(quad), collect(quad - 1) if quad else [])
    interleave(collect(QUADS - 1))
    for n, c in enumerate(clips):
        s0, s1, s2 = shifts[c, 0], shifts[c, 1], shifts[c, 2]
        off0, off1 = s0 + HALO * c, s1 + HALO * c
        turn = (COLS + s2) % COLS
        base = clip_grad[c : c + 1]

        def cells(half, carry):
            for j in range(2 * WH):
                a, b = 2 * half + j // WH, j % WH
                halves = []
                for w in range(2):
                    start = pl.multiple_of((2 * n + w) * TOK + a * (WH * WW) + b * WW, WW)
                    dn = total[pl.ds(start, WW)]
                    y = n32[pl.ds(start, WW)]
                    inv = istd[pl.ds(start, WW)][:, :1]
                    first = jnp.mean(dn, axis=-1, keepdims=True)
                    second = jnp.mean(dn * y, axis=-1, keepdims=True)
                    halves.append(base + inv * (dn - first - y * second))
                cell = pltpu.roll(jnp.concatenate(halves, axis=0), turn, 0)
                ext[n, a + off0, b + off1] = cell.astype(BF16)
            return carry

        lax.fori_loop(0, WT // 2, cells, 0)
        f, nf, r, nr = OWN[c]
        outs[4 * n][...] = ext[n, f : f + nf, r : r + nr]
        for k in range(3):
            f, nf, r, nr = PIECES[c][k]
            outs[4 * n + 1 + k][...] = ext[n, f : f + nf, r : r + nr]


def backward(clips, shifts, hscale, clip_grad, d_out, stored, w_qkv):
    nc = len(clips)
    n = nc * 2 * TOK
    shapes = ((WT, WH, COLS, D),) + PIECE_SHAPES
    return pl.pallas_call(
        partial(backward_kernel, clips),
        out_shape=[jax.ShapeDtypeStruct(s, BF16) for s in shapes * nc],
        in_specs=[smem(), smem()] + [vmem()] * 12,
        out_specs=[vmem()] * (4 * nc),
        scratch_shapes=[
            pltpu.VMEM((nc, GRID, GRID, COLS, D), BF16),
            pltpu.VMEM((n, D), F32),
            pltpu.VMEM((QW, QW), BF16),
            pltpu.VMEM((n, D), F32),
            pltpu.VMEM((n, D), F32),
            pltpu.VMEM((n, D), BF16),
            pltpu.VMEM((n, D), BF16),
            pltpu.VMEM((n, D), BF16),
        ],
        compiler_params=params(),
        cost_estimate=pl.CostEstimate(
            flops=2 * n * D * 3 * D, bytes_accessed=16 * 2**20, transcendentals=0
        ),
        name="backward",
    )(shifts, hscale, clip_grad, d_out, *stored, w_qkv)


def merge_kernel(shifts, *refs):
    own, got, out = refs[:2], refs[2:8], refs[8]
    for c in range(2):
        s0, s1 = shifts[c, 0], shifts[c, 1]
        a, b, corner = got[3 * c : 3 * c + 3]
        for f in range(WT):
            for r in range(WH):
                if c == 0:
                    far_f, far_r = f < HALO, r < HALO
                    gone_f, gone_r = f < s0, r < s1
                    at_a, at_b, at_c = (f, r - 1), (f - 1, r), (f, r)
                else:
                    far_f, far_r = f >= WT - HALO, r >= WH - HALO
                    gone_f, gone_r = f >= WT + s0, r >= WH + s1
                    at_a, at_b, at_c = (f - 2, r), (f, r - 2), (f - 2, r - 2)
                value = own[c][f, r]
                in_a = far_f and 0 <= at_a[1] < 3
                in_b = far_r and 0 <= at_b[0] < 3
                if in_a:
                    take = jnp.logical_and(gone_f, jnp.logical_not(gone_r))
                    value = jnp.where(take, a[at_a], value)
                if in_b:
                    take = jnp.logical_and(jnp.logical_not(gone_f), gone_r)
                    value = jnp.where(take, b[at_b], value)
                if far_f and far_r:
                    value = jnp.where(jnp.logical_and(gone_f, gone_r), corner[at_c], value)
                out[c, f, r] = value


def merge(shifts, own, got):
    return pl.pallas_call(
        merge_kernel,
        out_shape=jax.ShapeDtypeStruct((2, WT, WH, COLS, D), BF16),
        in_specs=[smem()] + [vmem()] * 8,
        out_specs=vmem(),
        compiler_params=params(),
        name="merge",
    )(shifts, *own, *got)


def local(video, shifts, head_scale, w_qkv, w_out, w_emb, text, bucket, bucket_scale):
    tokens = lax.axis_size("tm") * lax.axis_size("space") * WT * WH * COLS
    plane = lax.axis_size("tm") * lax.axis_size("space")
    peers = lax.axis_size("batch")
    pos = jnp.stack(
        [lax.axis_index("tm"), lax.axis_index("space"), lax.axis_index("batch")]
    ).astype(jnp.int32)
    pieces = pack(video)
    halo = exchange(pieces[:3], 0, -1) + exchange(pieces[3:], 1, -1)
    *stored, sums = forward((0, 1), pos, shifts, head_scale, video, halo, w_qkv)
    spread = jnp.broadcast_to(sums[None], (plane,) + sums.shape)
    got = lax.all_to_all(spread, ("tm", "space"), 0, 0)
    packed = embed(got, w_out, w_emb, text, bucket, bucket_scale, tokens, peers)
    got = lax.all_to_all(packed, "batch", 0, 0)
    text_grad, loss, clip_grad, d_out = contrast(pos, got, w_emb, w_out)
    outs = backward((0, 1), shifts, head_scale, clip_grad, d_out, stored, w_qkv)
    back = exchange(outs[1:4], 0, 1) + exchange(outs[5:8], 1, 1)
    video_grad = merge(shifts, (outs[0], outs[4]), back)
    return (video_grad, text_grad, loss[0, 0])


def solution(mesh):
    in_specs = (
        P("batch", "tm", "space", None, None),
        P("batch", None),
        P(),
        P(),
        P(),
        P(),
        P("batch", None),
        P("batch", None),
        P(),
    )
    out_specs = (P("batch", "tm", "space", None, None), P("batch", None), P())
    return jax.shard_map(local, mesh=mesh, in_specs=in_specs, out_specs=out_specs, check_vma=False)
```

time: 158 us -> 108 us (0.68)
  Pallas kernels: 79 us -> 22.2 us
  local copies, waits for them, and re-layouts: 2.18 us -> 11.4 us
    pallas_call x1, Pallas kernels: 32.9 us -> 0.07 us  [pack(): pl.pallas_call(pack_kernel, out_shape=[jax.ShapeDtypeStruct(s, BF16) for...]
    pallas_call x2, Pallas kernels: 35.3 us -> 16.5 us  [the longest x1 8.88 us: backward(): pl.pallas_call(partial(backward_kernel, clips), out_shape=[jax.ShapeDtype...]
    unnamed x24 -> x38, local copies, waits for them, and re-layouts: 1.35 us -> 11.3 us
    pallas_call x1, Pallas kernels: 3.61 us -> 1.28 us  [embed(): pl.pallas_call(partial(embed_kernel, tokens), out_shape=jax.ShapeDtypeStr...]
    pallas_call x1, Pallas kernels: 4.54 us -> 2.72 us  [contrast(): pl.pallas_call(contrast_kernel, out_shape=[jax.ShapeDtypeStruct((2, EMB),...]
  transfers between devices with their start and end apart: 12 -> 12, of which waited for: 8 -> 7; matrix products, arithmetic and copies ran while one was open for 0% -> 0% of each run, Pallas kernels for 0% -> 0%
where the time goes in v2:
time: 108 us
  blocking collectives  35.5 us (33%)
  Pallas kernels  22.2 us (21%)
  starting transfers between devices  20 us (19%)
  waiting for transfers between devices  18.1 us (17%)
  local copies, waits for them, and re-layouts  11.4 us (11%)
    ppermute x12, starting transfers between devices, exchange(): out.append(lax.ppermute(piece, ('tm', 'space'), pairs))  20 us
    all_to_all x1, blocking collectives, local(): got = lax.all_to_all(spread, ('tm', 'space'), 0, 0)  19.7 us
    ppermute x12, waiting for transfers between devices, exchange(): out.append(lax.ppermute(piece, ('tm', 'space'), pairs))  18.1 us
    all_to_all x1, blocking collectives, local(): got = lax.all_to_all(packed, 'batch', 0, 0)  15.8 us
    unnamed x38, local copies, waits for them, and re-layouts  11.3 us
    pallas_call x1, Pallas kernels, backward(): pl.pallas_call(partial(backward_kernel, clips), out_shape=[jax.ShapeDtype...  8.88 us
    pallas_call x1, Pallas kernels, forward(): pl.pallas_call(partial(forward_kernel, clips, frames, rows_all), out_shap...  7.62 us
    pallas_call x1, Pallas kernels, contrast(): pl.pallas_call(contrast_kernel, out_shape=[jax.ShapeDtypeStruct((2, EMB),...  2.72 us
  transfers between devices with their start and end apart: 12, of which 7 were waited for; matrix products, arithmetic and copies ran while one was open for 0% of the time, Pallas kernels for 0%

profile of v2, /device:TPU:1, one launch (start us, length us, event | category | flops | bytes accessed | tf_op | source)
XLA Modules:
  0.0 108.1 jit_solution(9688084986091965920)
XLA Ops:
  0.6 1.2 %copy-done.4 = bf16[2,4,4,16,1024]{4,3,2,1,0:T(8,128)(2,1)S(1)} copy-done((bf16[2,4,4,16,1024]{4,3,2,1,0:T(8,128)(2,1)S(1)}, bf16[2,4,4,16,1024]{4,3,2,1,0:T(8,128)(2,1)}, u32[]{:S(2)}) %copy-start.4) | copy-done | bytes 1048600
  1.9 5.0 %collective-permute-start.2 = (bf16[2,2,16,1024]{3,2,1,0:T(8,128)(2,1)S(1)}, bf16[2,2,16,1024]{3,2,1,0:T(8,128)(2,1)S(1)}, u32[]{:S(2)}, u32[]{:S(2)}) collective-permute-start(bf16[2,2,16,1024]{3,2,1,0:T(8,128)(2,1)S(1)} %get-tuple-element.33), channel_id=1, source_target_pairs={{0,31},{1,28},{2,29},{3,30},{4,3},{5,0},{6,1},{7,2},{8,7},{9,4},{1... | collective-permute-start | bytes 393224 | tf_op jit(solution)/shard_map/ppermute | solution.py:88
  7.1 1.2 %collective-permute-start.1 = (bf16[3,2,16,1024]{3,2,1,0:T(8,128)(2,1)S(1)}, bf16[3,2,16,1024]{3,2,1,0:T(8,128)(2,1)S(1)}, u32[]{:S(2)}, u32[]{:S(2)}) collective-permute-start(bf16[3,2,16,1024]{3,2,1,0:T(8,128)(2,1)S(1)} %get-tuple-element.32), channel_id=1, source_target_pairs={{0,3},{1,0},{2,1},{3,2},{4,7},{5,4},{6,5},{7,6},{8,11},{9,8},{10,9... | collective-permute-start | bytes 589832 | tf_op jit(solution)/shard_map/ppermute | solution.py:88
  8.3 1.6 %collective-permute-start.3 = (bf16[2,3,16,1024]{3,2,1,0:T(8,128)(2,1)S(1)}, bf16[2,3,16,1024]{3,2,1,0:T(8,128)(2,1)S(1)}, u32[]{:S(2)}, u32[]{:S(2)}) collective-permute-start(bf16[2,3,16,1024]{3,2,1,0:T(8,128)(2,1)S(1)} %get-tuple-element.34), channel_id=1, source_target_pairs={{0,4},{1,5},{2,6},{3,7},{4,8},{5,9},{6,10},{7,11},{8,12},{9,13},{1... | collective-permute-start | bytes 589832 | tf_op jit(solution)/shard_map/ppermute | solution.py:88
  9.9 2.6 %collective-permute-start.4 = (bf16[3,2,16,1024]{3,2,1,0:T(8,128)(2,1)S(1)}, bf16[3,2,16,1024]{3,2,1,0:T(8,128)(2,1)S(1)}, u32[]{:S(2)}, u32[]{:S(2)}) collective-permute-start(bf16[3,2,16,1024]{3,2,1,0:T(8,128)(2,1)S(1)} %get-tuple-element.35), channel_id=1, source_target_pairs={{0,1},{1,2},{2,3},{3,0},{4,5},{5,6},{6,7},{7,4},{8,9},{9,10},{10,1... | collective-permute-start | bytes 589832 | tf_op jit(solution)/shard_map/ppermute | solution.py:88
  12.5 0.6 copy-done.15
  13.5 7.0 %collective-permute-done.5.refs_5_ = bf16[2,2,16,1024]{3,2,1,0:T(8,128)(2,1)S(1)} collective-permute-done((bf16[2,2,16,1024]{3,2,1,0:T(8,128)(2,1)S(1)}, bf16[2,2,16,1024]{3,2,1,0:T(8,128)(2,1)S(1)}, u32[]{:S(2)}, u32[]{:S(2)}) %collective-permute-start.5) | collective-permute-done | bytes 131104 | tf_op jit(solution)/shard_map/ppermute | solution.py:88
  20.6 0.6 copy-done.17
  21.5 0.7 copy-done.13
  22.2 2.8 %copy-done.1 = bf16[1024,3072]{1,0:T(8,128)(2,1)S(1)} copy-done((bf16[1024,3072]{1,0:T(8,128)(2,1)S(1)}, bf16[1024,3072]{1,0:T(8,128)(2,1)}, u32[]{:S(2)}) %copy-start.1) | copy-done | bytes 6291480
  25.0 1.2 %copy-done.5 = bf16[2,4,4,16,1024]{4,3,2,1,0:T(8,128)(2,1)S(1)} copy-done((bf16[2,4,4,16,1024]{4,3,2,1,0:T(8,128)(2,1)S(1)}, bf16[2,4,4,16,1024]{4,3,2,1,0:T(8,128)(2,1)}, u32[]{:S(2)}) %copy-start.5) | copy-done | bytes 1048600
  26.2 0.7 copy-done.6
  26.9 0.7 copy-done.10
  27.6 0.9 copy-done.14
  28.5 0.9 copy-done.16
  29.4 0.9 copy-done.18
  30.3 7.6 %forward.1 = (bf16[512,1024]{1,0:T(8,128)(2,1)S(1)}, bf16[512,1024]{1,0:T(8,128)(2,1)S(1)}, bf16[512,1024]{1,0:T(8,128)(2,1)S(1)}, f32[512,1024]{1,0:T(8,128)S(1...) custom-call(s32[3]{0:T(128)S(1)} %pad_add_fusion.pos, ...), custom_call_target="tpu_custom_call" | custom-call | flops 3221225472 | bytes 12582912 | tf_op jit(solution)/shard_map/forward/pallas_call | solution.py:266
  38.0 19.7 %all_to_all.10.got = f32[32,4,1024]{2,1,0:T(4,128)S(1)} all-to-all(f32[32,4,1024]{2,1,0:T(4,128)S(1)} %broadcast_in_dim.2), channel_id=1, replica_groups=mesh['batch'=8,'tm'=8,'space'=4] {'tm','space'}, dimensions={0} | all-to-all | bytes 1048576 | tf_op jit(solution)/shard_map/all_to_all | solution.py:643
  57.8 1.3 %embed.1 = f32[8,4,896]{2,1,0:T(4,128)S(1)} custom-call(f32[32,4,1024]{2,1,0:T(4,128)S(1)} %all_to_all.10.got, bf16[1024,1024]{1,0:T(8,128)(2,1)S(1)} %copy-done, bf16[1024,768]{1,0:T(8,128)(2,1)S(1)} %copy-done.3, bf16[2,768]{1,0:T(2,128)(2,1)S(1)} %copy-done.8, s32[2,16]{1,0:T(2,128)S(1)} %copy-done.9, f32[4]{0:T(128)S(1)} %copy-done.12), custom_call_target="tpu_custom_call" | custom-call | tf_op jit(solution)/shard_map/embed/pallas_call | solution.py:321
  59.1 15.8 %all_to_all.11.got = f32[8,4,896]{2,1,0:T(4,128)S(1)} all-to-all(f32[8,4,896]{2,1,0:T(4,128)S(1)} %embed.1), channel_id=1, replica_groups=mesh['batch'=8,'tm'=8,'space'=4] {'batch'}, dimensions={0} | all-to-all | bytes 229376 | tf_op jit(solution)/shard_map/all_to_all | solution.py:645
  74.9 2.7 %contrast.1 = (f32[2,768]{1,0:T(2,128)}, f32[1,1]{1,0:T(1,128)}, f32[2,1024]{1,0:T(2,128)S(1)}, f32[2,1024]{1,0:T(2,128)S(1)}) custom-call(s32[3]{0:T(128)S(1)} %pad_add_fusion.pos, f32[8,4,896]{2,1,0:T(4,128)S(1)} %all_to_all.11.got, bf16[1024,768]{1,0:T(8,128)(2,1)S(1)} %copy-done.3, bf16[1024,1024]{1,0:T(8,128)(2,1)S(1)} %copy-done), custom_call_target="tpu_custom_call" | custom-call | tf_op jit(solution)/shard_map/contrast/pallas_call | solution.py:418
  77.6 8.9 %backward.1 = (bf16[4,4,16,1024]{3,2,1,0:T(8,128)(2,1)S(1)}, bf16[2,3,16,1024]{3,2,1,0:T(8,128)(2,1)S(1)}, bf16[3,2,16,1024]{3,2,1,0:T(8,128)(2,1)S(1)}, bf16[2,...) custom-call(s32[2,3]{1,0:T(2,128)S(1)} %copy-done.7, ...), custom_call_target="tpu_custom_call" | custom-call | flops 3221225472 | bytes 16777216 | tf_op jit(solution)/shard_map/backward/pallas_call | solution.py:569
  86.5 3.1 %collective-permute-start.8 = (bf16[2,2,16,1024]{3,2,1,0:T(8,128)(2,1)S(1)}, bf16[2,2,16,1024]{3,2,1,0:T(8,128)(2,1)S(1)}, u32[]{:S(2)}, u32[]{:S(2)}) collective-permute-start(bf16[2,2,16,1024]{3,2,1,0:T(8,128)(2,1)S(1)} %get-tuple-element.53), channel_id=1, source_target_pairs={{0,5},{1,6},{2,7},{3,4},{4,9},{5,10},{6,11},{7,8},{8,13},{9,14},{1... | collective-permute-start | bytes 393224 | tf_op jit(solution)/shard_map/ppermute | solution.py:88
  89.7 1.6 %collective-permute-start.7 = (bf16[3,2,16,1024]{3,2,1,0:T(8,128)(2,1)S(1)}, bf16[3,2,16,1024]{3,2,1,0:T(8,128)(2,1)S(1)}, u32[]{:S(2)}, u32[]{:S(2)}) collective-permute-start(bf16[3,2,16,1024]{3,2,1,0:T(8,128)(2,1)S(1)} %get-tuple-element.52), channel_id=1, source_target_pairs={{0,1},{1,2},{2,3},{3,0},{4,5},{5,6},{6,7},{7,4},{8,9},{9,10},{10,1... | collective-permute-start | bytes 589832 | tf_op jit(solution)/shard_map/ppermute | solution.py:88
  91.2 2.0 %collective-permute-start.9 = (bf16[2,3,16,1024]{3,2,1,0:T(8,128)(2,1)S(1)}, bf16[2,3,16,1024]{3,2,1,0:T(8,128)(2,1)S(1)}, u32[]{:S(2)}, u32[]{:S(2)}) collective-permute-start(bf16[2,3,16,1024]{3,2,1,0:T(8,128)(2,1)S(1)} %get-tuple-element.54), channel_id=1, source_target_pairs={{0,28},{1,29},{2,30},{3,31},{4,0},{5,1},{6,2},{7,3},{8,4},{9,5},{1... | collective-permute-start | bytes 589832 | tf_op jit(solution)/shard_map/ppermute | solution.py:88
  93.2 0.8 collective-permute-start.10
  94.0 1.6 %collective-permute-start.11 = (bf16[2,2,16,1024]{3,2,1,0:T(8,128)(2,1)S(1)}, bf16[2,2,16,1024]{3,2,1,0:T(8,128)(2,1)S(1)}, u32[]{:S(2)}, u32[]{:S(2)}) collective-permute-start(bf16[2,2,16,1024]{3,2,1,0:T(8,128)(2,1)S(1)} %get-tuple-element.56), channel_id=1, source_target_pairs={{0,31},{1,28},{2,29},{3,30},{4,3},{5,0},{6,1},{7,2},{8,7},{9,4},{1... | collective-permute-start | bytes 393224 | tf_op jit(solution)/shard_map/ppermute | solution.py:88
  95.7 4.2 %collective-permute-done.11.refs_7_ = bf16[2,2,16,1024]{3,2,1,0:T(8,128)(2,1)S(1)} collective-permute-done((bf16[2,2,16,1024]{3,2,1,0:T(8,128)(2,1)S(1)}, bf16[2,2,16,1024]{3,2,1,0:T(8,128)(2,1)S(1)}, u32[]{:S(2)}, u32[]{:S(2)}) %collective-permute-start.11) | collective-permute-done | bytes 131104 | tf_op jit(solution)/shard_map/ppermute | solution.py:88
  100.0 4.2 %collective-permute-done.7.refs_3_ = bf16[3,2,16,1024]{3,2,1,0:T(8,128)(2,1)S(1)} collective-permute-done((bf16[3,2,16,1024]{3,2,1,0:T(8,128)(2,1)S(1)}, bf16[3,2,16,1024]{3,2,1,0:T(8,128)(2,1)S(1)}, u32[]{:S(2)}, u32[]{:S(2)}) %collective-permute-start.7) | collective-permute-done | bytes 196640 | tf_op jit(solution)/shard_map/ppermute | solution.py:88
  104.2 1.5 %collective-permute-done.9.refs_5_ = bf16[2,3,16,1024]{3,2,1,0:T(8,128)(2,1)S(1)} collective-permute-done((bf16[2,3,16,1024]{3,2,1,0:T(8,128)(2,1)S(1)}, bf16[2,3,16,1024]{3,2,1,0:T(8,128)(2,1)S(1)}, u32[]{:S(2)}, u32[]{:S(2)}) %collective-permute-start.9) | collective-permute-done | bytes 196640 | tf_op jit(solution)/shard_map/ppermute | solution.py:88
  105.7 0.8 collective-permute-done.10.refs_6_
  106.4 1.6 %merge.1 = bf16[2,4,4,16,1024]{4,3,2,1,0:T(8,128)(2,1)} custom-call(s32[2,3]{1,0:T(2,128)S(1)} %copy-done.7, bf16[4,4,16,1024]{3,2,1,0:T(8,128)(2,1)S(1)} %get-tuple-element.49.refs_0_, bf16[4,4,16,1024]{3,2,1,0:T(8,128)(2,1)S(1)} %get-tuple-element.50.refs_1_, bf16[2,3,16,1024]{3,2,1,0:T(8,128)(2,1)S(1)} %collective-permute-done.6.refs_2_, ...), custom_call_target="tpu_custom_call" | custom-call | tf_op jit(solution)/shard_map/merge/pallas_call | solution.py:622
  (40 shorter events, 1.3 us)
Async XLA Ops:
  0.6 1.2 %copy-start.4 = (bf16[2,4,4,16,1024]{4,3,2,1,0:T(8,128)(2,1)S(1)}, bf16[2,4,4,16,1024]{4,3,2,1,0:T(8,128)(2,1)}, u32[]{:S(2)}) copy-start(bf16[2,4,4,16,1024]{4,3,2,1,0:T(8,128)(2,1)} %video.3) | copy-start | bytes 3145732
  1.9 10.6 %collective-permute-start.2 = (bf16[2,2,16,1024]{3,2,1,0:T(8,128)(2,1)S(1)}, bf16[2,2,16,1024]{3,2,1,0:T(8,128)(2,1)S(1)}, u32[]{:S(2)}, u32[]{:S(2)}) collective-permute-start(bf16[2,2,16,1024]{3,2,1,0:T(8,128)(2,1)S(1)} %get-tuple-element.33), channel_id=1, source_target_pairs={{0,31},{1,28},{2,29},{3,30},{4,3},{5,0},{6,1},{7,2},{8,7},{9,4},{1... | collective-permute-start | bytes 393224 | tf_op jit(solution)/shard_map/ppermute | solution.py:88
  6.9 14.3 %collective-permute-start = (bf16[2,3,16,1024]{3,2,1,0:T(8,128)(2,1)S(1)}, bf16[2,3,16,1024]{3,2,1,0:T(8,128)(2,1)S(1)}, u32[]{:S(2)}, u32[]{:S(2)}) collective-permute-start(bf16[2,3,16,1024]{3,2,1,0:T(8,128)(2,1)S(1)} %get-tuple-element.31), channel_id=1, source_target_pairs={{0,28},{1,29},{2,30},{3,31},{4,0},{5,1},{6,2},{7,3},{8,4},{9,5},{1... | collective-permute-start | bytes 589832 | tf_op jit(solution)/shard_map/ppermute | solution.py:88
  7.1 14.2 %collective-permute-start.1 = (bf16[3,2,16,1024]{3,2,1,0:T(8,128)(2,1)S(1)}, bf16[3,2,16,1024]{3,2,1,0:T(8,128)(2,1)S(1)}, u32[]{:S(2)}, u32[]{:S(2)}) collective-permute-start(bf16[3,2,16,1024]{3,2,1,0:T(8,128)(2,1)S(1)} %get-tuple-element.32), channel_id=1, source_target_pairs={{0,3},{1,0},{2,1},{3,2},{4,7},{5,4},{6,5},{7,6},{8,11},{9,8},{10,9... | collective-permute-start | bytes 589832 | tf_op jit(solution)/shard_map/ppermute | solution.py:88
  8.3 12.9 %collective-permute-start.3 = (bf16[2,3,16,1024]{3,2,1,0:T(8,128)(2,1)S(1)}, bf16[2,3,16,1024]{3,2,1,0:T(8,128)(2,1)S(1)}, u32[]{:S(2)}, u32[]{:S(2)}) collective-permute-start(bf16[2,3,16,1024]{3,2,1,0:T(8,128)(2,1)S(1)} %get-tuple-element.34), channel_id=1, source_target_pairs={{0,4},{1,5},{2,6},{3,7},{4,8},{5,9},{6,10},{7,11},{8,12},{9,13},{1... | collective-permute-start | bytes 589832 | tf_op jit(solution)/shard_map/ppermute | solution.py:88
  9.9 11.6 %collective-permute-start.4 = (bf16[3,2,16,1024]{3,2,1,0:T(8,128)(2,1)S(1)}, bf16[3,2,16,1024]{3,2,1,0:T(8,128)(2,1)S(1)}, u32[]{:S(2)}, u32[]{:S(2)}) collective-permute-start(bf16[3,2,16,1024]{3,2,1,0:T(8,128)(2,1)S(1)} %get-tuple-element.35), channel_id=1, source_target_pairs={{0,1},{1,2},{2,3},{3,0},{4,5},{5,6},{6,7},{7,4},{8,9},{9,10},{10,1... | collective-permute-start | bytes 589832 | tf_op jit(solution)/shard_map/ppermute | solution.py:88
  12.5 0.6 copy-start.15
  13.1 7.4 %collective-permute-start.5 = (bf16[2,2,16,1024]{3,2,1,0:T(8,128)(2,1)S(1)}, bf16[2,2,16,1024]{3,2,1,0:T(8,128)(2,1)S(1)}, u32[]{:S(2)}, u32[]{:S(2)}) collective-permute-start(bf16[2,2,16,1024]{3,2,1,0:T(8,128)(2,1)S(1)} %get-tuple-element.36), channel_id=1, source_target_pairs={{0,5},{1,6},{2,7},{3,4},{4,9},{5,10},{6,11},{7,8},{8,13},{9,14},{1... | collective-permute-start | bytes 393224 | tf_op jit(solution)/shard_map/ppermute | solution.py:88
  13.5 44.3 %copy-start.9 = (s32[2,16]{1,0:T(2,128)S(1)}, s32[2,16]{1,0:T(2,128)}, u32[]{:S(2)}) copy-start(s32[2,16]{1,0:T(2,128)} %bucket.1) | copy-start | bytes 388
  13.5 44.3 %copy-start.8 = (bf16[2,768]{1,0:T(2,128)(2,1)S(1)}, bf16[2,768]{1,0:T(2,128)(2,1)}, u32[]{:S(2)}) copy-start(bf16[2,768]{1,0:T(2,128)(2,1)} %text.1) | copy-start | bytes 9220
  13.5 44.3 %copy-start.12 = (f32[4]{0:T(128)S(1)}, f32[4]{0:T(128)}, u32[]{:S(2)}) copy-start(f32[4]{0:T(128)} %levels.1) | copy-start | bytes 52
  20.6 0.6 copy-start.17
  21.5 0.7 copy-start.13
  22.2 2.8 %copy-start.1 = (bf16[1024,3072]{1,0:T(8,128)(2,1)S(1)}, bf16[1024,3072]{1,0:T(8,128)(2,1)}, u32[]{:S(2)}) copy-start(bf16[1024,3072]{1,0:T(8,128)(2,1)} %refs_9_.1) | copy-start | bytes 18874372
  25.0 1.2 %copy-start.5 = (bf16[2,4,4,16,1024]{4,3,2,1,0:T(8,128)(2,1)S(1)}, bf16[2,4,4,16,1024]{4,3,2,1,0:T(8,128)(2,1)}, u32[]{:S(2)}) copy-start(bf16[2,4,4,16,1024]{4,3,2,1,0:T(8,128)(2,1)} %video.3) | copy-start | bytes 3145732
  26.2 0.7 copy-start.6
  26.9 0.7 copy-start.10
  27.6 0.9 copy-start.14
  28.5 0.9 copy-start.16
  29.4 0.9 copy-start.18
  30.3 27.5 %copy-start = (bf16[1024,1024]{1,0:T(8,128)(2,1)S(1)}, bf16[1024,1024]{1,0:T(8,128)(2,1)}, u32[]{:S(2)}) copy-start(bf16[1024,1024]{1,0:T(8,128)(2,1)} %w_out.3) | copy-start | bytes 6291460
  37.9 19.9 %copy-start.3 = (bf16[1024,768]{1,0:T(8,128)(2,1)S(1)}, bf16[1024,768]{1,0:T(8,128)(2,1)}, u32[]{:S(2)}) copy-start(bf16[1024,768]{1,0:T(8,128)(2,1)} %w_emb.3) | copy-start | bytes 4718596
  57.8 19.8 %copy-start.2 = (bf16[1024,3072]{1,0:T(8,128)(2,1)S(1)}, bf16[1024,3072]{1,0:T(8,128)(2,1)}, u32[]{:S(2)}) copy-start(bf16[1024,3072]{1,0:T(8,128)(2,1)} %refs_9_.1) | copy-start | bytes 18874372
  59.1 18.5 %copy-start.7 = (s32[2,3]{1,0:T(2,128)S(1)}, s32[2,3]{1,0:T(2,128)}, u32[]{:S(2)}) copy-start(s32[2,3]{1,0:T(2,128)} %shifts.5) | copy-start | bytes 76
  59.1 18.5 %copy-start.11 = (f32[16]{0:T(128)S(1)}, f32[16]{0:T(128)}, u32[]{:S(2)}) copy-start(f32[16]{0:T(128)} %hscale.3) | copy-start | bytes 196
  86.5 7.5 %collective-permute-start.8 = (bf16[2,2,16,1024]{3,2,1,0:T(8,128)(2,1)S(1)}, bf16[2,2,16,1024]{3,2,1,0:T(8,128)(2,1)S(1)}, u32[]{:S(2)}, u32[]{:S(2)}) collective-permute-start(bf16[2,2,16,1024]{3,2,1,0:T(8,128)(2,1)S(1)} %get-tuple-element.53), channel_id=1, source_target_pairs={{0,5},{1,6},{2,7},{3,4},{4,9},{5,10},{6,11},{7,8},{8,13},{9,14},{1... | collective-permute-start | bytes 393224 | tf_op jit(solution)/shard_map/ppermute | solution.py:88
  89.7 10.3 %collective-permute-start.6 = (bf16[2,3,16,1024]{3,2,1,0:T(8,128)(2,1)S(1)}, bf16[2,3,16,1024]{3,2,1,0:T(8,128)(2,1)S(1)}, u32[]{:S(2)}, u32[]{:S(2)}) collective-permute-start(bf16[2,3,16,1024]{3,2,1,0:T(8,128)(2,1)S(1)} %get-tuple-element.51), channel_id=1, source_target_pairs={{0,4},{1,5},{2,6},{3,7},{4,8},{5,9},{6,10},{7,11},{8,12},{9,13},{1... | collective-permute-start | bytes 589832 | tf_op jit(solution)/shard_map/ppermute | solution.py:88
  89.7 14.5 %collective-permute-start.7 = (bf16[3,2,16,1024]{3,2,1,0:T(8,128)(2,1)S(1)}, bf16[3,2,16,1024]{3,2,1,0:T(8,128)(2,1)S(1)}, u32[]{:S(2)}, u32[]{:S(2)}) collective-permute-start(bf16[3,2,16,1024]{3,2,1,0:T(8,128)(2,1)S(1)} %get-tuple-element.52), channel_id=1, source_target_pairs={{0,1},{1,2},{2,3},{3,0},{4,5},{5,6},{6,7},{7,4},{8,9},{9,10},{10,1... | collective-permute-start | bytes 589832 | tf_op jit(solution)/shard_map/ppermute | solution.py:88
  91.2 14.4 %collective-permute-start.9 = (bf16[2,3,16,1024]{3,2,1,0:T(8,128)(2,1)S(1)}, bf16[2,3,16,1024]{3,2,1,0:T(8,128)(2,1)S(1)}, u32[]{:S(2)}, u32[]{:S(2)}) collective-permute-start(bf16[2,3,16,1024]{3,2,1,0:T(8,128)(2,1)S(1)} %get-tuple-element.54), channel_id=1, source_target_pairs={{0,28},{1,29},{2,30},{3,31},{4,0},{5,1},{6,2},{7,3},{8,4},{9,5},{1... | collective-permute-start | bytes 589832 | tf_op jit(solution)/shard_map/ppermute | solution.py:88
  93.2 13.2 %collective-permute-start.10 = (bf16[3,2,16,1024]{3,2,1,0:T(8,128)(2,1)S(1)}, bf16[3,2,16,1024]{3,2,1,0:T(8,128)(2,1)S(1)}, u32[]{:S(2)}, u32[]{:S(2)}) collective-permute-start(bf16[3,2,16,1024]{3,2,1,0:T(8,128)(2,1)S(1)} %get-tuple-element.55), channel_id=1, source_target_pairs={{0,3},{1,0},{2,1},{3,2},{4,7},{5,4},{6,5},{7,6},{8,11},{9,8},{10,9... | collective-permute-start | bytes 589832 | tf_op jit(solution)/shard_map/ppermute | solution.py:88
  94.0 5.8 %collective-permute-start.11 = (bf16[2,2,16,1024]{3,2,1,0:T(8,128)(2,1)S(1)}, bf16[2,2,16,1024]{3,2,1,0:T(8,128)(2,1)S(1)}, u32[]{:S(2)}, u32[]{:S(2)}) collective-permute-start(bf16[2,2,16,1024]{3,2,1,0:T(8,128)(2,1)S(1)} %get-tuple-element.56), channel_id=1, source_target_pairs={{0,31},{1,28},{2,29},{3,30},{4,3},{5,0},{6,1},{7,2},{8,7},{9,4},{1... | collective-permute-start | bytes 393224 | tf_op jit(solution)/shard_map/ppermute | solution.py:88

commit v3 on v2

--- a/solution.py
+++ b/solution.py
@@ -27,8 +27,9 @@
 LOG2E = 1.4426950408889634
 F32 = jnp.float32
 BF16 = jnp.bfloat16
-VMEM_LIMIT = 24 * 1024 * 1024
-
+MIB = 1024 * 1024
+
+NN = (((1,), (0,)), ((), ()))
 NT = (((1,), (1,)), ((), ()))
 TN = (((0,), (0,)), ((), ()))
 
@@ -53,8 +54,8 @@
     return pl.BlockSpec(memory_space=pltpu.SMEM)
 
 
-def params(**more):
-    return pltpu.CompilerParams(vmem_limit_bytes=VMEM_LIMIT, **more)
+def params(mib):
+    return pltpu.CompilerParams(vmem_limit_bytes=mib * MIB)
 
 
 def pack_kernel(video, *outs):
@@ -70,9 +71,42 @@
         out_shape=[jax.ShapeDtypeStruct(s, BF16) for s in PIECE_SHAPES * 2],
         in_specs=[vmem()],
         out_specs=[vmem()] * 6,
-        compiler_params=params(),
+        compiler_params=params(4),
         name="pack",
     )(video)
+
+
+def load_kernel(after, w_hbm, video_hbm, shifts, hscale, w_out, video_out, shifts_out, scale_out, sems):
+    copies = [
+        pltpu.make_async_copy(w_hbm, w_out, sems.at[0]),
+        pltpu.make_async_copy(video_hbm, video_out, sems.at[1]),
+    ]
+    for copy in copies:
+        copy.start()
+    for c in range(2):
+        for k in range(3):
+            shifts_out[c, k] = shifts[c, k]
+    for h in range(HEADS):
+        scale_out[h] = hscale[h]
+    for copy in copies:
+        copy.wait()
+
+
+def load(after, w_qkv, video, shifts, hscale):
+    return pl.pallas_call(
+        load_kernel,
+        out_shape=[
+            jax.ShapeDtypeStruct(x.shape, x.dtype) for x in (w_qkv, video, shifts, hscale)
+        ],
+        in_specs=[pl.BlockSpec(memory_space=pl.ANY)] * 3 + [smem()] * 2,
+        out_specs=[vmem()] * 2 + [smem()] * 2,
+        scratch_shapes=[pltpu.SemaphoreType.DMA((2,))],
+        compiler_params=params(4),
+        cost_estimate=pl.CostEstimate(
+            flops=0, bytes_accessed=2 * (w_qkv.size + video.size), transcendentals=0
+        ),
+        name="load",
+    )(after, w_qkv, video, shifts, hscale)
 
 
 def exchange(pieces, clip, sign):
@@ -121,12 +155,14 @@
     return jnp.where(label(key) == label(query), 1.0, 0.0)
 
 
-def forward_kernel(clips, frames, rows_all, pos, shifts, hscale, video, *refs):
+def forward_kernel(clips, frames, rows_all, shifts, hscale, video, *refs):
     nc = len(clips)
-    halo = refs[: 3 * nc]
-    w_qkv = refs[3 * nc]
-    ql, kl, vl, rq, rk, mass, prob, n32, istd, sums = refs[3 * nc + 1 : 3 * nc + 11]
-    ext, xb, masks, ones4, ones2, qs, ks = refs[3 * nc + 11 :]
+    frame0 = lax.axis_index("tm") * WT
+    row0 = lax.axis_index("space") * WH
+    halo, refs = refs[: 3 * nc], refs[3 * nc :]
+    w_qkv, refs = refs[0], refs[1:]
+    ql, kl, vl, rq, rk, mass, prob, n32, istd, sums = refs[:10]
+    ext, xb, masks, ones4, ones2, qs, ks = refs[10:]
     ones4[...] = head_blocks((QW, QW), HEAD_DIM)
     ones2[...] = head_blocks((2 * TOK, 2 * HEAD_DIM), TOK)
     for n, c in enumerate(clips):
@@ -161,7 +197,7 @@
         sums[2 * n : 2 * n + 1] = jnp.sum(total, axis=0, keepdims=True)
         for w in range(2):
             masks[2 * n + w] = window_mask(
-                pos[0] * WT, pos[1] * WH, w * WW, s0, s1, s2, frames, rows_all
+                frame0, row0, w * WW, s0, s1, s2, frames, rows_all
             )
     xb[...] = n32[...].astype(BF16)
     lane = lax.broadcasted_iota(jnp.int32, (1, 2 * TOK), 1)
@@ -258,7 +294,8 @@
         item[3]()
 
 
-def forward(clips, pos, shifts, hscale, video, halo, w_qkv):
+def forward(shifts, hscale, video, halo, w_qkv):
+    clips = (0, 1)
     nc = len(clips)
     n = nc * 2 * TOK
     frames = lax.axis_size("tm") * WT
@@ -273,7 +310,7 @@
             jax.ShapeDtypeStruct((n, 128), F32),
             jax.ShapeDtypeStruct((2 * nc, D), F32),
         ],
-        in_specs=[smem(), smem(), smem()] + [vmem()] * (2 + 3 * nc),
+        in_specs=[smem(), smem()] + [vmem()] * (2 + 3 * nc),
         out_specs=[vmem()] * 10,
         scratch_shapes=[
             pltpu.VMEM((nc, GRID, GRID, COLS, D), BF16),
@@ -284,20 +321,38 @@
             pltpu.VMEM((n, QW), F32),
             pltpu.VMEM((n, QW), F32),
         ],
-        compiler_params=params(),
+        compiler_params=params(12),
         cost_estimate=pl.CostEstimate(
             flops=2 * n * D * 3 * D, bytes_accessed=12 * 2**20, transcendentals=n * 2048
         ),
         name="forward",
-    )(pos, shifts, hscale, video, *halo, w_qkv)
-
-
-def embed_kernel(tokens, got, w_out, w_emb, text, bucket, levels, out):
-    total = jnp.sum(got[...], axis=0)
-    mean = (jnp.concatenate([total[1:2], total[3:4]], axis=0) / tokens).astype(BF16)
-    token_mean = jnp.concatenate([total[0:1], total[2:3]], axis=0) / tokens
-    pooled = token_mean + jnp.dot(mean, w_out[...], preferred_element_type=F32)
-    embedded = jnp.dot(pooled.astype(BF16), w_emb[...], preferred_element_type=F32)
+    )(shifts, hscale, video, *halo, w_qkv)
+
+
+def share_kernel(tokens, sums, w_out, w_emb, out):
+    means = sums[...] / tokens
+    pooled = jnp.concatenate([means[0:1], means[2:3]], axis=0) + full_dot(
+        jnp.concatenate([means[1:2], means[3:4]], axis=0), w_out[...], NN
+    )
+    block = full_dot(pooled, w_emb[...], NN)
+    for peer in range(out.shape[0]):
+        out[peer] = block
+
+
+def share(sums, w_out, w_emb, tokens):
+    plane = lax.axis_size("tm") * lax.axis_size("space")
+    return pl.pallas_call(
+        partial(share_kernel, tokens),
+        out_shape=jax.ShapeDtypeStruct((plane, 2, EMB), F32),
+        in_specs=[vmem()] * 3,
+        out_specs=vmem(),
+        compiler_params=params(4),
+        name="share",
+    )(sums, w_out, w_emb)
+
+
+def embed_kernel(got, text, bucket, levels, out):
+    embedded = jnp.sum(got[...], axis=0)
     held = bucket[...]
     weight = jnp.zeros(held.shape, F32)
     for level in range(levels.shape[0]):
@@ -317,15 +372,15 @@
         out[peer] = block
 
 
-def embed(got, w_out, w_emb, text, bucket, levels, tokens, peers):
+def embed(got, text, bucket, levels, peers):
     return pl.pallas_call(
-        partial(embed_kernel, tokens),
+        embed_kernel,
         out_shape=jax.ShapeDtypeStruct((peers, 4, EMB + 128), F32),
-        in_specs=[vmem()] * 5 + [smem()],
+        in_specs=[vmem()] * 3 + [smem()],
         out_specs=vmem(),
-        compiler_params=params(),
+        compiler_params=params(4),
         name="embed",
-    )(got, w_out, w_emb, text, bucket, levels)
+    )(got, text, bucket, levels)
 
 
 def three_parts(wide):
@@ -336,15 +391,16 @@
     return jnp.concatenate([high, middle, low], axis=0)
 
 
-def full_dot(wide, weight):
+def full_dot(wide, weight, dims):
     n = wide.shape[0]
-    got = lax.dot_general(three_parts(wide), weight, NT, preferred_element_type=F32)
+    got = lax.dot_general(three_parts(wide), weight, dims, preferred_element_type=F32)
     return got[:n] + got[n : 2 * n] + got[2 * n :]
 
 
-def contrast_kernel(pos, got, w_emb, w_out, text_grad, loss, clip_grad, d_out):
+def contrast_kernel(got, w_emb, w_out, text_grad, loss, clip_grad, d_out):
     peers = got.shape[0]
     n = 2 * peers
+    first_clip = 2 * lax.axis_index("batch")
     embedded = jnp.concatenate([got[p, 0:2, :EMB] for p in range(peers)], axis=0)
     weights = jnp.concatenate([got[p, 0:2, EMB:] for p in range(peers)], axis=0)[:, :n]
     words = jnp.concatenate([got[p, 2:4, :EMB] for p in range(peers)], axis=0)
@@ -401,7 +457,7 @@
         return jnp.concatenate(
             [
                 jnp.sum(
-                    jnp.where(row == 2 * pos[2] + c, array, 0.0), axis=0, keepdims=True
+                    jnp.where(row == first_clip + c, array, 0.0), axis=0, keepdims=True
                 )
                 for c in range(2)
             ],
@@ -409,12 +465,12 @@
         )
 
     text_grad[...] = mine(text_all)
-    pooled_grad = full_dot(mine(embed_all), w_emb[...])
+    pooled_grad = full_dot(mine(embed_all), w_emb[...], NT)
     clip_grad[...] = pooled_grad
-    d_out[...] = full_dot(pooled_grad, w_out[...])
-
-
-def contrast(pos, got, w_emb, w_out):
+    d_out[...] = full_dot(pooled_grad, w_out[...], NT)
+
+
+def contrast(got, w_emb, w_out):
     return pl.pallas_call(
         contrast_kernel,
         out_shape=[
@@ -423,16 +479,20 @@
             jax.ShapeDtypeStruct((2, D), F32),
             jax.ShapeDtypeStruct((2, D), F32),
         ],
-        in_specs=[smem(), vmem(), vmem(), vmem()],
+        in_specs=[vmem()] * 3,
         out_specs=[vmem()] * 4,
-        compiler_params=params(),
+        compiler_params=params(4),
         name="contrast",
-    )(pos, got, w_emb, w_out)
+    )(got, w_emb, w_out)
 
 
 def backward_kernel(clips, shifts, hscale, clip_grad, d_out, *refs):
     nc = len(clips)
-    ql, kl, vl, rq, rk, mass, prob, n32, istd, w_qkv = refs[:10]
+    mine = pl.ds(clips[0] * 2 * TOK, nc * 2 * TOK)
+    ql, kl, vl, rq, rk, mass = (ref.at[mine] for ref in refs[:6])
+    prob = refs[6].at[:, pl.ds(clips[0] * 4, nc * 4)]
+    n32, istd = (ref.at[mine] for ref in refs[7:9])
+    w_qkv = refs[9]
     outs = refs[10 : 10 + 4 * nc]
     ext, total, ones4, dqs, dks, dqb, dkb, dvb = refs[10 + 4 * nc :]
     rows = nc * 2 * TOK
@@ -581,7 +641,7 @@
             pltpu.VMEM((n, D), BF16),
             pltpu.VMEM((n, D), BF16),
         ],
-        compiler_params=params(),
+        compiler_params=params(14),
         cost_estimate=pl.CostEstimate(
             flops=2 * n * D * 3 * D, bytes_accessed=16 * 2**20, transcendentals=0
         ),
@@ -589,64 +649,63 @@
     )(shifts, hscale, clip_grad, d_out, *stored, w_qkv)
 
 
-def merge_kernel(shifts, *refs):
-    own, got, out = refs[:2], refs[2:8], refs[8]
-    for c in range(2):
-        s0, s1 = shifts[c, 0], shifts[c, 1]
-        a, b, corner = got[3 * c : 3 * c + 3]
-        for f in range(WT):
-            for r in range(WH):
-                if c == 0:
-                    far_f, far_r = f < HALO, r < HALO
-                    gone_f, gone_r = f < s0, r < s1
-                    at_a, at_b, at_c = (f, r - 1), (f - 1, r), (f, r)
-                else:
-                    far_f, far_r = f >= WT - HALO, r >= WH - HALO
-                    gone_f, gone_r = f >= WT + s0, r >= WH + s1
-                    at_a, at_b, at_c = (f - 2, r), (f, r - 2), (f - 2, r - 2)
-                value = own[c][f, r]
-                in_a = far_f and 0 <= at_a[1] < 3
-                in_b = far_r and 0 <= at_b[0] < 3
-                if in_a:
-                    take = jnp.logical_and(gone_f, jnp.logical_not(gone_r))
-                    value = jnp.where(take, a[at_a], value)
-                if in_b:
-                    take = jnp.logical_and(jnp.logical_not(gone_f), gone_r)
-                    value = jnp.where(take, b[at_b], value)
-                if far_f and far_r:
-                    value = jnp.where(jnp.logical_and(gone_f, gone_r), corner[at_c], value)
-                out[c, f, r] = value
-
-
-def merge(shifts, own, got):
+def merge_kernel(c, shifts, own, a, b, corner, *refs):
+    out = refs[-1]
+    s0, s1 = shifts[c, 0], shifts[c, 1]
+    for f in range(WT):
+        for r in range(WH):
+            if c == 0:
+                far_f, far_r = f < HALO, r < HALO
+                gone_f, gone_r = f < s0, r < s1
+                at_a, at_b, at_c = (f, r - 1), (f - 1, r), (f, r)
+            else:
+                far_f, far_r = f >= WT - HALO, r >= WH - HALO
+                gone_f, gone_r = f >= WT + s0, r >= WH + s1
+                at_a, at_b, at_c = (f - 2, r), (f, r - 2), (f - 2, r - 2)
+            value = own[f, r]
+            if far_f and 0 <= at_a[1] < 3:
+                take = jnp.logical_and(gone_f, jnp.logical_not(gone_r))
+                value = jnp.where(take, a[at_a], value)
+            if far_r and 0 <= at_b[0] < 3:
+                take = jnp.logical_and(jnp.logical_not(gone_f), gone_r)
+                value = jnp.where(take, b[at_b], value)
+            if far_f and far_r:
+                value = jnp.where(jnp.logical_and(gone_f, gone_r), corner[at_c], value)
+            out[0, f, r] = value
+
+
+def merge(clip, shifts, own, got, other=None):
+    rest = [] if other is None else [other]
     return pl.pallas_call(
-        merge_kernel,
+        partial(merge_kernel, clip),
+        grid=(1,),
         out_shape=jax.ShapeDtypeStruct((2, WT, WH, COLS, D), BF16),
-        in_specs=[smem()] + [vmem()] * 8,
-        out_specs=vmem(),
-        compiler_params=params(),
+        in_specs=[smem()] + [vmem()] * 4 + [pl.BlockSpec(memory_space=pl.ANY)] * len(rest),
+        out_specs=pl.BlockSpec((1, WT, WH, COLS, D), lambda i: (clip, 0, 0, 0, 0)),
+        input_output_aliases={5: 0} if rest else {},
+        compiler_params=params(4),
         name="merge",
-    )(shifts, *own, *got)
+    )(shifts, own, *got, *rest)
 
 
 def local(video, shifts, head_scale, w_qkv, w_out, w_emb, text, bucket, bucket_scale):
     tokens = lax.axis_size("tm") * lax.axis_size("space") * WT * WH * COLS
-    plane = lax.axis_size("tm") * lax.axis_size("space")
     peers = lax.axis_size("batch")
-    pos = jnp.stack(
-        [lax.axis_index("tm"), lax.axis_index("space"), lax.axis_index("batch")]
-    ).astype(jnp.int32)
     pieces = pack(video)
     halo = exchange(pieces[:3], 0, -1) + exchange(pieces[3:], 1, -1)
-    *stored, sums = forward((0, 1), pos, shifts, head_scale, video, halo, w_qkv)
-    spread = jnp.broadcast_to(sums[None], (plane,) + sums.shape)
+    w_qkv, video, shifts, head_scale = load(halo[2], w_qkv, video, shifts, head_scale)
+    *stored, sums = forward(shifts, head_scale, video, halo, w_qkv)
+    spread = share(sums, w_out, w_emb, tokens)
     got = lax.all_to_all(spread, ("tm", "space"), 0, 0)
-    packed = embed(got, w_out, w_emb, text, bucket, bucket_scale, tokens, peers)
+    packed = embed(got, text, bucket, bucket_scale, peers)
     got = lax.all_to_all(packed, "batch", 0, 0)
-    text_grad, loss, clip_grad, d_out = contrast(pos, got, w_emb, w_out)
-    outs = backward((0, 1), shifts, head_scale, clip_grad, d_out, stored, w_qkv)
-    back = exchange(outs[1:4], 0, 1) + exchange(outs[5:8], 1, 1)
-    video_grad = merge(shifts, (outs[0], outs[4]), back)
+    text_grad, loss, clip_grad, d_out = contrast(got, w_emb, w_out)
+    parts = []
+    for c in range(2):
+        mine, *pieces = backward((c,), shifts, head_scale, clip_grad, d_out, stored, w_qkv)
+        parts.append((mine, exchange(pieces, c, 1)))
+    video_grad = merge(0, shifts, *parts[0])
+    video_grad = merge(1, shifts, *parts[1], video_grad)
     return (video_grad, text_grad, loss[0, 0])
 
 

time: 108 us -> 92.7 us (0.86)
  waiting for transfers between devices: 18.1 us -> 8.68 us
  local copies, waits for them, and re-layouts: 11.4 us -> 5.36 us
  blocking collectives: 35.5 us -> 31.3 us
  Pallas kernels: 22.2 us -> 26 us
    ppermute x12, waiting for transfers between devices: 18.1 us -> 8.68 us  [exchange(): out.append(lax.ppermute(piece, ('tm', 'space'), pairs))]
    unnamed x38 -> x18, local copies, waits for them, and re-layouts: 11.3 us -> 5.36 us
    all_to_all x1, blocking collectives: 19.7 us -> 15.7 us  [local(): got = lax.all_to_all(spread, ('tm', 'space'), 0, 0)]
    pallas_call x2 -> x5, Pallas kernels: 2.91 us -> 5.87 us  [the longest x2 2.79 us: merge(): pl.pallas_call(partial(merge_kernel, clip), grid=(1,), out_shape=jax.Shap...]
    pallas_call x1 -> x2, Pallas kernels: 8.88 us -> 10.2 us  [backward(): pl.pallas_call(partial(backward_kernel, clips), out_shape=[jax.ShapeDtype...]
  transfers between devices with their start and end apart: 12 -> 12, of which waited for: 7 -> 4; matrix products, arithmetic and copies ran while one was open for 0% -> 0% of each run, Pallas kernels for 0% -> 9%
where the time goes in v3:
time: 92.7 us; the launch traced here: 92.5 us
  blocking collectives  31.3 us (34%)
  Pallas kernels  26 us (28%)
  starting transfers between devices  20.3 us (22%)
  waiting for transfers between devices  8.68 us (9%)
  local copies, waits for them, and re-layouts  5.36 us (6%)
    ppermute x12, starting transfers between devices, exchange(): out.append(lax.ppermute(piece, ('tm', 'space'), pairs))  20.3 us
    all_to_all x1, blocking collectives, local(): got = lax.all_to_all(spread, ('tm', 'space'), 0, 0)  15.7 us
    all_to_all x1, blocking collectives, local(): got = lax.all_to_all(packed, 'batch', 0, 0)  15.6 us
    pallas_call x2, Pallas kernels, backward(): pl.pallas_call(partial(backward_kernel, clips), out_shape=[jax.ShapeDtype...  10.2 us
    ppermute x12, waiting for transfers between devices, exchange(): out.append(lax.ppermute(piece, ('tm', 'space'), pairs))  8.68 us
    pallas_call x1, Pallas kernels, forward(): pl.pallas_call(partial(forward_kernel, clips, frames, rows_all), out_shap...  7.62 us
    unnamed x18, local copies, waits for them, and re-layouts  5.36 us
    pallas_call x2, Pallas kernels, merge(): pl.pallas_call(partial(merge_kernel, clip), grid=(1,), out_shape=jax.Shap...  2.79 us
  transfers between devices with their start and end apart: 12, of which 4 were waited for; matrix products, arithmetic and copies ran while one was open for 0% of the time, Pallas kernels for 9%

profile of v3, /device:TPU:1, one launch (start us, length us, event | category | flops | bytes accessed | tf_op | source)
XLA Modules:
  0.0 92.5 jit_solution(15087533360031424156)
XLA Ops:
  0.6 1.2 %copy-done.3 = bf16[2,4,4,16,1024]{4,3,2,1,0:T(8,128)(2,1)S(1)} copy-done((bf16[2,4,4,16,1024]{4,3,2,1,0:T(8,128)(2,1)S(1)}, bf16[2,4,4,16,1024]{4,3,2,1,0:T(8,128)(2,1)}, u32[]{:S(2)}) %copy-start.3) | copy-done | bytes 1048600
  1.9 0.1 pack.1
  1.9 5.0 %collective-permute-start = (bf16[2,2,16,1024]{3,2,1,0:T(8,128)(2,1)S(1)}, bf16[2,2,16,1024]{3,2,1,0:T(8,128)(2,1)S(1)}, u32[]{:S(2)}, u32[]{:S(2)}) collective-permute-start(bf16[2,2,16,1024]{3,2,1,0:T(8,128)(2,1)S(1)} %get-tuple-element.35), channel_id=1, source_target_pairs={{0,31},{1,28},{2,29},{3,30},{4,3},{5,0},{6,1},{7,2},{8,7},{9,4},{1... | collective-permute-start | bytes 393224 | tf_op jit(solution)/shard_map/ppermute | solution.py:122
  6.9 0.2 collective-permute-start.1
  7.1 1.2 %collective-permute-start.2 = (bf16[3,2,16,1024]{3,2,1,0:T(8,128)(2,1)S(1)}, bf16[3,2,16,1024]{3,2,1,0:T(8,128)(2,1)S(1)}, u32[]{:S(2)}, u32[]{:S(2)}) collective-permute-start(bf16[3,2,16,1024]{3,2,1,0:T(8,128)(2,1)S(1)} %get-tuple-element.40), channel_id=1, source_target_pairs={{0,3},{1,0},{2,1},{3,2},{4,7},{5,4},{6,5},{7,6},{8,11},{9,8},{10,9... | collective-permute-start | bytes 589832 | tf_op jit(solution)/shard_map/ppermute | solution.py:122
  8.3 1.6 %collective-permute-start.3 = (bf16[2,3,16,1024]{3,2,1,0:T(8,128)(2,1)S(1)}, bf16[2,3,16,1024]{3,2,1,0:T(8,128)(2,1)S(1)}, u32[]{:S(2)}, u32[]{:S(2)}) collective-permute-start(bf16[2,3,16,1024]{3,2,1,0:T(8,128)(2,1)S(1)} %get-tuple-element.41), channel_id=1, source_target_pairs={{0,4},{1,5},{2,6},{3,7},{4,8},{5,9},{6,10},{7,11},{8,12},{9,13},{1... | collective-permute-start | bytes 589832 | tf_op jit(solution)/shard_map/ppermute | solution.py:122
  9.9 2.6 %collective-permute-start.4 = (bf16[3,2,16,1024]{3,2,1,0:T(8,128)(2,1)S(1)}, bf16[3,2,16,1024]{3,2,1,0:T(8,128)(2,1)S(1)}, u32[]{:S(2)}, u32[]{:S(2)}) collective-permute-start(bf16[3,2,16,1024]{3,2,1,0:T(8,128)(2,1)S(1)} %get-tuple-element.42), channel_id=1, source_target_pairs={{0,1},{1,2},{2,3},{3,0},{4,5},{5,6},{6,7},{7,4},{8,9},{9,10},{10,1... | collective-permute-start | bytes 589832 | tf_op jit(solution)/shard_map/ppermute | solution.py:122
  12.5 0.3 collective-permute-start.5
  12.8 2.8 %copy-done.1 = bf16[1024,3072]{1,0:T(8,128)(2,1)S(1)} copy-done((bf16[1024,3072]{1,0:T(8,128)(2,1)S(1)}, bf16[1024,3072]{1,0:T(8,128)(2,1)}, u32[]{:S(2)}) %copy-start.1) | copy-done | bytes 6291480
  15.6 0.7 copy-done.5
  16.3 0.7 copy-done.7
  16.9 1.7 %load.1 = (bf16[1024,3072]{1,0:T(8,128)(2,1)S(1)}, bf16[2,4,4,16,1024]{4,3,2,1,0:T(8,128)(2,1)S(1)}, s32[2,3]{1,0:T(2,128)S(1)}, f32[16]{0:T(128)S(1)}) custom-call(bf16[2,2,16,1024]{3,2,1,0:T(8,128)(2,1)S(1)} %collective-permute-done.after.refs_2_, bf16[1024,3072]{1,0:T(8,128)(2,1)S(1)} %copy-done.1, bf16[2,4,4,16,1024]{4,3,2,1,0:T(8,128)(2,1)S(1)} %copy-done.3, ...), custom_call_target="tpu_custom_call" | custom-call | bytes 7340032 | tf_op jit(solution)/shard_map/load/pallas_call | solution.py:96
  18.6 1.8 %collective-permute-done.5.refs_5_ = bf16[2,2,16,1024]{3,2,1,0:T(8,128)(2,1)S(1)} collective-permute-done((bf16[2,2,16,1024]{3,2,1,0:T(8,128)(2,1)S(1)}, bf16[2,2,16,1024]{3,2,1,0:T(8,128)(2,1)S(1)}, u32[]{:S(2)}, u32[]{:S(2)}) %collective-permute-start.5) | collective-permute-done | bytes 131104 | tf_op jit(solution)/shard_map/ppermute | solution.py:122
  20.5 1.1 %collective-permute-done.4.refs_4_ = bf16[3,2,16,1024]{3,2,1,0:T(8,128)(2,1)S(1)} collective-permute-done((bf16[3,2,16,1024]{3,2,1,0:T(8,128)(2,1)S(1)}, bf16[3,2,16,1024]{3,2,1,0:T(8,128)(2,1)S(1)}, u32[]{:S(2)}, u32[]{:S(2)}) %collective-permute-start.4) | collective-permute-done | bytes 196640 | tf_op jit(solution)/shard_map/ppermute | solution.py:122
  21.5 7.6 %forward.1 = (bf16[512,1024]{1,0:T(8,128)(2,1)S(1)}, bf16[512,1024]{1,0:T(8,128)(2,1)S(1)}, bf16[512,1024]{1,0:T(8,128)(2,1)S(1)}, f32[512,1024]{1,0:T(8,128)S(1...) custom-call(s32[2,3]{1,0:T(2,128)S(1)} %get-tuple-element.36.shifts,, ...), custom_call_target="tpu_custom_call" | custom-call | flops 3221225472 | bytes 12582912 | tf_op jit(solution)/shard_map/forward/pallas_call | solution.py:303
  29.2 0.0 copy-start.4
  29.2 0.7 share.1
  30.0 15.7 %all_to_all.10.got = f32[32,2,768]{2,1,0:T(2,128)S(1)} all-to-all(f32[32,2,768]{2,1,0:T(2,128)S(1)} %share.1), channel_id=1, replica_groups=mesh['batch'=8,'tm'=8,'space'=4] {'tm','space'}, dimensions={0} | all-to-all | bytes 393216 | tf_op jit(solution)/shard_map/all_to_all | solution.py:699
  45.7 0.6 embed.1
  46.4 15.6 %all_to_all.11.got = f32[8,4,896]{2,1,0:T(4,128)S(1)} all-to-all(f32[8,4,896]{2,1,0:T(4,128)S(1)} %embed.1), channel_id=1, replica_groups=mesh['batch'=8,'tm'=8,'space'=4] {'batch'}, dimensions={0} | all-to-all | bytes 229376 | tf_op jit(solution)/shard_map/all_to_all | solution.py:701
  62.0 2.2 %contrast.1 = (f32[2,768]{1,0:T(2,128)}, f32[1,1]{1,0:T(1,128)}, f32[2,1024]{1,0:T(2,128)S(1)}, f32[2,1024]{1,0:T(2,128)S(1)}) custom-call(f32[8,4,896]{2,1,0:T(4,128)S(1)} %all_to_all.11.got, bf16[1024,768]{1,0:T(8,128)(2,1)S(1)} %copy-done.2, bf16[1024,1024]{1,0:T(8,128)(2,1)S(1)} %copy-done), custom_call_target="tpu_custom_call" | custom-call | tf_op jit(solution)/shard_map/contrast/pallas_call | solution.py:474
  64.2 5.1 %backward.3 = (bf16[4,4,16,1024]{3,2,1,0:T(8,128)(2,1)S(1)}, bf16[2,3,16,1024]{3,2,1,0:T(8,128)(2,1)S(1)}, bf16[3,2,16,1024]{3,2,1,0:T(8,128)(2,1)S(1)}, bf16[2,2,16,1024]{3,2,1,0:T(8,128)(2,1)S(1)}) custom-call(s32[2,3]{1,0:T(2,128)S(1)} %get-tuple-element.36.shifts, f32[16]{0:T(128)S(1)} %get-tuple-element.37.hscale, ...), custom_call_target="tpu_custom_call" | custom-call | flops 1610612736 | bytes 16777216 | tf_op jit(solution)/shard_map/backward/pallas_call | solution.py:629
  69.3 3.3 %collective-permute-start.11 = (bf16[2,2,16,1024]{3,2,1,0:T(8,128)(2,1)S(1)}, bf16[2,2,16,1024]{3,2,1,0:T(8,128)(2,1)S(1)}, u32[]{:S(2)}, u32[]{:S(2)}) collective-permute-start(bf16[2,2,16,1024]{3,2,1,0:T(8,128)(2,1)S(1)} %get-tuple-element.64), channel_id=1, source_target_pairs={{0,5},{1,6},{2,7},{3,4},{4,9},{5,10},{6,11},{7,8},{8,13},{9,14},{1... | collective-permute-start | bytes 393224 | tf_op jit(solution)/shard_map/ppermute | solution.py:122
  72.6 1.6 %collective-permute-start.10 = (bf16[3,2,16,1024]{3,2,1,0:T(8,128)(2,1)S(1)}, bf16[3,2,16,1024]{3,2,1,0:T(8,128)(2,1)S(1)}, u32[]{:S(2)}, u32[]{:S(2)}) collective-permute-start(bf16[3,2,16,1024]{3,2,1,0:T(8,128)(2,1)S(1)} %get-tuple-element.63), channel_id=1, source_target_pairs={{0,1},{1,2},{2,3},{3,0},{4,5},{5,6},{6,7},{7,4},{8,9},{9,10},{10,1... | collective-permute-start | bytes 589832 | tf_op jit(solution)/shard_map/ppermute | solution.py:122
  74.2 5.1 %backward.2 = (bf16[4,4,16,1024]{3,2,1,0:T(8,128)(2,1)S(1)}, bf16[2,3,16,1024]{3,2,1,0:T(8,128)(2,1)S(1)}, bf16[3,2,16,1024]{3,2,1,0:T(8,128)(2,1)S(1)}, bf16[2,2,16,1024]{3,2,1,0:T(8,128)(2,1)S(1)}) custom-call(s32[2,3]{1,0:T(2,128)S(1)} %get-tuple-element.36.shifts, f32[16]{0:T(128)S(1)} %get-tuple-element.37.hscale, ...), custom_call_target="tpu_custom_call" | custom-call | flops 1610612736 | bytes 16777216 | tf_op jit(solution)/shard_map/backward/pallas_call | solution.py:629
  79.3 2.1 %collective-permute-start.6 = (bf16[2,3,16,1024]{3,2,1,0:T(8,128)(2,1)S(1)}, bf16[2,3,16,1024]{3,2,1,0:T(8,128)(2,1)S(1)}, u32[]{:S(2)}, u32[]{:S(2)}) collective-permute-start(bf16[2,3,16,1024]{3,2,1,0:T(8,128)(2,1)S(1)} %get-tuple-element.58), channel_id=1, source_target_pairs={{0,28},{1,29},{2,30},{3,31},{4,0},{5,1},{6,2},{7,3},{8,4},{9,5},{1... | collective-permute-start | bytes 589832 | tf_op jit(solution)/shard_map/ppermute | solution.py:122
  81.4 0.8 collective-permute-start.7
  82.2 1.7 %collective-permute-start.8 = (bf16[2,2,16,1024]{3,2,1,0:T(8,128)(2,1)S(1)}, bf16[2,2,16,1024]{3,2,1,0:T(8,128)(2,1)S(1)}, u32[]{:S(2)}, u32[]{:S(2)}) collective-permute-start(bf16[2,2,16,1024]{3,2,1,0:T(8,128)(2,1)S(1)} %get-tuple-element.60), channel_id=1, source_target_pairs={{0,31},{1,28},{2,29},{3,30},{4,3},{5,0},{6,1},{7,2},{8,7},{9,4},{1... | collective-permute-start | bytes 393224 | tf_op jit(solution)/shard_map/ppermute | solution.py:122
  83.9 1.4 %merge.2.refs_0_ = bf16[2,4,4,16,1024]{4,3,2,1,0:T(8,128)(2,1)} custom-call(s32[2,3]{1,0:T(2,128)S(1)} %get-tuple-element.36.shifts, bf16[4,4,16,1024]{3,2,1,0:T(8,128)(2,1)S(1)} %get-tuple-element.61.own, bf16[2,3,16,1024]{3,2,1,0:T(8,128)(2,1)S(1)} %collective-permute-done.9.a, bf16[3,2,16,1024]{3,2,1,0:T(8,128)(2,1)S(1)} %collective-permute-done.10.b, ...), custom_call_target="tpu_custom_call" | custom-call | tf_op jit(solution)/shard_map/merge/pallas_call | solution.py:679
  85.3 3.1 %collective-permute-done.8.corner = bf16[2,2,16,1024]{3,2,1,0:T(8,128)(2,1)S(1)} collective-permute-done((bf16[2,2,16,1024]{3,2,1,0:T(8,128)(2,1)S(1)}, bf16[2,2,16,1024]{3,2,1,0:T(8,128)(2,1)S(1)}, u32[]{:S(2)}, u32[]{:S(2)}) %collective-permute-start.8) | collective-permute-done | bytes 131104 | tf_op jit(solution)/shard_map/ppermute | solution.py:122
  88.4 2.6 %collective-permute-done.7.b = bf16[3,2,16,1024]{3,2,1,0:T(8,128)(2,1)S(1)} collective-permute-done((bf16[3,2,16,1024]{3,2,1,0:T(8,128)(2,1)S(1)}, bf16[3,2,16,1024]{3,2,1,0:T(8,128)(2,1)S(1)}, u32[]{:S(2)}, u32[]{:S(2)}) %collective-permute-start.7) | collective-permute-done | bytes 196640 | tf_op jit(solution)/shard_map/ppermute | solution.py:122
  91.1 1.4 %merge.3 = bf16[2,4,4,16,1024]{4,3,2,1,0:T(8,128)(2,1)} custom-call(s32[2,3]{1,0:T(2,128)S(1)} %get-tuple-element.36.shifts, bf16[4,4,16,1024]{3,2,1,0:T(8,128)(2,1)S(1)} %get-tuple-element.57.own, bf16[2,3,16,1024]{3,2,1,0:T(8,128)(2,1)S(1)} %collective-permute-done.6.a, ...), custom_call_target="tpu_custom_call", output_to_operand_aliasing={{}: (5, {})} | custom-call | tf_op jit(solution)/shard_map/merge/pallas_call | solution.py:679
  (22 shorter events, 0.1 us)
Async XLA Ops:
  0.6 1.2 %copy-start.3 = (bf16[2,4,4,16,1024]{4,3,2,1,0:T(8,128)(2,1)S(1)}, bf16[2,4,4,16,1024]{4,3,2,1,0:T(8,128)(2,1)}, u32[]{:S(2)}) copy-start(bf16[2,4,4,16,1024]{4,3,2,1,0:T(8,128)(2,1)} %video_hbm.1) | copy-start | bytes 3145732
  1.9 10.6 %collective-permute-start = (bf16[2,2,16,1024]{3,2,1,0:T(8,128)(2,1)S(1)}, bf16[2,2,16,1024]{3,2,1,0:T(8,128)(2,1)S(1)}, u32[]{:S(2)}, u32[]{:S(2)}) collective-permute-start(bf16[2,2,16,1024]{3,2,1,0:T(8,128)(2,1)S(1)} %get-tuple-element.35), channel_id=1, source_target_pairs={{0,31},{1,28},{2,29},{3,30},{4,3},{5,0},{6,1},{7,2},{8,7},{9,4},{1... | collective-permute-start | bytes 393224 | tf_op jit(solution)/shard_map/ppermute | solution.py:122
  6.9 13.6 %collective-permute-start.1 = (bf16[2,3,16,1024]{3,2,1,0:T(8,128)(2,1)S(1)}, bf16[2,3,16,1024]{3,2,1,0:T(8,128)(2,1)S(1)}, u32[]{:S(2)}, u32[]{:S(2)}) collective-permute-start(bf16[2,3,16,1024]{3,2,1,0:T(8,128)(2,1)S(1)} %get-tuple-element.39), channel_id=1, source_target_pairs={{0,28},{1,29},{2,30},{3,31},{4,0},{5,1},{6,2},{7,3},{8,4},{9,5},{1... | collective-permute-start | bytes 589832 | tf_op jit(solution)/shard_map/ppermute | solution.py:122
  7.1 13.4 %collective-permute-start.2 = (bf16[3,2,16,1024]{3,2,1,0:T(8,128)(2,1)S(1)}, bf16[3,2,16,1024]{3,2,1,0:T(8,128)(2,1)S(1)}, u32[]{:S(2)}, u32[]{:S(2)}) collective-permute-start(bf16[3,2,16,1024]{3,2,1,0:T(8,128)(2,1)S(1)} %get-tuple-element.40), channel_id=1, source_target_pairs={{0,3},{1,0},{2,1},{3,2},{4,7},{5,4},{6,5},{7,6},{8,11},{9,8},{10,9... | collective-permute-start | bytes 589832 | tf_op jit(solution)/shard_map/ppermute | solution.py:122
  8.3 12.2 %collective-permute-start.3 = (bf16[2,3,16,1024]{3,2,1,0:T(8,128)(2,1)S(1)}, bf16[2,3,16,1024]{3,2,1,0:T(8,128)(2,1)S(1)}, u32[]{:S(2)}, u32[]{:S(2)}) collective-permute-start(bf16[2,3,16,1024]{3,2,1,0:T(8,128)(2,1)S(1)} %get-tuple-element.41), channel_id=1, source_target_pairs={{0,4},{1,5},{2,6},{3,7},{4,8},{5,9},{6,10},{7,11},{8,12},{9,13},{1... | collective-permute-start | bytes 589832 | tf_op jit(solution)/shard_map/ppermute | solution.py:122
  9.9 11.6 %collective-permute-start.4 = (bf16[3,2,16,1024]{3,2,1,0:T(8,128)(2,1)S(1)}, bf16[3,2,16,1024]{3,2,1,0:T(8,128)(2,1)S(1)}, u32[]{:S(2)}, u32[]{:S(2)}) collective-permute-start(bf16[3,2,16,1024]{3,2,1,0:T(8,128)(2,1)S(1)} %get-tuple-element.42), channel_id=1, source_target_pairs={{0,1},{1,2},{2,3},{3,0},{4,5},{5,6},{6,7},{7,4},{8,9},{9,10},{10,1... | collective-permute-start | bytes 589832 | tf_op jit(solution)/shard_map/ppermute | solution.py:122
  12.5 8.0 %collective-permute-start.5 = (bf16[2,2,16,1024]{3,2,1,0:T(8,128)(2,1)S(1)}, bf16[2,2,16,1024]{3,2,1,0:T(8,128)(2,1)S(1)}, u32[]{:S(2)}, u32[]{:S(2)}) collective-permute-start(bf16[2,2,16,1024]{3,2,1,0:T(8,128)(2,1)S(1)} %get-tuple-element.43), channel_id=1, source_target_pairs={{0,5},{1,6},{2,7},{3,4},{4,9},{5,10},{6,11},{7,8},{8,13},{9,14},{1... | collective-permute-start | bytes 393224 | tf_op jit(solution)/shard_map/ppermute | solution.py:122
  12.8 2.8 %copy-start.1 = (bf16[1024,3072]{1,0:T(8,128)(2,1)S(1)}, bf16[1024,3072]{1,0:T(8,128)(2,1)}, u32[]{:S(2)}) copy-start(bf16[1024,3072]{1,0:T(8,128)(2,1)} %w_hbm.1) | copy-start | bytes 18874372
  15.6 0.7 copy-start.5
  16.3 0.7 copy-start.7
  21.5 7.6 %copy-start = (bf16[1024,1024]{1,0:T(8,128)(2,1)S(1)}, bf16[1024,1024]{1,0:T(8,128)(2,1)}, u32[]{:S(2)}) copy-start(bf16[1024,1024]{1,0:T(8,128)(2,1)} %w_out.3) | copy-start | bytes 6291460
  21.5 7.6 %copy-start.2 = (bf16[1024,768]{1,0:T(8,128)(2,1)S(1)}, bf16[1024,768]{1,0:T(8,128)(2,1)}, u32[]{:S(2)}) copy-start(bf16[1024,768]{1,0:T(8,128)(2,1)} %w_emb.3) | copy-start | bytes 4718596
  29.2 16.5 %copy-start.4 = (bf16[2,768]{1,0:T(2,128)(2,1)S(1)}, bf16[2,768]{1,0:T(2,128)(2,1)}, u32[]{:S(2)}) copy-start(bf16[2,768]{1,0:T(2,128)(2,1)} %text.1) | copy-start | bytes 9220
  29.2 16.5 %copy-start.6 = (s32[2,16]{1,0:T(2,128)S(1)}, s32[2,16]{1,0:T(2,128)}, u32[]{:S(2)}) copy-start(s32[2,16]{1,0:T(2,128)} %bucket.1) | copy-start | bytes 388
  29.2 16.5 %copy-start.8 = (f32[4]{0:T(128)S(1)}, f32[4]{0:T(128)}, u32[]{:S(2)}) copy-start(f32[4]{0:T(128)} %levels.1) | copy-start | bytes 52
  69.3 12.9 %collective-permute-start.11 = (bf16[2,2,16,1024]{3,2,1,0:T(8,128)(2,1)S(1)}, bf16[2,2,16,1024]{3,2,1,0:T(8,128)(2,1)S(1)}, u32[]{:S(2)}, u32[]{:S(2)}) collective-permute-start(bf16[2,2,16,1024]{3,2,1,0:T(8,128)(2,1)S(1)} %get-tuple-element.64), channel_id=1, source_target_pairs={{0,5},{1,6},{2,7},{3,4},{4,9},{5,10},{6,11},{7,8},{8,13},{9,14},{1... | collective-permute-start | bytes 393224 | tf_op jit(solution)/shard_map/ppermute | solution.py:122
  72.6 11.3 %collective-permute-start.9 = (bf16[2,3,16,1024]{3,2,1,0:T(8,128)(2,1)S(1)}, bf16[2,3,16,1024]{3,2,1,0:T(8,128)(2,1)S(1)}, u32[]{:S(2)}, u32[]{:S(2)}) collective-permute-start(bf16[2,3,16,1024]{3,2,1,0:T(8,128)(2,1)S(1)} %get-tuple-element.62), channel_id=1, source_target_pairs={{0,4},{1,5},{2,6},{3,7},{4,8},{5,9},{6,10},{7,11},{8,12},{9,13},{1... | collective-permute-start | bytes 589832 | tf_op jit(solution)/shard_map/ppermute | solution.py:122
  72.6 11.3 %collective-permute-start.10 = (bf16[3,2,16,1024]{3,2,1,0:T(8,128)(2,1)S(1)}, bf16[3,2,16,1024]{3,2,1,0:T(8,128)(2,1)S(1)}, u32[]{:S(2)}, u32[]{:S(2)}) collective-permute-start(bf16[3,2,16,1024]{3,2,1,0:T(8,128)(2,1)S(1)} %get-tuple-element.63), channel_id=1, source_target_pairs={{0,1},{1,2},{2,3},{3,0},{4,5},{5,6},{6,7},{7,4},{8,9},{9,10},{10,1... | collective-permute-start | bytes 589832 | tf_op jit(solution)/shard_map/ppermute | solution.py:122
  79.3 9.1 %collective-permute-start.6 = (bf16[2,3,16,1024]{3,2,1,0:T(8,128)(2,1)S(1)}, bf16[2,3,16,1024]{3,2,1,0:T(8,128)(2,1)S(1)}, u32[]{:S(2)}, u32[]{:S(2)}) collective-permute-start(bf16[2,3,16,1024]{3,2,1,0:T(8,128)(2,1)S(1)} %get-tuple-element.58), channel_id=1, source_target_pairs={{0,28},{1,29},{2,30},{3,31},{4,0},{5,1},{6,2},{7,3},{8,4},{9,5},{1... | collective-permute-start | bytes 589832 | tf_op jit(solution)/shard_map/ppermute | solution.py:122
  81.4 9.7 %collective-permute-start.7 = (bf16[3,2,16,1024]{3,2,1,0:T(8,128)(2,1)S(1)}, bf16[3,2,16,1024]{3,2,1,0:T(8,128)(2,1)S(1)}, u32[]{:S(2)}, u32[]{:S(2)}) collective-permute-start(bf16[3,2,16,1024]{3,2,1,0:T(8,128)(2,1)S(1)} %get-tuple-element.59), channel_id=1, source_target_pairs={{0,3},{1,0},{2,1},{3,2},{4,7},{5,4},{6,5},{7,6},{8,11},{9,8},{10,9... | collective-permute-start | bytes 589832 | tf_op jit(solution)/shard_map/ppermute | solution.py:122
  82.2 6.2 %collective-permute-start.8 = (bf16[2,2,16,1024]{3,2,1,0:T(8,128)(2,1)S(1)}, bf16[2,2,16,1024]{3,2,1,0:T(8,128)(2,1)S(1)}, u32[]{:S(2)}, u32[]{:S(2)}) collective-permute-start(bf16[2,2,16,1024]{3,2,1,0:T(8,128)(2,1)S(1)} %get-tuple-element.60), channel_id=1, source_target_pairs={{0,31},{1,28},{2,29},{3,30},{4,3},{5,0},{6,1},{7,2},{8,7},{9,4},{1... | collective-permute-start | bytes 393224 | tf_op jit(solution)/shard_map/ppermute | solution.py:122

commit v4 on v3

--- a/solution.py
+++ b/solution.py
@@ -141,8 +141,6 @@
 
 
 def window_mask(frame0, row0, col0, s0, s1, s2, frames, rows):
-    shape = (TOK, 2 * TOK)
-
     def label(index):
         f = frame0 + index // (WH * WW) + s0
         r = row0 + (index // WW) % WH + s1
@@ -150,8 +148,8 @@
         one = lambda v, n: jnp.where((v < 0) | (v >= n), 1, 0)
         return one(f, frames) * 4 + one(r, rows) * 2 + one(c, COLS)
 
-    key = lax.broadcasted_iota(jnp.int32, shape, 0)
-    query = lax.broadcasted_iota(jnp.int32, shape, 1) % TOK
+    key = lax.broadcasted_iota(jnp.int32, (TOK, 1), 0)
+    query = lax.broadcasted_iota(jnp.int32, (1, 2 * TOK), 1) % TOK
     return jnp.where(label(key) == label(query), 1.0, 0.0)
 
 
@@ -193,7 +191,9 @@
                     istd[pl.ds(start, WW)] = wide[w * WW : (w + 1) * WW]
             return total
 
-        total = lax.fori_loop(0, WT // 2, cells, jnp.zeros((COLS, D), F32))
+        total = jnp.zeros((COLS, D), F32)
+        for half in range(WT // 2):
+            total = cells(half, total)
         sums[2 * n : 2 * n + 1] = jnp.sum(total, axis=0, keepdims=True)
         for w in range(2):
             masks[2 * n + w] = window_mask(
@@ -267,31 +267,31 @@
 
                 firsts.append(first)
                 seconds.append(second)
-        return staged(firsts, seconds)
-
-    interleave(project(0))
+        return firsts, seconds
+
+    units = 4 * nc
+    plan = spread_jobs(project(0), -1, 0)
     for quad in range(QUADS):
-        interleave(attend(quad), project(quad + 1) if quad + 1 < QUADS else [])
-
-
-def staged(*stages, lag=3):
-    count = len(stages[0])
-    jobs = []
-    for turn in range(count + lag * (len(stages) - 1)):
-        for depth, stage in enumerate(stages):
-            unit = turn - lag * depth
-            if 0 <= unit < count:
-                jobs.append(stage[unit])
-    return jobs
-
-
-def interleave(*lists):
-    order = []
-    for which, jobs in enumerate(lists):
-        for k, job in enumerate(jobs):
-            order.append(((k + 0.5) / len(jobs), which, k, job))
-    for item in sorted(order, key=lambda t: t[:3]):
-        item[3]()
+        start = quad * units
+        for depth, stage in enumerate(attend(quad)):
+            plan += spread_jobs(stage, start + depth * LAG_F, start + depth * LAG_F + units)
+        if quad + 1 < QUADS:
+            plan += spread_jobs(project(quad + 1), start, start + units - 0.1)
+    emit(plan)
+
+
+LAG_F = 3
+LAG_B = 2
+
+
+def spread_jobs(jobs, start, end):
+    step = (end - start) / len(jobs)
+    return [(start + k * step, job) for k, job in enumerate(jobs)]
+
+
+def emit(plan):
+    for _, job in sorted(plan, key=lambda item: item[0]):
+        job()
 
 
 def forward(shifts, hscale, video, halo, w_qkv):
@@ -567,7 +567,7 @@
                         done[at, q] = ((g - u * inner) * inverse[at, q]).astype(BF16)
 
                     norms.append(job)
-        return staged(firsts, seconds, thirds, lag=2) + norms
+        return firsts, seconds, thirds, norms
 
     def collect(quad):
         jobs = []
@@ -589,16 +589,24 @@
             jobs.append(job)
         return jobs
 
+    units = 4 * nc
+    plan = []
     for quad in range(QUADS):
-        interleave(attend(quad), collect(quad - 1) if quad else [])
-    interleave(collect(QUADS - 1))
+        *stages, norms = attend(quad)
+        start = quad * units
+        for depth, stage in enumerate(stages):
+            plan += spread_jobs(stage, start + depth * LAG_B, start + depth * LAG_B + units)
+        done = start + 2 * LAG_B + units - 0.9
+        plan += spread_jobs(norms, done, done + 1)
+        plan += spread_jobs(collect(quad), done + 1, done + 1 + units)
+    emit(plan)
     for n, c in enumerate(clips):
         s0, s1, s2 = shifts[c, 0], shifts[c, 1], shifts[c, 2]
         off0, off1 = s0 + HALO * c, s1 + HALO * c
         turn = (COLS + s2) % COLS
         base = clip_grad[c : c + 1]
 
-        def cells(half, carry):
+        def cells(half):
             for j in range(2 * WH):
                 a, b = 2 * half + j // WH, j % WH
                 halves = []
@@ -612,9 +620,9 @@
                     halves.append(base + inv * (dn - first - y * second))
                 cell = pltpu.roll(jnp.concatenate(halves, axis=0), turn, 0)
                 ext[n, a + off0, b + off1] = cell.astype(BF16)
-            return carry
-
-        lax.fori_loop(0, WT // 2, cells, 0)
+
+        for half in range(WT // 2):
+            cells(half)
         f, nf, r, nr = OWN[c]
         outs[4 * n][...] = ext[n, f : f + nf, r : r + nr]
         for k in range(3):

time: 92.7 us -> 91.4 us (0.986)
  Pallas kernels: 26 us -> 24.7 us
where the time goes in v4:
time: 91.4 us; the launch traced here: 91.2 us
  blocking collectives  31.3 us (34%)
  Pallas kernels  24.7 us (27%)
  starting transfers between devices  20.3 us (22%)
  waiting for transfers between devices  8.67 us (9%)
  local copies, waits for them, and re-layouts  5.36 us (6%)
    ppermute x12, starting transfers between devices, exchange(): out.append(lax.ppermute(piece, ('tm', 'space'), pairs))  20.3 us
    all_to_all x1, blocking collectives, local(): got = lax.all_to_all(spread, ('tm', 'space'), 0, 0)  15.8 us
    all_to_all x1, blocking collectives, local(): got = lax.all_to_all(packed, 'batch', 0, 0)  15.6 us
    pallas_call x2, Pallas kernels, backward(): pl.pallas_call(partial(backward_kernel, clips), out_shape=[jax.ShapeDtype...  9.51 us
    ppermute x12, waiting for transfers between devices, exchange(): out.append(lax.ppermute(piece, ('tm', 'space'), pairs))  8.67 us
    pallas_call x1, Pallas kernels, forward(): pl.pallas_call(partial(forward_kernel, clips, frames, rows_all), out_shap...  7.07 us
    unnamed x18, local copies, waits for them, and re-layouts  5.36 us
    pallas_call x2, Pallas kernels, merge(): pl.pallas_call(partial(merge_kernel, clip), grid=(1,), out_shape=jax.Shap...  2.79 us
  transfers between devices with their start and end apart: 12, of which 4 were waited for; matrix products, arithmetic and copies ran while one was open for 0% of the time, Pallas kernels for 9%

profile of v4, /device:TPU:1, one launch (start us, length us, event | category | flops | bytes accessed | tf_op | source)
XLA Modules:
  0.0 91.2 jit_solution(16785248049121902823)
XLA Ops:
  0.6 1.2 %copy-done.3 = bf16[2,4,4,16,1024]{4,3,2,1,0:T(8,128)(2,1)S(1)} copy-done((bf16[2,4,4,16,1024]{4,3,2,1,0:T(8,128)(2,1)S(1)}, bf16[2,4,4,16,1024]{4,3,2,1,0:T(8,128)(2,1)}, u32[]{:S(2)}) %copy-start.3) | copy-done | bytes 1048600
  1.9 0.1 pack.1
  1.9 5.0 %collective-permute-start = (bf16[2,2,16,1024]{3,2,1,0:T(8,128)(2,1)S(1)}, bf16[2,2,16,1024]{3,2,1,0:T(8,128)(2,1)S(1)}, u32[]{:S(2)}, u32[]{:S(2)}) collective-permute-start(bf16[2,2,16,1024]{3,2,1,0:T(8,128)(2,1)S(1)} %get-tuple-element.35), channel_id=1, source_target_pairs={{0,31},{1,28},{2,29},{3,30},{4,3},{5,0},{6,1},{7,2},{8,7},{9,4},{1... | collective-permute-start | bytes 393224 | tf_op jit(solution)/shard_map/ppermute | solution.py:122
  6.9 0.2 collective-permute-start.1
  7.1 1.2 %collective-permute-start.2 = (bf16[3,2,16,1024]{3,2,1,0:T(8,128)(2,1)S(1)}, bf16[3,2,16,1024]{3,2,1,0:T(8,128)(2,1)S(1)}, u32[]{:S(2)}, u32[]{:S(2)}) collective-permute-start(bf16[3,2,16,1024]{3,2,1,0:T(8,128)(2,1)S(1)} %get-tuple-element.40), channel_id=1, source_target_pairs={{0,3},{1,0},{2,1},{3,2},{4,7},{5,4},{6,5},{7,6},{8,11},{9,8},{10,9... | collective-permute-start | bytes 589832 | tf_op jit(solution)/shard_map/ppermute | solution.py:122
  8.3 1.6 %collective-permute-start.3 = (bf16[2,3,16,1024]{3,2,1,0:T(8,128)(2,1)S(1)}, bf16[2,3,16,1024]{3,2,1,0:T(8,128)(2,1)S(1)}, u32[]{:S(2)}, u32[]{:S(2)}) collective-permute-start(bf16[2,3,16,1024]{3,2,1,0:T(8,128)(2,1)S(1)} %get-tuple-element.41), channel_id=1, source_target_pairs={{0,4},{1,5},{2,6},{3,7},{4,8},{5,9},{6,10},{7,11},{8,12},{9,13},{1... | collective-permute-start | bytes 589832 | tf_op jit(solution)/shard_map/ppermute | solution.py:122
  9.9 2.6 %collective-permute-start.4 = (bf16[3,2,16,1024]{3,2,1,0:T(8,128)(2,1)S(1)}, bf16[3,2,16,1024]{3,2,1,0:T(8,128)(2,1)S(1)}, u32[]{:S(2)}, u32[]{:S(2)}) collective-permute-start(bf16[3,2,16,1024]{3,2,1,0:T(8,128)(2,1)S(1)} %get-tuple-element.42), channel_id=1, source_target_pairs={{0,1},{1,2},{2,3},{3,0},{4,5},{5,6},{6,7},{7,4},{8,9},{9,10},{10,1... | collective-permute-start | bytes 589832 | tf_op jit(solution)/shard_map/ppermute | solution.py:122
  12.5 0.3 collective-permute-start.5
  12.8 2.8 %copy-done.1 = bf16[1024,3072]{1,0:T(8,128)(2,1)S(1)} copy-done((bf16[1024,3072]{1,0:T(8,128)(2,1)S(1)}, bf16[1024,3072]{1,0:T(8,128)(2,1)}, u32[]{:S(2)}) %copy-start.1) | copy-done | bytes 6291480
  15.6 0.7 copy-done.5
  16.3 0.7 copy-done.7
  16.9 1.7 %load.1 = (bf16[1024,3072]{1,0:T(8,128)(2,1)S(1)}, bf16[2,4,4,16,1024]{4,3,2,1,0:T(8,128)(2,1)S(1)}, s32[2,3]{1,0:T(2,128)S(1)}, f32[16]{0:T(128)S(1)}) custom-call(bf16[2,2,16,1024]{3,2,1,0:T(8,128)(2,1)S(1)} %collective-permute-done.after.refs_2_, bf16[1024,3072]{1,0:T(8,128)(2,1)S(1)} %copy-done.1, bf16[2,4,4,16,1024]{4,3,2,1,0:T(8,128)(2,1)S(1)} %copy-done.3, ...), custom_call_target="tpu_custom_call" | custom-call | bytes 7340032 | tf_op jit(solution)/shard_map/load/pallas_call | solution.py:96
  18.6 1.8 %collective-permute-done.5.refs_5_ = bf16[2,2,16,1024]{3,2,1,0:T(8,128)(2,1)S(1)} collective-permute-done((bf16[2,2,16,1024]{3,2,1,0:T(8,128)(2,1)S(1)}, bf16[2,2,16,1024]{3,2,1,0:T(8,128)(2,1)S(1)}, u32[]{:S(2)}, u32[]{:S(2)}) %collective-permute-start.5) | collective-permute-done | bytes 131104 | tf_op jit(solution)/shard_map/ppermute | solution.py:122
  20.5 1.1 %collective-permute-done.4.refs_4_ = bf16[3,2,16,1024]{3,2,1,0:T(8,128)(2,1)S(1)} collective-permute-done((bf16[3,2,16,1024]{3,2,1,0:T(8,128)(2,1)S(1)}, bf16[3,2,16,1024]{3,2,1,0:T(8,128)(2,1)S(1)}, u32[]{:S(2)}, u32[]{:S(2)}) %collective-permute-start.4) | collective-permute-done | bytes 196640 | tf_op jit(solution)/shard_map/ppermute | solution.py:122
  21.5 7.1 %forward.1 = (bf16[512,1024]{1,0:T(8,128)(2,1)S(1)}, bf16[512,1024]{1,0:T(8,128)(2,1)S(1)}, bf16[512,1024]{1,0:T(8,128)(2,1)S(1)}, f32[512,1024]{1,0:T(8,128)S(1...) custom-call(s32[2,3]{1,0:T(2,128)S(1)} %get-tuple-element.36.shifts,, ...), custom_call_target="tpu_custom_call" | custom-call | flops 3221225472 | bytes 12582912 | tf_op jit(solution)/shard_map/forward/pallas_call | solution.py:303
  28.6 0.0 copy-start.6
  28.7 0.7 share.1
  29.4 15.8 %all_to_all.10.got = f32[32,2,768]{2,1,0:T(2,128)S(1)} all-to-all(f32[32,2,768]{2,1,0:T(2,128)S(1)} %share.1), channel_id=1, replica_groups=mesh['batch'=8,'tm'=8,'space'=4] {'tm','space'}, dimensions={0} | all-to-all | bytes 393216 | tf_op jit(solution)/shard_map/all_to_all | solution.py:707
  45.2 0.6 embed.1
  45.8 15.6 %all_to_all.11.got = f32[8,4,896]{2,1,0:T(4,128)S(1)} all-to-all(f32[8,4,896]{2,1,0:T(4,128)S(1)} %embed.1), channel_id=1, replica_groups=mesh['batch'=8,'tm'=8,'space'=4] {'batch'}, dimensions={0} | all-to-all | bytes 229376 | tf_op jit(solution)/shard_map/all_to_all | solution.py:709
  61.4 2.2 %contrast.1 = (f32[2,768]{1,0:T(2,128)}, f32[1,1]{1,0:T(1,128)}, f32[2,1024]{1,0:T(2,128)S(1)}, f32[2,1024]{1,0:T(2,128)S(1)}) custom-call(f32[8,4,896]{2,1,0:T(4,128)S(1)} %all_to_all.11.got, bf16[1024,768]{1,0:T(8,128)(2,1)S(1)} %copy-done.2, bf16[1024,1024]{1,0:T(8,128)(2,1)S(1)} %copy-done), custom_call_target="tpu_custom_call" | custom-call | tf_op jit(solution)/shard_map/contrast/pallas_call | solution.py:474
  63.6 4.8 %backward.3 = (bf16[4,4,16,1024]{3,2,1,0:T(8,128)(2,1)S(1)}, bf16[2,3,16,1024]{3,2,1,0:T(8,128)(2,1)S(1)}, bf16[3,2,16,1024]{3,2,1,0:T(8,128)(2,1)S(1)}, bf16[2,2,16,1024]{3,2,1,0:T(8,128)(2,1)S(1)}) custom-call(s32[2,3]{1,0:T(2,128)S(1)} %get-tuple-element.36.shifts, f32[16]{0:T(128)S(1)} %get-tuple-element.37.hscale, ...), custom_call_target="tpu_custom_call" | custom-call | flops 1610612736 | bytes 16777216 | tf_op jit(solution)/shard_map/backward/pallas_call | solution.py:637
  68.4 3.3 %collective-permute-start.11 = (bf16[2,2,16,1024]{3,2,1,0:T(8,128)(2,1)S(1)}, bf16[2,2,16,1024]{3,2,1,0:T(8,128)(2,1)S(1)}, u32[]{:S(2)}, u32[]{:S(2)}) collective-permute-start(bf16[2,2,16,1024]{3,2,1,0:T(8,128)(2,1)S(1)} %get-tuple-element.64), channel_id=1, source_target_pairs={{0,5},{1,6},{2,7},{3,4},{4,9},{5,10},{6,11},{7,8},{8,13},{9,14},{1... | collective-permute-start | bytes 393224 | tf_op jit(solution)/shard_map/ppermute | solution.py:122
  71.7 1.6 %collective-permute-start.10 = (bf16[3,2,16,1024]{3,2,1,0:T(8,128)(2,1)S(1)}, bf16[3,2,16,1024]{3,2,1,0:T(8,128)(2,1)S(1)}, u32[]{:S(2)}, u32[]{:S(2)}) collective-permute-start(bf16[3,2,16,1024]{3,2,1,0:T(8,128)(2,1)S(1)} %get-tuple-element.63), channel_id=1, source_target_pairs={{0,1},{1,2},{2,3},{3,0},{4,5},{5,6},{6,7},{7,4},{8,9},{9,10},{10,1... | collective-permute-start | bytes 589832 | tf_op jit(solution)/shard_map/ppermute | solution.py:122
  73.2 4.8 %backward.2 = (bf16[4,4,16,1024]{3,2,1,0:T(8,128)(2,1)S(1)}, bf16[2,3,16,1024]{3,2,1,0:T(8,128)(2,1)S(1)}, bf16[3,2,16,1024]{3,2,1,0:T(8,128)(2,1)S(1)}, bf16[2,2,16,1024]{3,2,1,0:T(8,128)(2,1)S(1)}) custom-call(s32[2,3]{1,0:T(2,128)S(1)} %get-tuple-element.36.shifts, f32[16]{0:T(128)S(1)} %get-tuple-element.37.hscale, ...), custom_call_target="tpu_custom_call" | custom-call | flops 1610612736 | bytes 16777216 | tf_op jit(solution)/shard_map/backward/pallas_call | solution.py:637
  78.0 2.1 %collective-permute-start.6 = (bf16[2,3,16,1024]{3,2,1,0:T(8,128)(2,1)S(1)}, bf16[2,3,16,1024]{3,2,1,0:T(8,128)(2,1)S(1)}, u32[]{:S(2)}, u32[]{:S(2)}) collective-permute-start(bf16[2,3,16,1024]{3,2,1,0:T(8,128)(2,1)S(1)} %get-tuple-element.58), channel_id=1, source_target_pairs={{0,28},{1,29},{2,30},{3,31},{4,0},{5,1},{6,2},{7,3},{8,4},{9,5},{1... | collective-permute-start | bytes 589832 | tf_op jit(solution)/shard_map/ppermute | solution.py:122
  80.1 0.8 collective-permute-start.7
  80.9 1.7 %collective-permute-start.8 = (bf16[2,2,16,1024]{3,2,1,0:T(8,128)(2,1)S(1)}, bf16[2,2,16,1024]{3,2,1,0:T(8,128)(2,1)S(1)}, u32[]{:S(2)}, u32[]{:S(2)}) collective-permute-start(bf16[2,2,16,1024]{3,2,1,0:T(8,128)(2,1)S(1)} %get-tuple-element.60), channel_id=1, source_target_pairs={{0,31},{1,28},{2,29},{3,30},{4,3},{5,0},{6,1},{7,2},{8,7},{9,4},{1... | collective-permute-start | bytes 393224 | tf_op jit(solution)/shard_map/ppermute | solution.py:122
  82.6 1.4 %merge.2.refs_0_ = bf16[2,4,4,16,1024]{4,3,2,1,0:T(8,128)(2,1)} custom-call(s32[2,3]{1,0:T(2,128)S(1)} %get-tuple-element.36.shifts, bf16[4,4,16,1024]{3,2,1,0:T(8,128)(2,1)S(1)} %get-tuple-element.61.own, bf16[2,3,16,1024]{3,2,1,0:T(8,128)(2,1)S(1)} %collective-permute-done.9.a, bf16[3,2,16,1024]{3,2,1,0:T(8,128)(2,1)S(1)} %collective-permute-done.10.b, ...), custom_call_target="tpu_custom_call" | custom-call | tf_op jit(solution)/shard_map/merge/pallas_call | solution.py:687
  84.0 3.1 %collective-permute-done.8.corner = bf16[2,2,16,1024]{3,2,1,0:T(8,128)(2,1)S(1)} collective-permute-done((bf16[2,2,16,1024]{3,2,1,0:T(8,128)(2,1)S(1)}, bf16[2,2,16,1024]{3,2,1,0:T(8,128)(2,1)S(1)}, u32[]{:S(2)}, u32[]{:S(2)}) %collective-permute-start.8) | collective-permute-done | bytes 131104 | tf_op jit(solution)/shard_map/ppermute | solution.py:122
  87.2 2.6 %collective-permute-done.7.b = bf16[3,2,16,1024]{3,2,1,0:T(8,128)(2,1)S(1)} collective-permute-done((bf16[3,2,16,1024]{3,2,1,0:T(8,128)(2,1)S(1)}, bf16[3,2,16,1024]{3,2,1,0:T(8,128)(2,1)S(1)}, u32[]{:S(2)}, u32[]{:S(2)}) %collective-permute-start.7) | collective-permute-done | bytes 196640 | tf_op jit(solution)/shard_map/ppermute | solution.py:122
  89.8 1.4 %merge.3 = bf16[2,4,4,16,1024]{4,3,2,1,0:T(8,128)(2,1)} custom-call(s32[2,3]{1,0:T(2,128)S(1)} %get-tuple-element.36.shifts, bf16[4,4,16,1024]{3,2,1,0:T(8,128)(2,1)S(1)} %get-tuple-element.57.own, bf16[2,3,16,1024]{3,2,1,0:T(8,128)(2,1)S(1)} %collective-permute-done.6.a, ...), custom_call_target="tpu_custom_call", output_to_operand_aliasing={{}: (5, {})} | custom-call | tf_op jit(solution)/shard_map/merge/pallas_call | solution.py:687
  (22 shorter events, 0.1 us)
Async XLA Ops:
  0.6 1.2 %copy-start.3 = (bf16[2,4,4,16,1024]{4,3,2,1,0:T(8,128)(2,1)S(1)}, bf16[2,4,4,16,1024]{4,3,2,1,0:T(8,128)(2,1)}, u32[]{:S(2)}) copy-start(bf16[2,4,4,16,1024]{4,3,2,1,0:T(8,128)(2,1)} %video_hbm.1) | copy-start | bytes 3145732
  1.9 10.6 %collective-permute-start = (bf16[2,2,16,1024]{3,2,1,0:T(8,128)(2,1)S(1)}, bf16[2,2,16,1024]{3,2,1,0:T(8,128)(2,1)S(1)}, u32[]{:S(2)}, u32[]{:S(2)}) collective-permute-start(bf16[2,2,16,1024]{3,2,1,0:T(8,128)(2,1)S(1)} %get-tuple-element.35), channel_id=1, source_target_pairs={{0,31},{1,28},{2,29},{3,30},{4,3},{5,0},{6,1},{7,2},{8,7},{9,4},{1... | collective-permute-start | bytes 393224 | tf_op jit(solution)/shard_map/ppermute | solution.py:122
  6.9 13.6 %collective-permute-start.1 = (bf16[2,3,16,1024]{3,2,1,0:T(8,128)(2,1)S(1)}, bf16[2,3,16,1024]{3,2,1,0:T(8,128)(2,1)S(1)}, u32[]{:S(2)}, u32[]{:S(2)}) collective-permute-start(bf16[2,3,16,1024]{3,2,1,0:T(8,128)(2,1)S(1)} %get-tuple-element.39), channel_id=1, source_target_pairs={{0,28},{1,29},{2,30},{3,31},{4,0},{5,1},{6,2},{7,3},{8,4},{9,5},{1... | collective-permute-start | bytes 589832 | tf_op jit(solution)/shard_map/ppermute | solution.py:122
  7.1 13.4 %collective-permute-start.2 = (bf16[3,2,16,1024]{3,2,1,0:T(8,128)(2,1)S(1)}, bf16[3,2,16,1024]{3,2,1,0:T(8,128)(2,1)S(1)}, u32[]{:S(2)}, u32[]{:S(2)}) collective-permute-start(bf16[3,2,16,1024]{3,2,1,0:T(8,128)(2,1)S(1)} %get-tuple-element.40), channel_id=1, source_target_pairs={{0,3},{1,0},{2,1},{3,2},{4,7},{5,4},{6,5},{7,6},{8,11},{9,8},{10,9... | collective-permute-start | bytes 589832 | tf_op jit(solution)/shard_map/ppermute | solution.py:122
  8.3 12.2 %collective-permute-start.3 = (bf16[2,3,16,1024]{3,2,1,0:T(8,128)(2,1)S(1)}, bf16[2,3,16,1024]{3,2,1,0:T(8,128)(2,1)S(1)}, u32[]{:S(2)}, u32[]{:S(2)}) collective-permute-start(bf16[2,3,16,1024]{3,2,1,0:T(8,128)(2,1)S(1)} %get-tuple-element.41), channel_id=1, source_target_pairs={{0,4},{1,5},{2,6},{3,7},{4,8},{5,9},{6,10},{7,11},{8,12},{9,13},{1... | collective-permute-start | bytes 589832 | tf_op jit(solution)/shard_map/ppermute | solution.py:122
  9.9 11.6 %collective-permute-start.4 = (bf16[3,2,16,1024]{3,2,1,0:T(8,128)(2,1)S(1)}, bf16[3,2,16,1024]{3,2,1,0:T(8,128)(2,1)S(1)}, u32[]{:S(2)}, u32[]{:S(2)}) collective-permute-start(bf16[3,2,16,1024]{3,2,1,0:T(8,128)(2,1)S(1)} %get-tuple-element.42), channel_id=1, source_target_pairs={{0,1},{1,2},{2,3},{3,0},{4,5},{5,6},{6,7},{7,4},{8,9},{9,10},{10,1... | collective-permute-start | bytes 589832 | tf_op jit(solution)/shard_map/ppermute | solution.py:122
  12.5 8.0 %collective-permute-start.5 = (bf16[2,2,16,1024]{3,2,1,0:T(8,128)(2,1)S(1)}, bf16[2,2,16,1024]{3,2,1,0:T(8,128)(2,1)S(1)}, u32[]{:S(2)}, u32[]{:S(2)}) collective-permute-start(bf16[2,2,16,1024]{3,2,1,0:T(8,128)(2,1)S(1)} %get-tuple-element.43), channel_id=1, source_target_pairs={{0,5},{1,6},{2,7},{3,4},{4,9},{5,10},{6,11},{7,8},{8,13},{9,14},{1... | collective-permute-start | bytes 393224 | tf_op jit(solution)/shard_map/ppermute | solution.py:122
  12.8 2.8 %copy-start.1 = (bf16[1024,3072]{1,0:T(8,128)(2,1)S(1)}, bf16[1024,3072]{1,0:T(8,128)(2,1)}, u32[]{:S(2)}) copy-start(bf16[1024,3072]{1,0:T(8,128)(2,1)} %w_hbm.1) | copy-start | bytes 18874372
  15.6 0.7 copy-start.5
  16.3 0.7 copy-start.7
  21.5 7.1 %copy-start = (bf16[1024,1024]{1,0:T(8,128)(2,1)S(1)}, bf16[1024,1024]{1,0:T(8,128)(2,1)}, u32[]{:S(2)}) copy-start(bf16[1024,1024]{1,0:T(8,128)(2,1)} %w_out.3) | copy-start | bytes 6291460
  21.5 7.1 %copy-start.2 = (bf16[1024,768]{1,0:T(8,128)(2,1)S(1)}, bf16[1024,768]{1,0:T(8,128)(2,1)}, u32[]{:S(2)}) copy-start(bf16[1024,768]{1,0:T(8,128)(2,1)} %w_emb.3) | copy-start | bytes 4718596
  28.6 16.5 %copy-start.4 = (bf16[2,768]{1,0:T(2,128)(2,1)S(1)}, bf16[2,768]{1,0:T(2,128)(2,1)}, u32[]{:S(2)}) copy-start(bf16[2,768]{1,0:T(2,128)(2,1)} %text.1) | copy-start | bytes 9220
  28.6 16.5 %copy-start.6 = (s32[2,16]{1,0:T(2,128)S(1)}, s32[2,16]{1,0:T(2,128)}, u32[]{:S(2)}) copy-start(s32[2,16]{1,0:T(2,128)} %bucket.1) | copy-start | bytes 388
  28.7 16.5 %copy-start.8 = (f32[4]{0:T(128)S(1)}, f32[4]{0:T(128)}, u32[]{:S(2)}) copy-start(f32[4]{0:T(128)} %levels.1) | copy-start | bytes 52
  68.4 12.5 %collective-permute-start.11 = (bf16[2,2,16,1024]{3,2,1,0:T(8,128)(2,1)S(1)}, bf16[2,2,16,1024]{3,2,1,0:T(8,128)(2,1)S(1)}, u32[]{:S(2)}, u32[]{:S(2)}) collective-permute-start(bf16[2,2,16,1024]{3,2,1,0:T(8,128)(2,1)S(1)} %get-tuple-element.64), channel_id=1, source_target_pairs={{0,5},{1,6},{2,7},{3,4},{4,9},{5,10},{6,11},{7,8},{8,13},{9,14},{1... | collective-permute-start | bytes 393224 | tf_op jit(solution)/shard_map/ppermute | solution.py:122
  71.7 10.9 %collective-permute-start.9 = (bf16[2,3,16,1024]{3,2,1,0:T(8,128)(2,1)S(1)}, bf16[2,3,16,1024]{3,2,1,0:T(8,128)(2,1)S(1)}, u32[]{:S(2)}, u32[]{:S(2)}) collective-permute-start(bf16[2,3,16,1024]{3,2,1,0:T(8,128)(2,1)S(1)} %get-tuple-element.62), channel_id=1, source_target_pairs={{0,4},{1,5},{2,6},{3,7},{4,8},{5,9},{6,10},{7,11},{8,12},{9,13},{1... | collective-permute-start | bytes 589832 | tf_op jit(solution)/shard_map/ppermute | solution.py:122
  71.7 10.9 %collective-permute-start.10 = (bf16[3,2,16,1024]{3,2,1,0:T(8,128)(2,1)S(1)}, bf16[3,2,16,1024]{3,2,1,0:T(8,128)(2,1)S(1)}, u32[]{:S(2)}, u32[]{:S(2)}) collective-permute-start(bf16[3,2,16,1024]{3,2,1,0:T(8,128)(2,1)S(1)} %get-tuple-element.63), channel_id=1, source_target_pairs={{0,1},{1,2},{2,3},{3,0},{4,5},{5,6},{6,7},{7,4},{8,9},{9,10},{10,1... | collective-permute-start | bytes 589832 | tf_op jit(solution)/shard_map/ppermute | solution.py:122
  78.0 9.1 %collective-permute-start.6 = (bf16[2,3,16,1024]{3,2,1,0:T(8,128)(2,1)S(1)}, bf16[2,3,16,1024]{3,2,1,0:T(8,128)(2,1)S(1)}, u32[]{:S(2)}, u32[]{:S(2)}) collective-permute-start(bf16[2,3,16,1024]{3,2,1,0:T(8,128)(2,1)S(1)} %get-tuple-element.58), channel_id=1, source_target_pairs={{0,28},{1,29},{2,30},{3,31},{4,0},{5,1},{6,2},{7,3},{8,4},{9,5},{1... | collective-permute-start | bytes 589832 | tf_op jit(solution)/shard_map/ppermute | solution.py:122
  80.1 9.7 %collective-permute-start.7 = (bf16[3,2,16,1024]{3,2,1,0:T(8,128)(2,1)S(1)}, bf16[3,2,16,1024]{3,2,1,0:T(8,128)(2,1)S(1)}, u32[]{:S(2)}, u32[]{:S(2)}) collective-permute-start(bf16[3,2,16,1024]{3,2,1,0:T(8,128)(2,1)S(1)} %get-tuple-element.59), channel_id=1, source_target_pairs={{0,3},{1,0},{2,1},{3,2},{4,7},{5,4},{6,5},{7,6},{8,11},{9,8},{10,9... | collective-permute-start | bytes 589832 | tf_op jit(solution)/shard_map/ppermute | solution.py:122
  80.9 6.3 %collective-permute-start.8 = (bf16[2,2,16,1024]{3,2,1,0:T(8,128)(2,1)S(1)}, bf16[2,2,16,1024]{3,2,1,0:T(8,128)(2,1)S(1)}, u32[]{:S(2)}, u32[]{:S(2)}) collective-permute-start(bf16[2,2,16,1024]{3,2,1,0:T(8,128)(2,1)S(1)} %get-tuple-element.60), channel_id=1, source_target_pairs={{0,31},{1,28},{2,29},{3,30},{4,3},{5,0},{6,1},{7,2},{8,7},{9,4},{1... | collective-permute-start | bytes 393224 | tf_op jit(solution)/shard_map/ppermute | solution.py:122

commit v5 on v4

--- a/solution.py
+++ b/solution.py
@@ -63,50 +63,44 @@
         for k in range(3):
             f, nf, r, nr = GIVEN[c][k]
             outs[3 * c + k][...] = video[c, f : f + nf, r : r + nr]
+    outs[6][...] = video[...]
 
 
 def pack(video):
     return pl.pallas_call(
         pack_kernel,
-        out_shape=[jax.ShapeDtypeStruct(s, BF16) for s in PIECE_SHAPES * 2],
+        out_shape=[jax.ShapeDtypeStruct(s, BF16) for s in PIECE_SHAPES * 2 + (video.shape,)],
         in_specs=[vmem()],
-        out_specs=[vmem()] * 6,
+        out_specs=[vmem()] * 7,
         compiler_params=params(4),
         name="pack",
     )(video)
 
 
-def load_kernel(after, w_hbm, video_hbm, shifts, hscale, w_out, video_out, shifts_out, scale_out, sems):
-    copies = [
-        pltpu.make_async_copy(w_hbm, w_out, sems.at[0]),
-        pltpu.make_async_copy(video_hbm, video_out, sems.at[1]),
-    ]
-    for copy in copies:
-        copy.start()
-    for c in range(2):
-        for k in range(3):
-            shifts_out[c, k] = shifts[c, k]
-    for h in range(HEADS):
-        scale_out[h] = hscale[h]
-    for copy in copies:
-        copy.wait()
-
-
-def load(after, w_qkv, video, shifts, hscale):
+def load_kernel(after, w_hbm, w_out, sem):
+    copy = pltpu.make_async_copy(w_hbm, w_out, sem)
+    copy.start()
+    copy.wait()
+
+
+def load(after, w_qkv):
+    anywhere = pl.BlockSpec(memory_space=pl.ANY)
     return pl.pallas_call(
         load_kernel,
-        out_shape=[
-            jax.ShapeDtypeStruct(x.shape, x.dtype) for x in (w_qkv, video, shifts, hscale)
-        ],
-        in_specs=[pl.BlockSpec(memory_space=pl.ANY)] * 3 + [smem()] * 2,
-        out_specs=[vmem()] * 2 + [smem()] * 2,
-        scratch_shapes=[pltpu.SemaphoreType.DMA((2,))],
+        out_shape=jax.ShapeDtypeStruct(w_qkv.shape, w_qkv.dtype),
+        in_specs=[anywhere] * 2,
+        out_specs=vmem(),
+        scratch_shapes=[pltpu.SemaphoreType.DMA],
         compiler_params=params(4),
         cost_estimate=pl.CostEstimate(
-            flops=0, bytes_accessed=2 * (w_qkv.size + video.size), transcendentals=0
+            flops=0, bytes_accessed=4 * w_qkv.size, transcendentals=0
         ),
         name="load",
-    )(after, w_qkv, video, shifts, hscale)
+    )(after, w_qkv)
+
+
+def shift_of(small, clip):
+    return tuple(small[1 + clip, k].astype(jnp.int32) for k in range(3))
 
 
 def exchange(pieces, clip, sign):
@@ -153,7 +147,7 @@
     return jnp.where(label(key) == label(query), 1.0, 0.0)
 
 
-def forward_kernel(clips, frames, rows_all, shifts, hscale, video, *refs):
+def forward_kernel(clips, frames, rows_all, small, video, *refs):
     nc = len(clips)
     frame0 = lax.axis_index("tm") * WT
     row0 = lax.axis_index("space") * WH
@@ -169,7 +163,7 @@
         for k in range(3):
             f, nf, r, nr = PIECES[c][k]
             ext[n, f : f + nf, r : r + nr] = halo[3 * n + k][...]
-        s0, s1, s2 = shifts[c, 0], shifts[c, 1], shifts[c, 2]
+        s0, s1, s2 = shift_of(small, c)
         off0, off1 = s0 + HALO * c, s1 + HALO * c
         turn = (COLS - s2) % COLS
 
@@ -243,7 +237,7 @@
                 held = {}
 
                 def first(head=head, lanes=lanes, w=w, at=at, p=p, held=held):
-                    factor = jnp.where(lane < TOK, hscale[head], hscale[head + 1]) * LOG2E
+                    factor = jnp.where(lane < TOK, small[0, head], small[0, head + 1]) * LOG2E
                     score = lax.dot_general(
                         kl[at, lanes], split_heads(ql[at, lanes]), NT, preferred_element_type=F32
                     )
@@ -294,7 +288,7 @@
         job()
 
 
-def forward(shifts, hscale, video, halo, w_qkv):
+def forward(small, video, halo, w_qkv):
     clips = (0, 1)
     nc = len(clips)
     n = nc * 2 * TOK
@@ -310,7 +304,7 @@
             jax.ShapeDtypeStruct((n, 128), F32),
             jax.ShapeDtypeStruct((2 * nc, D), F32),
         ],
-        in_specs=[smem(), smem()] + [vmem()] * (2 + 3 * nc),
+        in_specs=[smem()] + [vmem()] * (2 + 3 * nc),
         out_specs=[vmem()] * 10,
         scratch_shapes=[
             pltpu.VMEM((nc, GRID, GRID, COLS, D), BF16),
@@ -326,7 +320,7 @@
             flops=2 * n * D * 3 * D, bytes_accessed=12 * 2**20, transcendentals=n * 2048
         ),
         name="forward",
-    )(shifts, hscale, video, *halo, w_qkv)
+    )(small, video, *halo, w_qkv)
 
 
 def share_kernel(tokens, sums, w_out, w_emb, out):
@@ -486,7 +480,7 @@
     )(got, w_emb, w_out)
 
 
-def backward_kernel(clips, shifts, hscale, clip_grad, d_out, *refs):
+def backward_kernel(clips, small, clip_grad, d_out, *refs):
     nc = len(clips)
     mine = pl.ds(clips[0] * 2 * TOK, nc * 2 * TOK)
     ql, kl, vl, rq, rk, mass = (ref.at[mine] for ref in refs[:6])
@@ -507,7 +501,7 @@
             for p in range(2):
                 head = quad * 4 + 2 * p
                 lanes = slice(quad * QW + p * 128, quad * QW + (p + 1) * 128)
-                factor = jnp.where(lane < HEAD_DIM, hscale[head], hscale[head + 1])
+                factor = jnp.where(lane < HEAD_DIM, small[0, head], small[0, head + 1])
                 shared = {}
                 for w in range(2 * n, 2 * n + 2):
                     at = slice(w * TOK, (w + 1) * TOK)
@@ -601,7 +595,7 @@
         plan += spread_jobs(collect(quad), done + 1, done + 1 + units)
     emit(plan)
     for n, c in enumerate(clips):
-        s0, s1, s2 = shifts[c, 0], shifts[c, 1], shifts[c, 2]
+        s0, s1, s2 = shift_of(small, c)
         off0, off1 = s0 + HALO * c, s1 + HALO * c
         turn = (COLS + s2) % COLS
         base = clip_grad[c : c + 1]
@@ -630,14 +624,14 @@
             outs[4 * n + 1 + k][...] = ext[n, f : f + nf, r : r + nr]
 
 
-def backward(clips, shifts, hscale, clip_grad, d_out, stored, w_qkv):
+def backward(clips, small, clip_grad, d_out, stored, w_qkv):
     nc = len(clips)
     n = nc * 2 * TOK
     shapes = ((WT, WH, COLS, D),) + PIECE_SHAPES
     return pl.pallas_call(
         partial(backward_kernel, clips),
         out_shape=[jax.ShapeDtypeStruct(s, BF16) for s in shapes * nc],
-        in_specs=[smem(), smem()] + [vmem()] * 12,
+        in_specs=[smem()] + [vmem()] * 12,
         out_specs=[vmem()] * (4 * nc),
         scratch_shapes=[
             pltpu.VMEM((nc, GRID, GRID, COLS, D), BF16),
@@ -654,12 +648,12 @@
             flops=2 * n * D * 3 * D, bytes_accessed=16 * 2**20, transcendentals=0
         ),
         name="backward",
-    )(shifts, hscale, clip_grad, d_out, *stored, w_qkv)
-
-
-def merge_kernel(c, shifts, own, a, b, corner, *refs):
+    )(small, clip_grad, d_out, *stored, w_qkv)
+
+
+def merge_kernel(c, small, own, a, b, corner, *refs):
     out = refs[-1]
-    s0, s1 = shifts[c, 0], shifts[c, 1]
+    s0, s1, _ = shift_of(small, c)
     for f in range(WT):
         for r in range(WH):
             if c == 0:
@@ -682,7 +676,7 @@
             out[0, f, r] = value
 
 
-def merge(clip, shifts, own, got, other=None):
+def merge(clip, small, own, got, other=None):
     rest = [] if other is None else [other]
     return pl.pallas_call(
         partial(merge_kernel, clip),
@@ -693,16 +687,18 @@
         input_output_aliases={5: 0} if rest else {},
         compiler_params=params(4),
         name="merge",
-    )(shifts, own, *got, *rest)
+    )(small, own, *got, *rest)
 
 
 def local(video, shifts, head_scale, w_qkv, w_out, w_emb, text, bucket, bucket_scale):
     tokens = lax.axis_size("tm") * lax.axis_size("space") * WT * WH * COLS
     peers = lax.axis_size("batch")
-    pieces = pack(video)
+    *pieces, video = pack(video)
     halo = exchange(pieces[:3], 0, -1) + exchange(pieces[3:], 1, -1)
-    w_qkv, video, shifts, head_scale = load(halo[2], w_qkv, video, shifts, head_scale)
-    *stored, sums = forward(shifts, head_scale, video, halo, w_qkv)
+    wide = jnp.pad(shifts.astype(F32), ((0, 0), (0, HEADS - shifts.shape[1])))
+    small = jnp.concatenate([head_scale[None], wide], axis=0)
+    w_qkv = load(halo[0], w_qkv)
+    *stored, sums = forward(small, video, halo, w_qkv)
     spread = share(sums, w_out, w_emb, tokens)
     got = lax.all_to_all(spread, ("tm", "space"), 0, 0)
     packed = embed(got, text, bucket, bucket_scale, peers)
@@ -710,10 +706,10 @@
     text_grad, loss, clip_grad, d_out = contrast(got, w_emb, w_out)
     parts = []
     for c in range(2):
-        mine, *pieces = backward((c,), shifts, head_scale, clip_grad, d_out, stored, w_qkv)
+        mine, *pieces = backward((c,), small, clip_grad, d_out, stored, w_qkv)
         parts.append((mine, exchange(pieces, c, 1)))
-    video_grad = merge(0, shifts, *parts[0])
-    video_grad = merge(1, shifts, *parts[1], video_grad)
+    video_grad = merge(0, small, *parts[0])
+    video_grad = merge(1, small, *parts[1], video_grad)
     return (video_grad, text_grad, loss[0, 0])
 
 

time: 91.4 us -> 91 us (level)
  starting transfers between devices: 20.3 us -> 21.7 us
  other arithmetic: 0 us -> 1.34 us
  local copies, waits for them, and re-layouts: 5.36 us -> 4.03 us
  Pallas kernels: 24.7 us -> 23.5 us
    ppermute x12, starting transfers between devices: 20.3 us -> 21.7 us  [exchange(): out.append(lax.ppermute(piece, ('tm', 'space'), pairs))]
    unnamed x18 -> x14, local copies, waits for them, and re-layouts: 5.36 us -> 4.03 us
    pallas_call x1, Pallas kernels: 1.68 us -> 0.43 us  [load(): pl.pallas_call(load_kernel, out_shape=jax.ShapeDtypeStruct(w_qkv.shape, w...]
  transfers between devices with their start and end apart: 12 -> 12, of which waited for: 4 -> 3; matrix products, arithmetic and copies ran while one was open for 0% -> 1% of each run, Pallas kernels for 9% -> 7%
where the time goes in v5:
time: 91 us; the launch traced here: 90.7 us
  blocking collectives  31.4 us (35%)
  Pallas kernels  23.5 us (26%)
  starting transfers between devices  21.7 us (24%)
  waiting for transfers between devices  7.93 us (9%)
  local copies, waits for them, and re-layouts  4.03 us (4%)
  other arithmetic  1.34 us (1%)
    ppermute x12, starting transfers between devices, exchange(): out.append(lax.ppermute(piece, ('tm', 'space'), pairs))  21.7 us
    all_to_all x1, blocking collectives, local(): got = lax.all_to_all(spread, ('tm', 'space'), 0, 0)  15.8 us
    all_to_all x1, blocking collectives, local(): got = lax.all_to_all(packed, 'batch', 0, 0)  15.6 us
    pallas_call x2, Pallas kernels, backward(): pl.pallas_call(partial(backward_kernel, clips), out_shape=[jax.ShapeDtype...  9.49 us
    ppermute x12, waiting for transfers between devices, exchange(): out.append(lax.ppermute(piece, ('tm', 'space'), pairs))  7.93 us
    pallas_call x1, Pallas kernels, forward(): pl.pallas_call(partial(forward_kernel, clips, frames, rows_all), out_shap...  7.08 us
    unnamed x14, local copies, waits for them, and re-layouts  4.03 us
    pallas_call x2, Pallas kernels, merge(): pl.pallas_call(partial(merge_kernel, clip), grid=(1,), out_shape=jax.Shap...  2.83 us
  transfers between devices with their start and end apart: 12, of which 3 were waited for; matrix products, arithmetic and copies ran while one was open for 1% of the time, Pallas kernels for 7%

profile of v5, /device:TPU:1, one launch (start us, length us, event | category | flops | bytes accessed | tf_op | source)
XLA Modules:
  0.0 90.7 jit_solution(14612276019854734306)
XLA Ops:
  0.6 1.2 %copy-done.3 = bf16[2,4,4,16,1024]{4,3,2,1,0:T(8,128)(2,1)S(1)} copy-done((bf16[2,4,4,16,1024]{4,3,2,1,0:T(8,128)(2,1)S(1)}, bf16[2,4,4,16,1024]{4,3,2,1,0:T(8,128)(2,1)}, u32[]{:S(2)}) %copy-start.3) | copy-done | bytes 1048600
  1.9 0.1 pack.1
  2.0 4.4 %collective-permute-start = (bf16[2,3,16,1024]{3,2,1,0:T(8,128)(2,1)S(1)}, bf16[2,3,16,1024]{3,2,1,0:T(8,128)(2,1)S(1)}, u32[]{:S(2)}, u32[]{:S(2)}) collective-permute-start(bf16[2,3,16,1024]{3,2,1,0:T(8,128)(2,1)S(1)} %get-tuple-element.33), channel_id=1, source_target_pairs={{0,28},{1,29},{2,30},{3,31},{4,0},{5,1},{6,2},{7,3},{8,4},{9,5},{1... | collective-permute-start | bytes 589832 | tf_op jit(solution)/shard_map/ppermute | solution.py:116
  6.4 1.0 %collective-permute-start.1 = (bf16[3,2,16,1024]{3,2,1,0:T(8,128)(2,1)S(1)}, bf16[3,2,16,1024]{3,2,1,0:T(8,128)(2,1)S(1)}, u32[]{:S(2)}, u32[]{:S(2)}) collective-permute-start(bf16[3,2,16,1024]{3,2,1,0:T(8,128)(2,1)S(1)} %get-tuple-element.34), channel_id=1, source_target_pairs={{0,3},{1,0},{2,1},{3,2},{4,7},{5,4},{6,5},{7,6},{8,11},{9,8},{10,9... | collective-permute-start | bytes 589832 | tf_op jit(solution)/shard_map/ppermute | solution.py:116
  7.4 2.5 %collective-permute-start.4 = (bf16[3,2,16,1024]{3,2,1,0:T(8,128)(2,1)S(1)}, bf16[3,2,16,1024]{3,2,1,0:T(8,128)(2,1)S(1)}, u32[]{:S(2)}, u32[]{:S(2)}) collective-permute-start(bf16[3,2,16,1024]{3,2,1,0:T(8,128)(2,1)S(1)} %get-tuple-element.37), channel_id=1, source_target_pairs={{0,1},{1,2},{2,3},{3,0},{4,5},{5,6},{6,7},{7,4},{8,9},{9,10},{10,1... | collective-permute-start | bytes 589832 | tf_op jit(solution)/shard_map/ppermute | solution.py:116
  9.9 3.3 %collective-permute-start.2 = (bf16[2,2,16,1024]{3,2,1,0:T(8,128)(2,1)S(1)}, bf16[2,2,16,1024]{3,2,1,0:T(8,128)(2,1)S(1)}, u32[]{:S(2)}, u32[]{:S(2)}) collective-permute-start(bf16[2,2,16,1024]{3,2,1,0:T(8,128)(2,1)S(1)} %get-tuple-element.35), channel_id=1, source_target_pairs={{0,31},{1,28},{2,29},{3,30},{4,3},{5,0},{6,1},{7,2},{8,7},{9,4},{1... | collective-permute-start | bytes 393224 | tf_op jit(solution)/shard_map/ppermute | solution.py:116
  13.2 1.1 %collective-permute-start.5 = (bf16[2,2,16,1024]{3,2,1,0:T(8,128)(2,1)S(1)}, bf16[2,2,16,1024]{3,2,1,0:T(8,128)(2,1)S(1)}, u32[]{:S(2)}, u32[]{:S(2)}) collective-permute-start(bf16[2,2,16,1024]{3,2,1,0:T(8,128)(2,1)S(1)} %get-tuple-element.38), channel_id=1, source_target_pairs={{0,5},{1,6},{2,7},{3,4},{4,9},{5,10},{6,11},{7,8},{8,13},{9,14},{1... | collective-permute-start | bytes 393224 | tf_op jit(solution)/shard_map/ppermute | solution.py:116
  14.3 0.7 convert_element_type.5
  14.9 0.7 select_maximum_fusion.small
  15.6 2.8 %copy-done.1 = bf16[1024,3072]{1,0:T(8,128)(2,1)S(1)} copy-done((bf16[1024,3072]{1,0:T(8,128)(2,1)S(1)}, bf16[1024,3072]{1,0:T(8,128)(2,1)}, u32[]{:S(2)}) %copy-start.1) | copy-done | bytes 6291480
  18.4 0.4 load.1.refs_6_.refs_9_
  18.8 2.2 %collective-permute-done.5.refs_5_ = bf16[2,2,16,1024]{3,2,1,0:T(8,128)(2,1)S(1)} collective-permute-done((bf16[2,2,16,1024]{3,2,1,0:T(8,128)(2,1)S(1)}, bf16[2,2,16,1024]{3,2,1,0:T(8,128)(2,1)S(1)}, u32[]{:S(2)}, u32[]{:S(2)}) %collective-permute-start.5) | collective-permute-done | bytes 131104 | tf_op jit(solution)/shard_map/ppermute | solution.py:116
  21.0 0.0 copy-start
  21.0 0.0 copy-start.2
  21.1 7.1 %forward.1 = (bf16[512,1024]{1,0:T(8,128)(2,1)S(1)}, bf16[512,1024]{1,0:T(8,128)(2,1)S(1)}, bf16[512,1024]{1,0:T(8,128)(2,1)S(1)}, f32[512,1024]{1,0:T(8,128)S(1...) custom-call(f32[3,16]{1,0:T(4,128)S(1)} %select_maximum_fusion.small, ...), custom_call_target="tpu_custom_call" | custom-call | flops 3221225472 | bytes 12582912 | tf_op jit(solution)/shard_map/forward/pallas_call | solution.py:297
  28.2 0.0 copy-start.6
  28.2 0.7 share.1
  28.9 15.8 %all_to_all.10.got = f32[32,2,768]{2,1,0:T(2,128)S(1)} all-to-all(f32[32,2,768]{2,1,0:T(2,128)S(1)} %share.1), channel_id=1, replica_groups=mesh['batch'=8,'tm'=8,'space'=4] {'tm','space'}, dimensions={0} | all-to-all | bytes 393216 | tf_op jit(solution)/shard_map/all_to_all | solution.py:703
  44.7 0.6 embed.1
  45.4 15.6 %all_to_all.11.got = f32[8,4,896]{2,1,0:T(4,128)S(1)} all-to-all(f32[8,4,896]{2,1,0:T(4,128)S(1)} %embed.1), channel_id=1, replica_groups=mesh['batch'=8,'tm'=8,'space'=4] {'batch'}, dimensions={0} | all-to-all | bytes 229376 | tf_op jit(solution)/shard_map/all_to_all | solution.py:705
  61.0 2.2 %contrast.1 = (f32[2,768]{1,0:T(2,128)}, f32[1,1]{1,0:T(1,128)}, f32[2,1024]{1,0:T(2,128)S(1)}, f32[2,1024]{1,0:T(2,128)S(1)}) custom-call(f32[8,4,896]{2,1,0:T(4,128)S(1)} %all_to_all.11.got, bf16[1024,768]{1,0:T(8,128)(2,1)S(1)} %copy-done.2, bf16[1024,1024]{1,0:T(8,128)(2,1)S(1)} %copy-done), custom_call_target="tpu_custom_call" | custom-call | tf_op jit(solution)/shard_map/contrast/pallas_call | solution.py:468
  63.2 4.7 %backward.3 = (bf16[4,4,16,1024]{3,2,1,0:T(8,128)(2,1)S(1)}, bf16[2,3,16,1024]{3,2,1,0:T(8,128)(2,1)S(1)}, bf16[3,2,16,1024]{3,2,1,0:T(8,128)(2,1)S(1)}, bf16[2,2,16,1024]{3,2,1,0:T(8,128)(2,1)S(1)}) custom-call(f32[3,16]{1,0:T(4,128)S(1)} %select_maximum_fusion.small, f32[2,1024]{1,0:T(2,128)S(1)} %get-tuple-element.40.clip_grad, ...), custom_call_target="tpu_custom_call" | custom-call | flops 1610612736 | bytes 16777216 | tf_op jit(solution)/shard_map/backward/pallas_call | solution.py:631
  67.9 3.3 %collective-permute-start.11 = (bf16[2,2,16,1024]{3,2,1,0:T(8,128)(2,1)S(1)}, bf16[2,2,16,1024]{3,2,1,0:T(8,128)(2,1)S(1)}, u32[]{:S(2)}, u32[]{:S(2)}) collective-permute-start(bf16[2,2,16,1024]{3,2,1,0:T(8,128)(2,1)S(1)} %get-tuple-element.58), channel_id=1, source_target_pairs={{0,5},{1,6},{2,7},{3,4},{4,9},{5,10},{6,11},{7,8},{8,13},{9,14},{1... | collective-permute-start | bytes 393224 | tf_op jit(solution)/shard_map/ppermute | solution.py:116
  71.2 1.6 %collective-permute-start.10 = (bf16[3,2,16,1024]{3,2,1,0:T(8,128)(2,1)S(1)}, bf16[3,2,16,1024]{3,2,1,0:T(8,128)(2,1)S(1)}, u32[]{:S(2)}, u32[]{:S(2)}) collective-permute-start(bf16[3,2,16,1024]{3,2,1,0:T(8,128)(2,1)S(1)} %get-tuple-element.57), channel_id=1, source_target_pairs={{0,1},{1,2},{2,3},{3,0},{4,5},{5,6},{6,7},{7,4},{8,9},{9,10},{10,1... | collective-permute-start | bytes 589832 | tf_op jit(solution)/shard_map/ppermute | solution.py:116
  72.8 4.7 %backward.2 = (bf16[4,4,16,1024]{3,2,1,0:T(8,128)(2,1)S(1)}, bf16[2,3,16,1024]{3,2,1,0:T(8,128)(2,1)S(1)}, bf16[3,2,16,1024]{3,2,1,0:T(8,128)(2,1)S(1)}, bf16[2,2,16,1024]{3,2,1,0:T(8,128)(2,1)S(1)}) custom-call(f32[3,16]{1,0:T(4,128)S(1)} %select_maximum_fusion.small, f32[2,1024]{1,0:T(2,128)S(1)} %get-tuple-element.40.clip_grad, ...), custom_call_target="tpu_custom_call" | custom-call | flops 1610612736 | bytes 16777216 | tf_op jit(solution)/shard_map/backward/pallas_call | solution.py:631
  77.5 2.1 %collective-permute-start.6 = (bf16[2,3,16,1024]{3,2,1,0:T(8,128)(2,1)S(1)}, bf16[2,3,16,1024]{3,2,1,0:T(8,128)(2,1)S(1)}, u32[]{:S(2)}, u32[]{:S(2)}) collective-permute-start(bf16[2,3,16,1024]{3,2,1,0:T(8,128)(2,1)S(1)} %get-tuple-element.52), channel_id=1, source_target_pairs={{0,28},{1,29},{2,30},{3,31},{4,0},{5,1},{6,2},{7,3},{8,4},{9,5},{1... | collective-permute-start | bytes 589832 | tf_op jit(solution)/shard_map/ppermute | solution.py:116
  79.6 0.8 collective-permute-start.7
  80.4 1.7 %collective-permute-start.8 = (bf16[2,2,16,1024]{3,2,1,0:T(8,128)(2,1)S(1)}, bf16[2,2,16,1024]{3,2,1,0:T(8,128)(2,1)S(1)}, u32[]{:S(2)}, u32[]{:S(2)}) collective-permute-start(bf16[2,2,16,1024]{3,2,1,0:T(8,128)(2,1)S(1)} %get-tuple-element.54), channel_id=1, source_target_pairs={{0,31},{1,28},{2,29},{3,30},{4,3},{5,0},{6,1},{7,2},{8,7},{9,4},{1... | collective-permute-start | bytes 393224 | tf_op jit(solution)/shard_map/ppermute | solution.py:116
  82.1 1.4 %merge.2.refs_0_ = bf16[2,4,4,16,1024]{4,3,2,1,0:T(8,128)(2,1)} custom-call(f32[3,16]{1,0:T(4,128)S(1)} %select_maximum_fusion.small, bf16[4,4,16,1024]{3,2,1,0:T(8,128)(2,1)S(1)} %get-tuple-element.55.own, bf16[2,3,16,1024]{3,2,1,0:T(8,128)(2,1)S(1)} %collective-permute-done.9.a, bf16[3,2,16,1024]{3,2,1,0:T(8,128)(2,1)S(1)} %collective-permute-done.10.b, ...), custom_call_target="tpu_custom_call" | custom-call | tf_op jit(solution)/shard_map/merge/pallas_call | solution.py:681
  83.6 3.1 %collective-permute-done.8.corner = bf16[2,2,16,1024]{3,2,1,0:T(8,128)(2,1)S(1)} collective-permute-done((bf16[2,2,16,1024]{3,2,1,0:T(8,128)(2,1)S(1)}, bf16[2,2,16,1024]{3,2,1,0:T(8,128)(2,1)S(1)}, u32[]{:S(2)}, u32[]{:S(2)}) %collective-permute-start.8) | collective-permute-done | bytes 131104 | tf_op jit(solution)/shard_map/ppermute | solution.py:116
  86.7 2.6 %collective-permute-done.7.b = bf16[3,2,16,1024]{3,2,1,0:T(8,128)(2,1)S(1)} collective-permute-done((bf16[3,2,16,1024]{3,2,1,0:T(8,128)(2,1)S(1)}, bf16[3,2,16,1024]{3,2,1,0:T(8,128)(2,1)S(1)}, u32[]{:S(2)}, u32[]{:S(2)}) %collective-permute-start.7) | collective-permute-done | bytes 196640 | tf_op jit(solution)/shard_map/ppermute | solution.py:116
  89.3 1.4 %merge.3 = bf16[2,4,4,16,1024]{4,3,2,1,0:T(8,128)(2,1)} custom-call(f32[3,16]{1,0:T(4,128)S(1)} %select_maximum_fusion.small, bf16[4,4,16,1024]{3,2,1,0:T(8,128)(2,1)S(1)} %get-tuple-element.51.own, bf16[2,3,16,1024]{3,2,1,0:T(8,128)(2,1)S(1)} %collective-permute-done.6.a, ...), custom_call_target="tpu_custom_call", output_to_operand_aliasing={{}: (5, {})} | custom-call | tf_op jit(solution)/shard_map/merge/pallas_call | solution.py:681
  (20 shorter events, 0.1 us)
Async XLA Ops:
  0.6 1.2 %copy-start.3 = (bf16[2,4,4,16,1024]{4,3,2,1,0:T(8,128)(2,1)S(1)}, bf16[2,4,4,16,1024]{4,3,2,1,0:T(8,128)(2,1)}, u32[]{:S(2)}) copy-start(bf16[2,4,4,16,1024]{4,3,2,1,0:T(8,128)(2,1)} %video.1) | copy-start | bytes 3145732
  2.0 11.2 %collective-permute-start = (bf16[2,3,16,1024]{3,2,1,0:T(8,128)(2,1)S(1)}, bf16[2,3,16,1024]{3,2,1,0:T(8,128)(2,1)S(1)}, u32[]{:S(2)}, u32[]{:S(2)}) collective-permute-start(bf16[2,3,16,1024]{3,2,1,0:T(8,128)(2,1)S(1)} %get-tuple-element.33), channel_id=1, source_target_pairs={{0,28},{1,29},{2,30},{3,31},{4,0},{5,1},{6,2},{7,3},{8,4},{9,5},{1... | collective-permute-start | bytes 589832 | tf_op jit(solution)/shard_map/ppermute | solution.py:116
  6.4 14.6 %collective-permute-start.1 = (bf16[3,2,16,1024]{3,2,1,0:T(8,128)(2,1)S(1)}, bf16[3,2,16,1024]{3,2,1,0:T(8,128)(2,1)S(1)}, u32[]{:S(2)}, u32[]{:S(2)}) collective-permute-start(bf16[3,2,16,1024]{3,2,1,0:T(8,128)(2,1)S(1)} %get-tuple-element.34), channel_id=1, source_target_pairs={{0,3},{1,0},{2,1},{3,2},{4,7},{5,4},{6,5},{7,6},{8,11},{9,8},{10,9... | collective-permute-start | bytes 589832 | tf_op jit(solution)/shard_map/ppermute | solution.py:116
  7.3 13.7 %collective-permute-start.3 = (bf16[2,3,16,1024]{3,2,1,0:T(8,128)(2,1)S(1)}, bf16[2,3,16,1024]{3,2,1,0:T(8,128)(2,1)S(1)}, u32[]{:S(2)}, u32[]{:S(2)}) collective-permute-start(bf16[2,3,16,1024]{3,2,1,0:T(8,128)(2,1)S(1)} %get-tuple-element.36), channel_id=1, source_target_pairs={{0,4},{1,5},{2,6},{3,7},{4,8},{5,9},{6,10},{7,11},{8,12},{9,13},{1... | collective-permute-start | bytes 589832 | tf_op jit(solution)/shard_map/ppermute | solution.py:116
  7.4 13.7 %collective-permute-start.4 = (bf16[3,2,16,1024]{3,2,1,0:T(8,128)(2,1)S(1)}, bf16[3,2,16,1024]{3,2,1,0:T(8,128)(2,1)S(1)}, u32[]{:S(2)}, u32[]{:S(2)}) collective-permute-start(bf16[3,2,16,1024]{3,2,1,0:T(8,128)(2,1)S(1)} %get-tuple-element.37), channel_id=1, source_target_pairs={{0,1},{1,2},{2,3},{3,0},{4,5},{5,6},{6,7},{7,4},{8,9},{9,10},{10,1... | collective-permute-start | bytes 589832 | tf_op jit(solution)/shard_map/ppermute | solution.py:116
  9.9 9.0 %collective-permute-start.2 = (bf16[2,2,16,1024]{3,2,1,0:T(8,128)(2,1)S(1)}, bf16[2,2,16,1024]{3,2,1,0:T(8,128)(2,1)S(1)}, u32[]{:S(2)}, u32[]{:S(2)}) collective-permute-start(bf16[2,2,16,1024]{3,2,1,0:T(8,128)(2,1)S(1)} %get-tuple-element.35), channel_id=1, source_target_pairs={{0,31},{1,28},{2,29},{3,30},{4,3},{5,0},{6,1},{7,2},{8,7},{9,4},{1... | collective-permute-start | bytes 393224 | tf_op jit(solution)/shard_map/ppermute | solution.py:116
  13.2 7.9 %collective-permute-start.5 = (bf16[2,2,16,1024]{3,2,1,0:T(8,128)(2,1)S(1)}, bf16[2,2,16,1024]{3,2,1,0:T(8,128)(2,1)S(1)}, u32[]{:S(2)}, u32[]{:S(2)}) collective-permute-start(bf16[2,2,16,1024]{3,2,1,0:T(8,128)(2,1)S(1)} %get-tuple-element.38), channel_id=1, source_target_pairs={{0,5},{1,6},{2,7},{3,4},{4,9},{5,10},{6,11},{7,8},{8,13},{9,14},{1... | collective-permute-start | bytes 393224 | tf_op jit(solution)/shard_map/ppermute | solution.py:116
  15.6 2.8 %copy-start.1 = (bf16[1024,3072]{1,0:T(8,128)(2,1)S(1)}, bf16[1024,3072]{1,0:T(8,128)(2,1)}, u32[]{:S(2)}) copy-start(bf16[1024,3072]{1,0:T(8,128)(2,1)} %w_hbm.1) | copy-start | bytes 18874372
  21.0 7.1 %copy-start = (bf16[1024,1024]{1,0:T(8,128)(2,1)S(1)}, bf16[1024,1024]{1,0:T(8,128)(2,1)}, u32[]{:S(2)}) copy-start(bf16[1024,1024]{1,0:T(8,128)(2,1)} %w_out.3) | copy-start | bytes 6291460
  21.0 7.1 %copy-start.2 = (bf16[1024,768]{1,0:T(8,128)(2,1)S(1)}, bf16[1024,768]{1,0:T(8,128)(2,1)}, u32[]{:S(2)}) copy-start(bf16[1024,768]{1,0:T(8,128)(2,1)} %w_emb.3) | copy-start | bytes 4718596
  28.2 16.6 %copy-start.4 = (bf16[2,768]{1,0:T(2,128)(2,1)S(1)}, bf16[2,768]{1,0:T(2,128)(2,1)}, u32[]{:S(2)}) copy-start(bf16[2,768]{1,0:T(2,128)(2,1)} %text.1) | copy-start | bytes 9220
  28.2 16.6 %copy-start.5 = (s32[2,16]{1,0:T(2,128)S(1)}, s32[2,16]{1,0:T(2,128)}, u32[]{:S(2)}) copy-start(s32[2,16]{1,0:T(2,128)} %bucket.1) | copy-start | bytes 388
  28.2 16.5 %copy-start.6 = (f32[4]{0:T(128)S(1)}, f32[4]{0:T(128)}, u32[]{:S(2)}) copy-start(f32[4]{0:T(128)} %levels.1) | copy-start | bytes 52
  67.9 12.5 %collective-permute-start.11 = (bf16[2,2,16,1024]{3,2,1,0:T(8,128)(2,1)S(1)}, bf16[2,2,16,1024]{3,2,1,0:T(8,128)(2,1)S(1)}, u32[]{:S(2)}, u32[]{:S(2)}) collective-permute-start(bf16[2,2,16,1024]{3,2,1,0:T(8,128)(2,1)S(1)} %get-tuple-element.58), channel_id=1, source_target_pairs={{0,5},{1,6},{2,7},{3,4},{4,9},{5,10},{6,11},{7,8},{8,13},{9,14},{1... | collective-permute-start | bytes 393224 | tf_op jit(solution)/shard_map/ppermute | solution.py:116
  71.2 10.9 %collective-permute-start.9 = (bf16[2,3,16,1024]{3,2,1,0:T(8,128)(2,1)S(1)}, bf16[2,3,16,1024]{3,2,1,0:T(8,128)(2,1)S(1)}, u32[]{:S(2)}, u32[]{:S(2)}) collective-permute-start(bf16[2,3,16,1024]{3,2,1,0:T(8,128)(2,1)S(1)} %get-tuple-element.56), channel_id=1, source_target_pairs={{0,4},{1,5},{2,6},{3,7},{4,8},{5,9},{6,10},{7,11},{8,12},{9,13},{1... | collective-permute-start | bytes 589832 | tf_op jit(solution)/shard_map/ppermute | solution.py:116
  71.2 10.9 %collective-permute-start.10 = (bf16[3,2,16,1024]{3,2,1,0:T(8,128)(2,1)S(1)}, bf16[3,2,16,1024]{3,2,1,0:T(8,128)(2,1)S(1)}, u32[]{:S(2)}, u32[]{:S(2)}) collective-permute-start(bf16[3,2,16,1024]{3,2,1,0:T(8,128)(2,1)S(1)} %get-tuple-element.57), channel_id=1, source_target_pairs={{0,1},{1,2},{2,3},{3,0},{4,5},{5,6},{6,7},{7,4},{8,9},{9,10},{10,1... | collective-permute-start | bytes 589832 | tf_op jit(solution)/shard_map/ppermute | solution.py:116
  77.5 9.2 %collective-permute-start.6 = (bf16[2,3,16,1024]{3,2,1,0:T(8,128)(2,1)S(1)}, bf16[2,3,16,1024]{3,2,1,0:T(8,128)(2,1)S(1)}, u32[]{:S(2)}, u32[]{:S(2)}) collective-permute-start(bf16[2,3,16,1024]{3,2,1,0:T(8,128)(2,1)S(1)} %get-tuple-element.52), channel_id=1, source_target_pairs={{0,28},{1,29},{2,30},{3,31},{4,0},{5,1},{6,2},{7,3},{8,4},{9,5},{1... | collective-permute-start | bytes 589832 | tf_op jit(solution)/shard_map/ppermute | solution.py:116
  79.6 9.7 %collective-permute-start.7 = (bf16[3,2,16,1024]{3,2,1,0:T(8,128)(2,1)S(1)}, bf16[3,2,16,1024]{3,2,1,0:T(8,128)(2,1)S(1)}, u32[]{:S(2)}, u32[]{:S(2)}) collective-permute-start(bf16[3,2,16,1024]{3,2,1,0:T(8,128)(2,1)S(1)} %get-tuple-element.53), channel_id=1, source_target_pairs={{0,3},{1,0},{2,1},{3,2},{4,7},{5,4},{6,5},{7,6},{8,11},{9,8},{10,9... | collective-permute-start | bytes 589832 | tf_op jit(solution)/shard_map/ppermute | solution.py:116
  80.4 6.3 %collective-permute-start.8 = (bf16[2,2,16,1024]{3,2,1,0:T(8,128)(2,1)S(1)}, bf16[2,2,16,1024]{3,2,1,0:T(8,128)(2,1)S(1)}, u32[]{:S(2)}, u32[]{:S(2)}) collective-permute-start(bf16[2,2,16,1024]{3,2,1,0:T(8,128)(2,1)S(1)} %get-tuple-element.54), channel_id=1, source_target_pairs={{0,31},{1,28},{2,29},{3,30},{4,3},{5,0},{6,1},{7,2},{8,7},{9,4},{1... | collective-permute-start | bytes 393224 | tf_op jit(solution)/shard_map/ppermute | solution.py:116

commit v6 on v5

--- a/solution.py
+++ b/solution.py
@@ -391,7 +391,50 @@
     return got[:n] + got[n : 2 * n] + got[2 * n :]
 
 
-def contrast_kernel(got, w_emb, w_out, text_grad, loss, clip_grad, d_out):
+def own_rows(first_clip, array):
+    row = lax.broadcasted_iota(jnp.int32, (array.shape[0], 1), 0)
+    return jnp.concatenate(
+        [
+            jnp.sum(jnp.where(row == first_clip + c, array, 0.0), axis=0, keepdims=True)
+            for c in range(2)
+        ],
+        axis=0,
+    )
+
+
+def caption_kernel(after, got, grad, clip_unit, out):
+    peers = got.shape[0]
+    words = jnp.concatenate([got[p, 2:4, :EMB] for p in range(peers)], axis=0)
+    text_norm = jnp.sqrt(jnp.sum(words * words, axis=-1, keepdims=True) + EMBED_EPS)
+    text_unit = words / text_norm
+    d_text = (
+        lax.dot_general(
+            grad[...],
+            clip_unit[...],
+            TN,
+            precision=lax.Precision.HIGHEST,
+            preferred_element_type=F32,
+        )
+        / SOFTMAX_TEMP
+    )
+    text_all = (
+        d_text - text_unit * jnp.sum(text_unit * d_text, axis=-1, keepdims=True)
+    ) / text_norm
+    out[...] = own_rows(2 * lax.axis_index("batch"), text_all)
+
+
+def caption(after, got, grad, clip_unit):
+    return pl.pallas_call(
+        caption_kernel,
+        out_shape=jax.ShapeDtypeStruct((2, EMB), F32),
+        in_specs=[pl.BlockSpec(memory_space=pl.ANY)] + [vmem()] * 3,
+        out_specs=vmem(),
+        compiler_params=params(4),
+        name="caption",
+    )(after, got, grad, clip_unit)
+
+
+def contrast_kernel(got, w_emb, w_out, loss, clip_grad, d_out, grad_out, clip_out):
     peers = got.shape[0]
     n = 2 * peers
     first_clip = 2 * lax.axis_index("batch")
@@ -435,46 +478,30 @@
     d_clip = (
         jnp.dot(grad, text_unit, precision=exact, preferred_element_type=F32) / SOFTMAX_TEMP
     )
-    d_text = (
-        lax.dot_general(grad, clip_unit, TN, precision=exact, preferred_element_type=F32)
-        / SOFTMAX_TEMP
-    )
-    text_all = (
-        d_text - text_unit * jnp.sum(text_unit * d_text, axis=-1, keepdims=True)
-    ) / text_norm
+    grad_out[...] = grad
+    clip_out[...] = clip_unit
     embed_all = (
         d_clip - clip_unit * jnp.sum(clip_unit * d_clip, axis=-1, keepdims=True)
     ) / clip_norm
-    row = lax.broadcasted_iota(jnp.int32, (n, 1), 0)
-
-    def mine(array):
-        return jnp.concatenate(
-            [
-                jnp.sum(
-                    jnp.where(row == first_clip + c, array, 0.0), axis=0, keepdims=True
-                )
-                for c in range(2)
-            ],
-            axis=0,
-        )
-
-    text_grad[...] = mine(text_all)
+    mine = partial(own_rows, first_clip)
     pooled_grad = full_dot(mine(embed_all), w_emb[...], NT)
     clip_grad[...] = pooled_grad
     d_out[...] = full_dot(pooled_grad, w_out[...], NT)
 
 
 def contrast(got, w_emb, w_out):
+    n = 2 * got.shape[0]
     return pl.pallas_call(
         contrast_kernel,
         out_shape=[
-            jax.ShapeDtypeStruct((2, EMB), F32),
             jax.ShapeDtypeStruct((1, 1), F32),
             jax.ShapeDtypeStruct((2, D), F32),
             jax.ShapeDtypeStruct((2, D), F32),
+            jax.ShapeDtypeStruct((n, n), F32),
+            jax.ShapeDtypeStruct((n, EMB), F32),
         ],
         in_specs=[vmem()] * 3,
-        out_specs=[vmem()] * 4,
+        out_specs=[vmem()] * 5,
         compiler_params=params(4),
         name="contrast",
     )(got, w_emb, w_out)
@@ -703,11 +730,12 @@
     got = lax.all_to_all(spread, ("tm", "space"), 0, 0)
     packed = embed(got, text, bucket, bucket_scale, peers)
     got = lax.all_to_all(packed, "batch", 0, 0)
-    text_grad, loss, clip_grad, d_out = contrast(got, w_emb, w_out)
+    loss, clip_grad, d_out, grad, clip_unit = contrast(got, w_emb, w_out)
     parts = []
     for c in range(2):
         mine, *pieces = backward((c,), small, clip_grad, d_out, stored, w_qkv)
         parts.append((mine, exchange(pieces, c, 1)))
+    text_grad = caption(parts[0][1][0], got, grad, clip_unit)
     video_grad = merge(0, small, *parts[0])
     video_grad = merge(1, small, *parts[1], video_grad)
     return (video_grad, text_grad, loss[0, 0])

time: 91 us -> 91.4 us (level)
  waiting for transfers between devices: 7.93 us -> 6.87 us
    ppermute x12, waiting for transfers between devices: 7.93 us -> 6.87 us  [exchange(): out.append(lax.ppermute(piece, ('tm', 'space'), pairs))]
    pallas_call x1 -> x2, Pallas kernels: 2.18 us -> 2.76 us  [the longest x1 1.82 us: contrast(): pl.pallas_call(contrast_kernel, out_shape=[jax.ShapeDtypeStruct((1, 1), F...]
  transfers between devices with their start and end apart: 12 -> 12, of which waited for: 3 -> 3; matrix products, arithmetic and copies ran while one was open for 1% -> 1% of each run, Pallas kernels for 7% -> 8%
where the time goes in v6:
time: 91.4 us; the launch traced here: 91.1 us
  blocking collectives  31.4 us (34%)
  Pallas kernels  24.2 us (26%)
  starting transfers between devices  22.6 us (25%)
  waiting for transfers between devices  6.87 us (8%)
  local copies, waits for them, and re-layouts  4.03 us (4%)
  other arithmetic  1.34 us (1%)
    ppermute x12, starting transfers between devices, exchange(): out.append(lax.ppermute(piece, ('tm', 'space'), pairs))  22.6 us
    all_to_all x1, blocking collectives, local(): got = lax.all_to_all(spread, ('tm', 'space'), 0, 0)  15.8 us
    all_to_all x1, blocking collectives, local(): got = lax.all_to_all(packed, 'batch', 0, 0)  15.6 us
    pallas_call x2, Pallas kernels, backward(): pl.pallas_call(partial(backward_kernel, clips), out_shape=[jax.ShapeDtype...  9.5 us
    pallas_call x1, Pallas kernels, forward(): pl.pallas_call(partial(forward_kernel, clips, frames, rows_all), out_shap...  7.08 us
    ppermute x12, waiting for transfers between devices, exchange(): out.append(lax.ppermute(piece, ('tm', 'space'), pairs))  6.87 us
    unnamed x14, local copies, waits for them, and re-layouts  4.03 us
    pallas_call x2, Pallas kernels, merge(): pl.pallas_call(partial(merge_kernel, clip), grid=(1,), out_shape=jax.Shap...  2.87 us
  transfers between devices with their start and end apart: 12, of which 3 were waited for; matrix products, arithmetic and copies ran while one was open for 1% of the time, Pallas kernels for 8%

profile of v6, /device:TPU:1, one launch (start us, length us, event | category | flops | bytes accessed | tf_op | source)
XLA Modules:
  0.0 91.1 jit_solution(9939942263325930657)
XLA Ops:
  0.6 1.2 %copy-done.3 = bf16[2,4,4,16,1024]{4,3,2,1,0:T(8,128)(2,1)S(1)} copy-done((bf16[2,4,4,16,1024]{4,3,2,1,0:T(8,128)(2,1)S(1)}, bf16[2,4,4,16,1024]{4,3,2,1,0:T(8,128)(2,1)}, u32[]{:S(2)}) %copy-start.3) | copy-done | bytes 1048600
  1.9 0.1 pack.1
  2.0 4.4 %collective-permute-start = (bf16[2,3,16,1024]{3,2,1,0:T(8,128)(2,1)S(1)}, bf16[2,3,16,1024]{3,2,1,0:T(8,128)(2,1)S(1)}, u32[]{:S(2)}, u32[]{:S(2)}) collective-permute-start(bf16[2,3,16,1024]{3,2,1,0:T(8,128)(2,1)S(1)} %get-tuple-element.34), channel_id=1, source_target_pairs={{0,28},{1,29},{2,30},{3,31},{4,0},{5,1},{6,2},{7,3},{8,4},{9,5},{1... | collective-permute-start | bytes 589832 | tf_op jit(solution)/shard_map/ppermute | solution.py:116
  6.4 1.0 %collective-permute-start.1 = (bf16[3,2,16,1024]{3,2,1,0:T(8,128)(2,1)S(1)}, bf16[3,2,16,1024]{3,2,1,0:T(8,128)(2,1)S(1)}, u32[]{:S(2)}, u32[]{:S(2)}) collective-permute-start(bf16[3,2,16,1024]{3,2,1,0:T(8,128)(2,1)S(1)} %get-tuple-element.35), channel_id=1, source_target_pairs={{0,3},{1,0},{2,1},{3,2},{4,7},{5,4},{6,5},{7,6},{8,11},{9,8},{10,9... | collective-permute-start | bytes 589832 | tf_op jit(solution)/shard_map/ppermute | solution.py:116
  7.4 2.5 %collective-permute-start.4 = (bf16[3,2,16,1024]{3,2,1,0:T(8,128)(2,1)S(1)}, bf16[3,2,16,1024]{3,2,1,0:T(8,128)(2,1)S(1)}, u32[]{:S(2)}, u32[]{:S(2)}) collective-permute-start(bf16[3,2,16,1024]{3,2,1,0:T(8,128)(2,1)S(1)} %get-tuple-element.38), channel_id=1, source_target_pairs={{0,1},{1,2},{2,3},{3,0},{4,5},{5,6},{6,7},{7,4},{8,9},{9,10},{10,1... | collective-permute-start | bytes 589832 | tf_op jit(solution)/shard_map/ppermute | solution.py:116
  9.9 3.3 %collective-permute-start.2 = (bf16[2,2,16,1024]{3,2,1,0:T(8,128)(2,1)S(1)}, bf16[2,2,16,1024]{3,2,1,0:T(8,128)(2,1)S(1)}, u32[]{:S(2)}, u32[]{:S(2)}) collective-permute-start(bf16[2,2,16,1024]{3,2,1,0:T(8,128)(2,1)S(1)} %get-tuple-element.36), channel_id=1, source_target_pairs={{0,31},{1,28},{2,29},{3,30},{4,3},{5,0},{6,1},{7,2},{8,7},{9,4},{1... | collective-permute-start | bytes 393224 | tf_op jit(solution)/shard_map/ppermute | solution.py:116
  13.2 1.1 %collective-permute-start.5 = (bf16[2,2,16,1024]{3,2,1,0:T(8,128)(2,1)S(1)}, bf16[2,2,16,1024]{3,2,1,0:T(8,128)(2,1)S(1)}, u32[]{:S(2)}, u32[]{:S(2)}) collective-permute-start(bf16[2,2,16,1024]{3,2,1,0:T(8,128)(2,1)S(1)} %get-tuple-element.39), channel_id=1, source_target_pairs={{0,5},{1,6},{2,7},{3,4},{4,9},{5,10},{6,11},{7,8},{8,13},{9,14},{1... | collective-permute-start | bytes 393224 | tf_op jit(solution)/shard_map/ppermute | solution.py:116
  14.3 0.7 convert_element_type.5
  14.9 0.7 select_maximum_fusion.small
  15.6 2.8 %copy-done.1 = bf16[1024,3072]{1,0:T(8,128)(2,1)S(1)} copy-done((bf16[1024,3072]{1,0:T(8,128)(2,1)S(1)}, bf16[1024,3072]{1,0:T(8,128)(2,1)}, u32[]{:S(2)}) %copy-start.1) | copy-done | bytes 6291480
  18.4 0.4 load.1.refs_6_.refs_9_
  18.8 2.2 %collective-permute-done.5.refs_5_ = bf16[2,2,16,1024]{3,2,1,0:T(8,128)(2,1)S(1)} collective-permute-done((bf16[2,2,16,1024]{3,2,1,0:T(8,128)(2,1)S(1)}, bf16[2,2,16,1024]{3,2,1,0:T(8,128)(2,1)S(1)}, u32[]{:S(2)}, u32[]{:S(2)}) %collective-permute-start.5) | collective-permute-done | bytes 131104 | tf_op jit(solution)/shard_map/ppermute | solution.py:116
  21.1 7.1 %forward.1 = (bf16[512,1024]{1,0:T(8,128)(2,1)S(1)}, bf16[512,1024]{1,0:T(8,128)(2,1)S(1)}, bf16[512,1024]{1,0:T(8,128)(2,1)S(1)}, f32[512,1024]{1,0:T(8,128)S(1...) custom-call(f32[3,16]{1,0:T(4,128)S(1)} %select_maximum_fusion.small, ...), custom_call_target="tpu_custom_call" | custom-call | flops 3221225472 | bytes 12582912 | tf_op jit(solution)/shard_map/forward/pallas_call | solution.py:297
  28.2 0.0 copy-start.5
  28.2 0.0 copy-start.6
  28.2 0.7 share.1
  28.9 15.8 %all_to_all.10.got = f32[32,2,768]{2,1,0:T(2,128)S(1)} all-to-all(f32[32,2,768]{2,1,0:T(2,128)S(1)} %share.1), channel_id=1, replica_groups=mesh['batch'=8,'tm'=8,'space'=4] {'tm','space'}, dimensions={0} | all-to-all | bytes 393216 | tf_op jit(solution)/shard_map/all_to_all | solution.py:730
  44.7 0.6 embed.1
  45.4 15.6 %all_to_all.11.got = f32[8,4,896]{2,1,0:T(4,128)S(1)} all-to-all(f32[8,4,896]{2,1,0:T(4,128)S(1)} %embed.1), channel_id=1, replica_groups=mesh['batch'=8,'tm'=8,'space'=4] {'batch'}, dimensions={0} | all-to-all | bytes 229376 | tf_op jit(solution)/shard_map/all_to_all | solution.py:732
  61.0 1.8 %contrast.1 = (f32[1,1]{1,0:T(1,128)}, f32[2,1024]{1,0:T(2,128)S(1)}, f32[2,1024]{1,0:T(2,128)S(1)}, f32[16,16]{1,0:T(8,128)S(1)}, f32[16,768]{1,0:T(8,128)S(1)}) custom-call(f32[8,4,896]{2,1,0:T(4,128)S(1)} %all_to_all.11.got, bf16[1024,768]{1,0:T(8,128)(2,1)S(1)} %copy-done.2, bf16[1024,1024]{1,0:T(8,128)(2,1)S(1)} %copy-done), custom_call_target="tpu_custom_call" | custom-call | tf_op jit(solution)/shard_map/contrast/pallas_call | solution.py:494
  62.8 4.8 %backward.3 = (bf16[4,4,16,1024]{3,2,1,0:T(8,128)(2,1)S(1)}, bf16[2,3,16,1024]{3,2,1,0:T(8,128)(2,1)S(1)}, bf16[3,2,16,1024]{3,2,1,0:T(8,128)(2,1)S(1)}, bf16[2,2,16,1024]{3,2,1,0:T(8,128)(2,1)S(1)}) custom-call(f32[3,16]{1,0:T(4,128)S(1)} %select_maximum_fusion.small, f32[2,1024]{1,0:T(2,128)S(1)} %get-tuple-element.41.clip_grad, ...), custom_call_target="tpu_custom_call" | custom-call | flops 1610612736 | bytes 16777216 | tf_op jit(solution)/shard_map/backward/pallas_call | solution.py:658
  67.6 0.5 collective-permute-start.9
  68.1 4.3 %collective-permute-start.10 = (bf16[3,2,16,1024]{3,2,1,0:T(8,128)(2,1)S(1)}, bf16[3,2,16,1024]{3,2,1,0:T(8,128)(2,1)S(1)}, u32[]{:S(2)}, u32[]{:S(2)}) collective-permute-start(bf16[3,2,16,1024]{3,2,1,0:T(8,128)(2,1)S(1)} %get-tuple-element.58), channel_id=1, source_target_pairs={{0,1},{1,2},{2,3},{3,0},{4,5},{5,6},{6,7},{7,4},{8,9},{9,10},{10,1... | collective-permute-start | bytes 589832 | tf_op jit(solution)/shard_map/ppermute | solution.py:116
  72.3 4.7 %backward.2 = (bf16[4,4,16,1024]{3,2,1,0:T(8,128)(2,1)S(1)}, bf16[2,3,16,1024]{3,2,1,0:T(8,128)(2,1)S(1)}, bf16[3,2,16,1024]{3,2,1,0:T(8,128)(2,1)S(1)}, bf16[2,2,16,1024]{3,2,1,0:T(8,128)(2,1)S(1)}) custom-call(f32[3,16]{1,0:T(4,128)S(1)} %select_maximum_fusion.small, f32[2,1024]{1,0:T(2,128)S(1)} %get-tuple-element.41.clip_grad, ...), custom_call_target="tpu_custom_call" | custom-call | flops 1610612736 | bytes 16777216 | tf_op jit(solution)/shard_map/backward/pallas_call | solution.py:658
  77.1 1.7 %collective-permute-start.6 = (bf16[2,3,16,1024]{3,2,1,0:T(8,128)(2,1)S(1)}, bf16[2,3,16,1024]{3,2,1,0:T(8,128)(2,1)S(1)}, u32[]{:S(2)}, u32[]{:S(2)}) collective-permute-start(bf16[2,3,16,1024]{3,2,1,0:T(8,128)(2,1)S(1)} %get-tuple-element.53), channel_id=1, source_target_pairs={{0,28},{1,29},{2,30},{3,31},{4,0},{5,1},{6,2},{7,3},{8,4},{9,5},{1... | collective-permute-start | bytes 589832 | tf_op jit(solution)/shard_map/ppermute | solution.py:116
  78.8 2.5 %collective-permute-start.11 = (bf16[2,2,16,1024]{3,2,1,0:T(8,128)(2,1)S(1)}, bf16[2,2,16,1024]{3,2,1,0:T(8,128)(2,1)S(1)}, u32[]{:S(2)}, u32[]{:S(2)}) collective-permute-start(bf16[2,2,16,1024]{3,2,1,0:T(8,128)(2,1)S(1)} %get-tuple-element.59), channel_id=1, source_target_pairs={{0,5},{1,6},{2,7},{3,4},{4,9},{5,10},{6,11},{7,8},{8,13},{9,14},{1... | collective-permute-start | bytes 393224 | tf_op jit(solution)/shard_map/ppermute | solution.py:116
  81.3 1.3 %collective-permute-start.8 = (bf16[2,2,16,1024]{3,2,1,0:T(8,128)(2,1)S(1)}, bf16[2,2,16,1024]{3,2,1,0:T(8,128)(2,1)S(1)}, u32[]{:S(2)}, u32[]{:S(2)}) collective-permute-start(bf16[2,2,16,1024]{3,2,1,0:T(8,128)(2,1)S(1)} %get-tuple-element.55), channel_id=1, source_target_pairs={{0,31},{1,28},{2,29},{3,30},{4,3},{5,0},{6,1},{7,2},{8,7},{9,4},{1... | collective-permute-start | bytes 393224 | tf_op jit(solution)/shard_map/ppermute | solution.py:116
  82.6 0.9 %caption.1 = f32[2,768]{1,0:T(2,128)} custom-call(bf16[2,3,16,1024]{3,2,1,0:T(8,128)(2,1)S(1)} %collective-permute-done.9.a.after, f32[8,4,896]{2,1,0:T(4,128)S(1)} %all_to_all.11.got, f32[16,16]{1,0:T(8,128)S(1)} %get-tuple-element.60.grad, f32[16,768]{1,0:T(8,128)S(1)} %get-tuple-element.61.clip_unit), custom_call_target="tpu_custom_call" | custom-call | tf_op jit(solution)/shard_map/caption/pallas_call | solution.py:427
  83.6 2.2 %collective-permute-done.11.corner = bf16[2,2,16,1024]{3,2,1,0:T(8,128)(2,1)S(1)} collective-permute-done((bf16[2,2,16,1024]{3,2,1,0:T(8,128)(2,1)S(1)}, bf16[2,2,16,1024]{3,2,1,0:T(8,128)(2,1)S(1)}, u32[]{:S(2)}, u32[]{:S(2)}) %collective-permute-start.11) | collective-permute-done | bytes 131104 | tf_op jit(solution)/shard_map/ppermute | solution.py:116
  85.8 1.4 %merge.2.refs_0_ = bf16[2,4,4,16,1024]{4,3,2,1,0:T(8,128)(2,1)} custom-call(f32[3,16]{1,0:T(4,128)S(1)} %select_maximum_fusion.small, bf16[4,4,16,1024]{3,2,1,0:T(8,128)(2,1)S(1)} %get-tuple-element.56.own, bf16[2,3,16,1024]{3,2,1,0:T(8,128)(2,1)S(1)} %collective-permute-done.9.a.after, bf16[3,2,16,1024]{3,2,1,0:T(8,128)(2,1)S(1)} %collective-permute-done.10.b, ...), custom_call_target="tpu_custom_call" | custom-call | tf_op jit(solution)/shard_map/merge/pallas_call | solution.py:708
  87.2 2.4 %collective-permute-done.8.corner = bf16[2,2,16,1024]{3,2,1,0:T(8,128)(2,1)S(1)} collective-permute-done((bf16[2,2,16,1024]{3,2,1,0:T(8,128)(2,1)S(1)}, bf16[2,2,16,1024]{3,2,1,0:T(8,128)(2,1)S(1)}, u32[]{:S(2)}, u32[]{:S(2)}) %collective-permute-start.8) | collective-permute-done | bytes 131104 | tf_op jit(solution)/shard_map/ppermute | solution.py:116
  89.7 1.4 %merge.3 = bf16[2,4,4,16,1024]{4,3,2,1,0:T(8,128)(2,1)} custom-call(f32[3,16]{1,0:T(4,128)S(1)} %select_maximum_fusion.small, bf16[4,4,16,1024]{3,2,1,0:T(8,128)(2,1)S(1)} %get-tuple-element.52.own, bf16[2,3,16,1024]{3,2,1,0:T(8,128)(2,1)S(1)} %collective-permute-done.6.a, ...), custom_call_target="tpu_custom_call", output_to_operand_aliasing={{}: (5, {})} | custom-call | tf_op jit(solution)/shard_map/merge/pallas_call | solution.py:708
  (21 shorter events, 0.1 us)
Async XLA Ops:
  0.6 1.2 %copy-start.3 = (bf16[2,4,4,16,1024]{4,3,2,1,0:T(8,128)(2,1)S(1)}, bf16[2,4,4,16,1024]{4,3,2,1,0:T(8,128)(2,1)}, u32[]{:S(2)}) copy-start(bf16[2,4,4,16,1024]{4,3,2,1,0:T(8,128)(2,1)} %video.1) | copy-start | bytes 3145732
  2.0 11.2 %collective-permute-start = (bf16[2,3,16,1024]{3,2,1,0:T(8,128)(2,1)S(1)}, bf16[2,3,16,1024]{3,2,1,0:T(8,128)(2,1)S(1)}, u32[]{:S(2)}, u32[]{:S(2)}) collective-permute-start(bf16[2,3,16,1024]{3,2,1,0:T(8,128)(2,1)S(1)} %get-tuple-element.34), channel_id=1, source_target_pairs={{0,28},{1,29},{2,30},{3,31},{4,0},{5,1},{6,2},{7,3},{8,4},{9,5},{1... | collective-permute-start | bytes 589832 | tf_op jit(solution)/shard_map/ppermute | solution.py:116
  6.4 14.6 %collective-permute-start.1 = (bf16[3,2,16,1024]{3,2,1,0:T(8,128)(2,1)S(1)}, bf16[3,2,16,1024]{3,2,1,0:T(8,128)(2,1)S(1)}, u32[]{:S(2)}, u32[]{:S(2)}) collective-permute-start(bf16[3,2,16,1024]{3,2,1,0:T(8,128)(2,1)S(1)} %get-tuple-element.35), channel_id=1, source_target_pairs={{0,3},{1,0},{2,1},{3,2},{4,7},{5,4},{6,5},{7,6},{8,11},{9,8},{10,9... | collective-permute-start | bytes 589832 | tf_op jit(solution)/shard_map/ppermute | solution.py:116
  7.3 13.7 %collective-permute-start.3 = (bf16[2,3,16,1024]{3,2,1,0:T(8,128)(2,1)S(1)}, bf16[2,3,16,1024]{3,2,1,0:T(8,128)(2,1)S(1)}, u32[]{:S(2)}, u32[]{:S(2)}) collective-permute-start(bf16[2,3,16,1024]{3,2,1,0:T(8,128)(2,1)S(1)} %get-tuple-element.37), channel_id=1, source_target_pairs={{0,4},{1,5},{2,6},{3,7},{4,8},{5,9},{6,10},{7,11},{8,12},{9,13},{1... | collective-permute-start | bytes 589832 | tf_op jit(solution)/shard_map/ppermute | solution.py:116
  7.4 13.7 %collective-permute-start.4 = (bf16[3,2,16,1024]{3,2,1,0:T(8,128)(2,1)S(1)}, bf16[3,2,16,1024]{3,2,1,0:T(8,128)(2,1)S(1)}, u32[]{:S(2)}, u32[]{:S(2)}) collective-permute-start(bf16[3,2,16,1024]{3,2,1,0:T(8,128)(2,1)S(1)} %get-tuple-element.38), channel_id=1, source_target_pairs={{0,1},{1,2},{2,3},{3,0},{4,5},{5,6},{6,7},{7,4},{8,9},{9,10},{10,1... | collective-permute-start | bytes 589832 | tf_op jit(solution)/shard_map/ppermute | solution.py:116
  9.9 9.0 %collective-permute-start.2 = (bf16[2,2,16,1024]{3,2,1,0:T(8,128)(2,1)S(1)}, bf16[2,2,16,1024]{3,2,1,0:T(8,128)(2,1)S(1)}, u32[]{:S(2)}, u32[]{:S(2)}) collective-permute-start(bf16[2,2,16,1024]{3,2,1,0:T(8,128)(2,1)S(1)} %get-tuple-element.36), channel_id=1, source_target_pairs={{0,31},{1,28},{2,29},{3,30},{4,3},{5,0},{6,1},{7,2},{8,7},{9,4},{1... | collective-permute-start | bytes 393224 | tf_op jit(solution)/shard_map/ppermute | solution.py:116
  13.2 7.9 %collective-permute-start.5 = (bf16[2,2,16,1024]{3,2,1,0:T(8,128)(2,1)S(1)}, bf16[2,2,16,1024]{3,2,1,0:T(8,128)(2,1)S(1)}, u32[]{:S(2)}, u32[]{:S(2)}) collective-permute-start(bf16[2,2,16,1024]{3,2,1,0:T(8,128)(2,1)S(1)} %get-tuple-element.39), channel_id=1, source_target_pairs={{0,5},{1,6},{2,7},{3,4},{4,9},{5,10},{6,11},{7,8},{8,13},{9,14},{1... | collective-permute-start | bytes 393224 | tf_op jit(solution)/shard_map/ppermute | solution.py:116
  15.6 2.8 %copy-start.1 = (bf16[1024,3072]{1,0:T(8,128)(2,1)S(1)}, bf16[1024,3072]{1,0:T(8,128)(2,1)}, u32[]{:S(2)}) copy-start(bf16[1024,3072]{1,0:T(8,128)(2,1)} %w_hbm.1) | copy-start | bytes 18874372
  21.0 7.1 %copy-start = (bf16[1024,1024]{1,0:T(8,128)(2,1)S(1)}, bf16[1024,1024]{1,0:T(8,128)(2,1)}, u32[]{:S(2)}) copy-start(bf16[1024,1024]{1,0:T(8,128)(2,1)} %w_out.3) | copy-start | bytes 6291460
  21.0 7.1 %copy-start.2 = (bf16[1024,768]{1,0:T(8,128)(2,1)S(1)}, bf16[1024,768]{1,0:T(8,128)(2,1)}, u32[]{:S(2)}) copy-start(bf16[1024,768]{1,0:T(8,128)(2,1)} %w_emb.3) | copy-start | bytes 4718596
  28.2 16.6 %copy-start.4 = (bf16[2,768]{1,0:T(2,128)(2,1)S(1)}, bf16[2,768]{1,0:T(2,128)(2,1)}, u32[]{:S(2)}) copy-start(bf16[2,768]{1,0:T(2,128)(2,1)} %text.1) | copy-start | bytes 9220
  28.2 16.6 %copy-start.5 = (s32[2,16]{1,0:T(2,128)S(1)}, s32[2,16]{1,0:T(2,128)}, u32[]{:S(2)}) copy-start(s32[2,16]{1,0:T(2,128)} %bucket.1) | copy-start | bytes 388
  28.2 16.5 %copy-start.6 = (f32[4]{0:T(128)S(1)}, f32[4]{0:T(128)}, u32[]{:S(2)}) copy-start(f32[4]{0:T(128)} %levels.1) | copy-start | bytes 52
  67.6 13.7 %collective-permute-start.9 = (bf16[2,3,16,1024]{3,2,1,0:T(8,128)(2,1)S(1)}, bf16[2,3,16,1024]{3,2,1,0:T(8,128)(2,1)S(1)}, u32[]{:S(2)}, u32[]{:S(2)}) collective-permute-start(bf16[2,3,16,1024]{3,2,1,0:T(8,128)(2,1)S(1)} %get-tuple-element.57), channel_id=1, source_target_pairs={{0,4},{1,5},{2,6},{3,7},{4,8},{5,9},{6,10},{7,11},{8,12},{9,13},{1... | collective-permute-start | bytes 589832 | tf_op jit(solution)/shard_map/ppermute | solution.py:116
  68.1 17.7 %collective-permute-start.10 = (bf16[3,2,16,1024]{3,2,1,0:T(8,128)(2,1)S(1)}, bf16[3,2,16,1024]{3,2,1,0:T(8,128)(2,1)S(1)}, u32[]{:S(2)}, u32[]{:S(2)}) collective-permute-start(bf16[3,2,16,1024]{3,2,1,0:T(8,128)(2,1)S(1)} %get-tuple-element.58), channel_id=1, source_target_pairs={{0,1},{1,2},{2,3},{3,0},{4,5},{5,6},{6,7},{7,4},{8,9},{9,10},{10,1... | collective-permute-start | bytes 589832 | tf_op jit(solution)/shard_map/ppermute | solution.py:116
  77.1 12.6 %collective-permute-start.6 = (bf16[2,3,16,1024]{3,2,1,0:T(8,128)(2,1)S(1)}, bf16[2,3,16,1024]{3,2,1,0:T(8,128)(2,1)S(1)}, u32[]{:S(2)}, u32[]{:S(2)}) collective-permute-start(bf16[2,3,16,1024]{3,2,1,0:T(8,128)(2,1)S(1)} %get-tuple-element.53), channel_id=1, source_target_pairs={{0,28},{1,29},{2,30},{3,31},{4,0},{5,1},{6,2},{7,3},{8,4},{9,5},{1... | collective-permute-start | bytes 589832 | tf_op jit(solution)/shard_map/ppermute | solution.py:116
  78.8 10.9 %collective-permute-start.7 = (bf16[3,2,16,1024]{3,2,1,0:T(8,128)(2,1)S(1)}, bf16[3,2,16,1024]{3,2,1,0:T(8,128)(2,1)S(1)}, u32[]{:S(2)}, u32[]{:S(2)}) collective-permute-start(bf16[3,2,16,1024]{3,2,1,0:T(8,128)(2,1)S(1)} %get-tuple-element.54), channel_id=1, source_target_pairs={{0,3},{1,0},{2,1},{3,2},{4,7},{5,4},{6,5},{7,6},{8,11},{9,8},{10,9... | collective-permute-start | bytes 589832 | tf_op jit(solution)/shard_map/ppermute | solution.py:116
  78.8 7.0 %collective-permute-start.11 = (bf16[2,2,16,1024]{3,2,1,0:T(8,128)(2,1)S(1)}, bf16[2,2,16,1024]{3,2,1,0:T(8,128)(2,1)S(1)}, u32[]{:S(2)}, u32[]{:S(2)}) collective-permute-start(bf16[2,2,16,1024]{3,2,1,0:T(8,128)(2,1)S(1)} %get-tuple-element.59), channel_id=1, source_target_pairs={{0,5},{1,6},{2,7},{3,4},{4,9},{5,10},{6,11},{7,8},{8,13},{9,14},{1... | collective-permute-start | bytes 393224 | tf_op jit(solution)/shard_map/ppermute | solution.py:116
  81.3 8.4 %collective-permute-start.8 = (bf16[2,2,16,1024]{3,2,1,0:T(8,128)(2,1)S(1)}, bf16[2,2,16,1024]{3,2,1,0:T(8,128)(2,1)S(1)}, u32[]{:S(2)}, u32[]{:S(2)}) collective-permute-start(bf16[2,2,16,1024]{3,2,1,0:T(8,128)(2,1)S(1)} %get-tuple-element.55), channel_id=1, source_target_pairs={{0,31},{1,28},{2,29},{3,30},{4,3},{5,0},{6,1},{7,2},{8,7},{9,4},{1... | collective-permute-start | bytes 393224 | tf_op jit(solution)/shard_map/ppermute | solution.py:116
